TPU v7x, 32 devices: a whole 2x2x4 slice. The times are simulated.
32 devices in a mesh: seq: 8 (over y, x, core), wt: 4 (over z).
Axes of the slice: x: 2, y: 2, z: 4, core: 2. Of those that a mesh axis runs over, the one named last changes fastest.
Arguments:
- tokens: bfloat16 [8, 224, 112, 128], P(None, 'seq', 'wt'), may hold values from -6 to 6
- region: int32 [8, 224, 112], P(None, 'seq', 'wt'), may hold values from 0 to 3
- rel_index: int32 [49, 49], replicated, may hold values from 0 to 168
- norm_gain: float32 [2, 2, 128], replicated, may hold values from 0.5 to 1.5
- norm_bias: float32 [2, 2, 128], replicated, may hold values from -3 to 3
- w_qkv: bfloat16 [2, 128, 384], P(None, 'wt'), may hold values from -0.5 to 0.5
- qv_bias: float32 [2, 2, 128], replicated, may hold values from -3 to 3
- pos_table: float32 [2, 169, 4], replicated, may hold values from -4 to 4
- w_proj: bfloat16 [2, 128, 128], P(None, 'wt'), may hold values from -1 to 1
- out_bias: float32 [2, 2, 128], replicated, may hold values from -2 to 2
- w_fc1: bfloat16 [2, 128, 512], P(None, 'wt'), may hold values from -0.5 to 0.5
- fc1_bias: float32 [2, 512], replicated, may hold values from -3 to 3
- w_fc2: bfloat16 [2, 512, 128], P(None, 'wt'), may hold values from -0.375 to 0.375
- cotangent: bfloat16 [8, 224, 112, 128], P(None, 'seq', 'wt'), may hold values from -6 to 6
Outputs:
- mixed: bfloat16 [8, 224, 112, 128], P(None, 'seq', 'wt')
- tokens_grad: float32 [8, 224, 112, 128], P(None, 'seq', 'wt')
- norm_gain_grad: float32 [2, 2, 128], replicated
- norm_bias_grad: float32 [2, 2, 128], replicated
- w_qkv_grad: float32 [2, 128, 384], P(None, 'wt')
- qv_bias_grad: float32 [2, 2, 128], replicated
- pos_table_grad: float32 [2, 169, 4], replicated
- w_proj_grad: float32 [2, 128, 128], P(None, 'wt')
- out_bias_grad: float32 [2, 2, 128], replicated
- w_fc1_grad: float32 [2, 128, 512], P(None, 'wt')
- fc1_bias_grad: float32 [2, 512], replicated
- w_fc2_grad: float32 [2, 512, 128], P(None, 'wt')
Inputs may be any that keep to these rules, and one draw needn't show every extreme that they name: `region`: region ids of the shifted layer's tokens, in shifted coordinates.
All inputs are finite; a program needn't handle non-finite values.
Results may differ from a plain program's by a relative error of at most 0.019.
Values may be sent and summed in bfloat16 or wider, within the bound.
No kernel may reach another device: no remote copies, remote signals or barrier semaphores. Data moves between devices by JAX's collectives and lax.ppermute only.
A program may use at most 320 MiB of HBM per device.

v0:
```python
from functools import partial
import math

import jax
import jax.numpy as jnp
from jax import lax
from jax.sharding import PartitionSpec as P

HEADS = 4
WIN = 7
SHIFT = 3
HEAD_DIM = 32


EPSILON = 1e-05


def shifted_2(array, axis, by):
    count = lax.axis_size(axis)
    return lax.ppermute(array, axis, [(i, (i + by) % count) for i in range(count)])


def to_windows(field):
    batch, height, width, depth = field.shape
    blocks = field.reshape(batch, height // WIN, WIN, width // WIN, WIN, depth)
    return blocks.transpose(0, 1, 3, 2, 4, 5).reshape(-1, WIN * WIN, depth)


def from_windows(blocks, batch, height, width):
    depth = blocks.shape[-1]
    field = blocks.reshape(batch, height // WIN, width // WIN, WIN, WIN, depth)
    return field.transpose(0, 1, 3, 2, 4, 5).reshape(batch, height, width, depth)


def roll_ahead(field):
    rim_rows = shifted_2(field[:, :SHIFT], "seq", -1)
    field = jnp.concatenate([field[:, SHIFT:], rim_rows], 1)
    rim_cols = shifted_2(field[:, :, :SHIFT], "wt", -1)
    return jnp.concatenate([field[:, :, SHIFT:], rim_cols], 2)


def roll_behind(field):
    rim_rows = shifted_2(field[:, -SHIFT:], "seq", 1)
    field = jnp.concatenate([rim_rows, field[:, :-SHIFT]], 1)
    rim_cols = shifted_2(field[:, :, -SHIFT:], "wt", 1)
    return jnp.concatenate([rim_cols, field[:, :, :-SHIFT]], 2)


def norm_forward(field, norm_scale, norm_shift):
    average = jnp.mean(field, -1, keepdims=True)
    centred = field - average
    inverse = lax.rsqrt(jnp.mean(centred * centred, -1, keepdims=True) + EPSILON)
    normed = centred * inverse
    return (normed * norm_scale + norm_shift, normed, inverse)


def norm_backward(upstream, normed, inverse, norm_scale):
    leading = tuple(range(upstream.ndim - 1))
    scale_grad = jnp.sum(upstream * normed, leading)
    shift_grad = jnp.sum(upstream, leading)
    scaled = upstream * norm_scale
    field_grad = inverse * (
        scaled
        - jnp.mean(scaled, -1, keepdims=True)
        - normed * jnp.mean(scaled * normed, -1, keepdims=True)
    )
    return (field_grad, scale_grad, shift_grad)


def attention_scores(query_heads, key_heads, rel_bias, mask_add, scale, shifted):
    scores = (
        jnp.einsum("wihd,wjhd->whij", query_heads, key_heads, preferred_element_type=jnp.float32)
        * scale
        + rel_bias[None]
    )
    if shifted:
        scores = scores + mask_add
    return scores


def per_device(
    tokens,
    region,
    rel_index,
    norm_gain,
    norm_bias,
    w_qkv,
    qv_bias,
    pos_table,
    w_proj,
    out_bias,
    w_fc1,
    fc1_bias,
    w_fc2,
    cotangent,
):
    whole_qkv, whole_proj, whole_fc1, whole_fc2 = (
        lax.all_gather(w_qkv, "wt", axis=1, tiled=True),
        lax.all_gather(w_proj, "wt", axis=1, tiled=True),
        lax.all_gather(w_fc1, "wt", axis=1, tiled=True),
        lax.all_gather(w_fc2, "wt", axis=1, tiled=True),
    )
    batch, height, width, depth = tokens.shape
    scale = 1.0 / math.sqrt(HEAD_DIM)
    table_size = pos_table.shape[1]
    selector = (
        rel_index.reshape(-1)[:, None] == jnp.arange(table_size, dtype=jnp.int32)[None, :]
    ).astype(jnp.float32)
    region_ids = to_windows(region[..., None])[..., 0]
    mask_add = jnp.where(region_ids[:, :, None] == region_ids[:, None, :], 0.0, -100.0).astype(
        jnp.float32
    )[:, None]
    window_count = region_ids.shape[0]
    heads_shape = (window_count, WIN * WIN, HEADS, HEAD_DIM)
    gelu_exact = partial(jax.nn.gelu, approximate=False)
    stream = tokens.astype(jnp.float32)
    stored = []
    for layer in range(2):
        shifted = layer == 1
        first, normed_one, inverse_one = norm_forward(
            stream, norm_gain[layer, 0], norm_bias[layer, 0]
        )
        hidden = first.astype(jnp.bfloat16)
        if shifted:
            hidden = roll_ahead(hidden)
        windows = to_windows(hidden)
        zeros = jnp.zeros((depth,), jnp.float32)
        projected = jnp.einsum(
            "wid,de->wie", windows, whole_qkv[layer], preferred_element_type=jnp.float32
        )
        projected = (
            projected + jnp.concatenate([qv_bias[layer, 0], zeros, qv_bias[layer, 1]])
        ).astype(jnp.bfloat16)
        query_heads = projected[..., :depth].reshape(heads_shape)
        key_heads = projected[..., depth : 2 * depth].reshape(heads_shape)
        value_heads = projected[..., 2 * depth :].reshape(heads_shape)
        table = jnp.dot(selector, pos_table[layer], precision=lax.Precision.HIGHEST)
        rel_bias = table.reshape(WIN * WIN, WIN * WIN, HEADS).transpose(2, 0, 1)
        scores = attention_scores(query_heads, key_heads, rel_bias, mask_add, scale, shifted)
        log_total = jax.nn.logsumexp(scores, -1, keepdims=True)
        attention = jnp.exp(scores - log_total).astype(jnp.bfloat16)
        attended = jnp.einsum(
            "whij,wjhd->wihd", attention, value_heads, preferred_element_type=jnp.float32
        )
        attended = attended.reshape(window_count, WIN * WIN, depth).astype(jnp.bfloat16)
        attended_map = from_windows(attended, batch, height, width)
        if shifted:
            attended_map = roll_behind(attended_map)
        branch = (
            jnp.dot(attended_map, whole_proj[layer], preferred_element_type=jnp.float32)
            + out_bias[layer, 0]
        )
        middle = stream + branch
        second, normed_two, inverse_two = norm_forward(
            middle, norm_gain[layer, 1], norm_bias[layer, 1]
        )
        inner = second.astype(jnp.bfloat16)
        expanded = (
            jnp.dot(inner, whole_fc1[layer], preferred_element_type=jnp.float32) + fc1_bias[layer]
        )
        activated = gelu_exact(expanded).astype(jnp.bfloat16)
        stream = (
            middle
            + jnp.dot(activated, whole_fc2[layer], preferred_element_type=jnp.float32)
            + out_bias[layer, 1]
        )
        stored.append(
            (
                normed_one,
                inverse_one,
                windows,
                query_heads,
                key_heads,
                value_heads,
                log_total,
                attended_map,
                normed_two,
                inverse_two,
                inner,
                expanded,
                rel_bias,
            )
        )
    outputs = stream.astype(jnp.bfloat16)
    gradient = cotangent.astype(jnp.float32)
    gains = [None, None]
    shifts = [None, None]
    qv_sums = [None, None]
    tables = [None, None]
    out_sums = [None, None]
    fc1_sums = [None, None]
    qkv_grads = [None, None]
    proj_grads = [None, None]
    fc1_grads = [None, None]
    fc2_grads = [None, None]
    image_axes = (0, 1, 2)
    for layer in (1, 0):
        shifted = layer == 1
        (
            normed_one,
            inverse_one,
            windows,
            query_heads,
            key_heads,
            value_heads,
            log_total,
            attended_map,
            normed_two,
            inverse_two,
            inner,
            expanded,
            rel_bias,
        ) = stored[layer]
        out_low = gradient.astype(jnp.bfloat16)
        activated_full, gelu_pull = jax.vjp(gelu_exact, expanded)
        activated = activated_full.astype(jnp.bfloat16)
        fc2_grads[layer] = jnp.einsum(
            "bhwf,bhwd->fd", activated, out_low, preferred_element_type=jnp.float32
        )
        fc2_bias_grad = jnp.sum(out_low.astype(jnp.float32), image_axes)
        activated_grad = jnp.einsum(
            "bhwd,fd->bhwf", out_low, whole_fc2[layer], preferred_element_type=jnp.float32
        )
        expanded_low = gelu_pull(activated_grad)[0].astype(jnp.bfloat16)
        fc1_sums[layer] = jnp.sum(expanded_low.astype(jnp.float32), image_axes)
        fc1_grads[layer] = jnp.einsum(
            "bhwd,bhwf->df", inner, expanded_low, preferred_element_type=jnp.float32
        )
        inner_grad = jnp.einsum(
            "bhwf,df->bhwd", expanded_low, whole_fc1[layer], preferred_element_type=jnp.float32
        )
        norm_term, gain_two, shift_two = norm_backward(
            inner_grad, normed_two, inverse_two, norm_gain[layer, 1]
        )
        gradient = gradient + norm_term
        branch_low = gradient.astype(jnp.bfloat16)
        proj_bias_grad = jnp.sum(branch_low.astype(jnp.float32), image_axes)
        proj_grads[layer] = jnp.einsum(
            "bhwd,bhwe->de", attended_map, branch_low, preferred_element_type=jnp.float32
        )
        attended_grad = jnp.einsum(
            "bhwe,de->bhwd", branch_low, whole_proj[layer], preferred_element_type=jnp.float32
        ).astype(jnp.bfloat16)
        if shifted:
            attended_grad = roll_ahead(attended_grad)
        attended_grad = to_windows(attended_grad).reshape(heads_shape)
        scores = attention_scores(query_heads, key_heads, rel_bias, mask_add, scale, shifted)
        attention_full = jnp.exp(scores - log_total)
        attention = attention_full.astype(jnp.bfloat16)
        attention_grad = jnp.einsum(
            "wihd,wjhd->whij", attended_grad, value_heads, preferred_element_type=jnp.float32
        )
        value_grad = jnp.einsum(
            "whij,wihd->wjhd", attention, attended_grad, preferred_element_type=jnp.float32
        ).astype(jnp.bfloat16)
        row_terms = jnp.sum(attention_grad * attention_full, -1, keepdims=True)
        score_grad = (attention_full * (attention_grad - row_terms)).astype(jnp.bfloat16)
        bias_grad = jnp.sum(score_grad.astype(jnp.float32), 0)
        tables[layer] = jnp.dot(
            selector.T,
            bias_grad.transpose(1, 2, 0).reshape(-1, HEADS),
            precision=lax.Precision.HIGHEST,
        )
        query_grad = (
            jnp.einsum("whij,wjhd->wihd", score_grad, key_heads, preferred_element_type=jnp.float32)
            * scale
        ).astype(jnp.bfloat16)
        key_grad = (
            jnp.einsum(
                "whij,wihd->wjhd", score_grad, query_heads, preferred_element_type=jnp.float32
            )
            * scale
        ).astype(jnp.bfloat16)
        flat_shape = (window_count, WIN * WIN, depth)
        joined_grad = jnp.concatenate(
            [
                query_grad.reshape(flat_shape),
                key_grad.reshape(flat_shape),
                value_grad.reshape(flat_shape),
            ],
            -1,
        )
        qv_sums[layer] = jnp.stack(
            [
                jnp.sum(query_grad.astype(jnp.float32), (0, 1)).reshape(depth),
                jnp.sum(value_grad.astype(jnp.float32), (0, 1)).reshape(depth),
            ]
        )
        qkv_grads[layer] = jnp.einsum(
            "wid,wie->de", windows, joined_grad, preferred_element_type=jnp.float32
        )
        hidden_grad = jnp.einsum(
            "wie,de->wid", joined_grad, whole_qkv[layer], preferred_element_type=jnp.float32
        )
        hidden_grad = from_windows(hidden_grad, batch, height, width)
        if shifted:
            hidden_grad = roll_behind(hidden_grad.astype(jnp.bfloat16)).astype(jnp.float32)
        norm_term, gain_one, shift_one = norm_backward(
            hidden_grad, normed_one, inverse_one, norm_gain[layer, 0]
        )
        gradient = gradient + norm_term
        gains[layer] = jnp.stack([gain_one, gain_two])
        shifts[layer] = jnp.stack([shift_one, shift_two])
        out_sums[layer] = jnp.stack([proj_bias_grad, fc2_bias_grad])
    small = lax.psum(
        (
            jnp.stack(gains),
            jnp.stack(shifts),
            jnp.stack(qv_sums),
            jnp.stack(tables),
            jnp.stack(out_sums),
            jnp.stack(fc1_sums),
        ),
        ("seq", "wt"),
    )
    large = (
        jnp.stack(qkv_grads),
        jnp.stack(proj_grads),
        jnp.stack(fc1_grads),
        jnp.stack(fc2_grads),
    )
    summed = (
        lax.psum(large[0].astype(jnp.bfloat16), "seq").astype(jnp.float32),
        lax.psum(large[1].astype(jnp.bfloat16), "seq").astype(jnp.float32),
        lax.psum(large[2].astype(jnp.bfloat16), "seq").astype(jnp.float32),
        lax.psum(large[3].astype(jnp.bfloat16), "seq").astype(jnp.float32),
    )
    owned = (
        lax.psum_scatter(
            summed[0].astype(jnp.bfloat16), "wt", scatter_dimension=1, tiled=True
        ).astype(jnp.float32),
        lax.psum_scatter(
            summed[1].astype(jnp.bfloat16), "wt", scatter_dimension=1, tiled=True
        ).astype(jnp.float32),
        lax.psum_scatter(
            summed[2].astype(jnp.bfloat16), "wt", scatter_dimension=1, tiled=True
        ).astype(jnp.float32),
        lax.psum_scatter(
            summed[3].astype(jnp.bfloat16), "wt", scatter_dimension=1, tiled=True
        ).astype(jnp.float32),
    )
    return (
        outputs,
        gradient,
        small[0],
        small[1],
        owned[0],
        small[2],
        small[3],
        owned[1],
        small[4],
        owned[2],
        small[5],
        owned[3],
    )


def solution(mesh):
    return jax.shard_map(
        per_device,
        mesh=mesh,
        in_specs=(
            P(None, "seq", "wt", None),
            P(None, "seq", "wt"),
            P(),
            P(),
            P(),
            P(None, "wt", None),
            P(),
            P(),
            P(None, "wt", None),
            P(),
            P(None, "wt", None),
            P(),
            P(None, "wt", None),
            P(None, "seq", "wt", None),
        ),
        out_specs=(
            P(None, "seq", "wt", None),
            P(None, "seq", "wt", None),
            P(),
            P(),
            P(None, "wt", None),
            P(),
            P(),
            P(None, "wt", None),
            P(),
            P(None, "wt", None),
            P(),
            P(None, "wt", None),
        ),
        check_vma=False,
    )
```

profile of v0, /device:TPU:0, one launch (start us, length us, event | category | flops | bytes accessed | tf_op | source)
XLA Modules:
  0.0 963.3 jit_solution(2163960260634030465)
XLA Ops:
  19.5 15.5 %all_gather.12 = bf16[2,128,384]{2,1,0:T(8,128)(2,1)S(1)} all-gather(bf16[2,32,384]{2,1,0:T(8,128)(2,1)S(1)} %copy-done.68), channel_id=1, replica_groups=mesh['seq'=8,'wt'=4] {'wt'}, dimensions={1}, use_global_device_ids=true | all-gather | bytes 245760 | tf_op jit(solution)/shard_map/all_gather | solution.py:98
  52.8 12.8 %fusion.12 = (f32[128,4,49]{2,1,0:T(4,128)S(1)}, f32[128,4,49,49]{2,3,1,0:T(8,128)}) fusion(f32[4,49,49]{1,2,0:T(8,128)S(1)} %copy.166, bf16[128,49,4,32]{1,3,2,0:T(8,128)(2,1)} %bitcast.395, bf16[128,49,4,32]{1,3,2,0:T(8,128)(2,1)} %bitcast.397), kind=kOutput, calls=%fused_computation.55 | convolution fusion | flops 82338816 | bytes 8267280 | tf_op jit(solution)/shard_map/wihd,wjhd->whij/dot_general | solution.py:72
  65.7 9.8 %exponential_reduce_fusion.1 = f32[128,4,49]{2,1,0:T(4,128)S(1)} fusion(f32[128,4,49,49]{2,3,1,0:T(8,128)} %get-tuple-element.119, f32[128,4,49]{2,1,0:T(4,128)S(1)} %is-finite_select_fusion.1, f32[4,49,49]{1,2,0:T(8,128)S(1)} %copy.166), kind=kLoop, calls=%fused_computation.53 | loop fusion | flops 4892160 | bytes 5156368 | tf_op jit(solution)/shard_map/reduce_sum | solution.py:140
  79.6 11.9 %convert_bitcast_fusion.1 = bf16[128,49,4,32]{1,3,2,0:T(8,128)(2,1)} fusion(bf16[128,49,4,32]{1,3,2,0:T(8,128)(2,1)} %bitcast.393, f32[128,4,49,49]{2,3,1,0:T(8,128)} %get-tuple-element.119, f32[128,4,49]{2,1,0:T(4,128)S(1)} %log_add_fusion.1, f32[4,49,49]{1,2,0:T(8,128)} %copy-done.28), kind=kOutput, calls=%fused_computation.110 | convolution fusion | flops 84396032 | bytes 8267280 | tf_op jit(solution)/shard_map/whij,wjhd->wihd/dot_general | solution.py:142
  91.6 10.6 %copy.169 = bf16[128,49,4,32]{3,2,0,1:T(4,128)(2,1)} copy(bf16[128,49,4,32]{1,3,2,0:T(8,128)(2,1)} %convert_bitcast_fusion.1) | data formatting | bytes 3211264 | tf_op jit(solution)/shard_map/convert_element_type | solution.py:145
  102.2 8.0 convert_element_type.204
  110.6 13.2 %all_gather.13 = bf16[2,128,128]{2,1,0:T(8,128)(2,1)S(1)} all-gather(bf16[2,32,128]{2,1,0:T(8,128)(2,1)S(1)} %copy-done.73), channel_id=1, replica_groups=mesh['seq'=8,'wt'=4] {'wt'}, dimensions={1}, use_global_device_ids=true | all-gather | bytes 81920 | tf_op jit(solution)/shard_map/all_gather | solution.py:99
  127.9 13.9 %all_gather.14 = bf16[2,128,512]{2,1,0:T(8,128)(2,1)S(1)} all-gather(bf16[2,32,512]{2,1,0:T(8,128)(2,1)S(1)} %copy-done.66), channel_id=1, replica_groups=mesh['seq'=8,'wt'=4] {'wt'}, dimensions={1}, use_global_device_ids=true | all-gather | bytes 327680 | tf_op jit(solution)/shard_map/all_gather | solution.py:100
  142.5 14.4 %all_gather.15 = bf16[2,512,128]{2,1,0:T(8,128)(2,1)S(1)} all-gather(bf16[2,128,128]{2,1,0:T(8,128)(2,1)S(1)} %copy-done.67), channel_id=1, replica_groups=mesh['seq'=8,'wt'=4] {'wt'}, dimensions={1}, use_global_device_ids=true | all-gather | bytes 327680 | tf_op jit(solution)/shard_map/all_gather | solution.py:101
  156.9 6.3 convert_reduce_fusion.3
  163.3 34.8 %multiply_convert_fusion.3 = (bf16[8,28,28,512]{3,2,1,0:T(8,128)(2,1)S(1)}, f32[8,28,28,512]{3,2,1,0:T(8,128)}) fusion(f32[8,28,28,512]{3,2,1,0:T(8,128)S(1)} %get-tuple-element.122, f32[512]{0:T(512)S(1)} %bitcast.444, u32[8,28,512]{2,1,0:T(8,128)S(1)} %get-tuple-element.51, u32[8,28,512]{2,1,0:T(8,128)S(1)} %get-tuple-element.50), kind=kLoop, calls=%fused_computation.39 | loop fusion | flops 221577216 | bytes 33032192 | tf_op jit(solution)/shard_map/convert_element_type | solution.py:161
  227.5 5.3 copy.271
  236.6 14.0 %fusion.178 = (f32[128,4,49]{2,1,0:T(4,128)S(1)}, f32[128,4,49,49]{2,3,1,0:T(8,128)}) fusion(f32[128,49,49]{1,2,0:T(8,128)} %compare_select_fusion, f32[4,49,49]{1,2,0:T(8,128)} %copy.179, bf16[128,49,4,32]{1,3,2,0:T(8,128)(2,1)} %bitcast.401, bf16[128,49,4,32]{1,3,2,0:T(8,128)(2,1)} %bitcast.403), kind=kOutput, calls=%fused_computation.309 | convolution fusion | flops 83568128 | bytes 9496592 | tf_op jit(solution)/shard_map/wihd,wjhd->whij/dot_general | solution.py:72
  250.7 9.4 exponential_reduce_fusion
  264.2 10.8 %convert_bitcast_fusion = bf16[128,49,4,32]{1,3,2,0:T(8,128)(2,1)} fusion(bf16[128,49,4,32]{1,3,2,0:T(8,128)(2,1)} %bitcast.399, f32[128,4,49,49]{2,3,1,0:T(8,128)} %get-tuple-element.126, f32[128,4,49]{2,1,0:T(4,128)S(1)} %log_add_fusion), kind=kOutput, calls=%fused_computation.109 | convolution fusion | flops 81937408 | bytes 8228864 | tf_op jit(solution)/shard_map/whij,wjhd->wihd/dot_general | solution.py:142
  275.0 10.6 %copy.183 = bf16[128,49,4,32]{3,2,0,1:T(4,128)(2,1)} copy(bf16[128,49,4,32]{1,3,2,0:T(8,128)(2,1)} %convert_bitcast_fusion) | data formatting | bytes 3211264 | tf_op jit(solution)/shard_map/convert_element_type | solution.py:145
  285.7 7.9 convert_element_type.212
  294.4 5.7 collective-permute-done.2
  302.1 7.0 collective-permute-done.3
  315.2 6.3 convert_reduce_fusion.1
  321.6 34.5 %multiply_convert_fusion.2 = (bf16[8,28,28,512]{3,2,1,0:T(8,128)(2,1)}, f32[8,28,28,512]{3,2,1,0:T(8,128)}) fusion(f32[8,28,28,512]{3,2,1,0:T(8,128)S(1)} %get-tuple-element.129, f32[512]{0:T(512)S(1)} %bitcast.447, u32[8,28,512]{2,1,0:T(8,128)S(1)} %get-tuple-element.49, u32[8,28,512]{2,1,0:T(8,128)S(1)} %get-tuple-element.48), kind=kLoop, calls=%fused_computation.23 | loop fusion | flops 221577216 | bytes 33032192 | tf_op jit(solution)/shard_map/convert_element_type | solution.py:161
  356.1 15.9 %convert_reduce_fusion.4 = (f32[512]{0:T(512)}, bf16[8,28,28,512]{3,2,1,0:T(8,128)(2,1)}) fusion(f32[8,28,28,512]{3,2,1,0:T(8,128)} %get-tuple-element.88, bf16[2,512,128]{2,1,0:T(8,128)(2,1)S(1)} %all_gather.15, bf16[8,28,28,128]{3,0,2,1:T(8,128)(2,1)S(1)} %copy-done.46, f32[8,28,28,512]{3,2,1,0:T(8,128)} %copy-done.18, f32[512]{0:T(512)S(1)} %bitcast.448), kind=kOutput, calls=%fused_computation.13 | convolution fusion | flops 876674560 | bytes 33853440 | tf_op jit(solution)/shard_map/bhwd,fd->bhwf/dot_general | solution.py:221
  372.1 7.6 multiply_reduce_fusion.2
  411.9 10.7 %copy.191 = bf16[128,49,4,32]{1,3,2,0:T(8,128)(2,1)} copy(bf16[128,49,4,32]{3,2,0,1:T(4,128)(2,1)} %reshape_reshape.6) | data formatting | bytes 3211264 | tf_op jit(solution)/shard_map/reshape;reshape | solution.py:246
  422.6 13.2 %multiply_reduce_fusion.1 = (f32[128,4,49]{2,1,0:T(4,128)S(1)}, f32[128,4,49,49]{2,3,1,0:T(8,128)}) fusion(f32[128,4,49,49]{2,3,1,0:T(8,128)} %get-tuple-element.126, f32[128,4,49]{2,1,0:T(4,128)S(1)} %log_add_fusion, bf16[128,49,4,32]{1,3,2,0:T(8,128)(2,1)} %copy.191, bf16[128,49,4,32]{1,3,2,0:T(8,128)(2,1)} %bitcast.400), kind=kOutput, calls=%fused_computation.21 | convolution fusion | flops 82338816 | bytes 13246464 | tf_op jit(solution)/shard_map/wihd,wjhd->whij/dot_general | solution.py:250
  435.8 12.0 %convert_reduce_fusion.6 = (f32[4,49,49]{1,2,0:T(8,128)}, bf16[128,4,49,49]{2,3,1,0:T(8,128)(2,1)S(1)}) fusion(f32[128,4,49,49]{2,3,1,0:T(8,128)} %get-tuple-element.132, f32[128,4,49]{2,1,0:T(4,128)S(1)} %get-tuple-element.131, f32[128,4,49,49]{2,3,1,0:T(8,128)} %get-tuple-element.126, f32[128,4,49]{2,1,0:T(4,128)S(1)} %log_add_fusion), kind=kLoop, calls=%fused_computation.15 | loop fusion | flops 7366268 | bytes 12532240 | tf_op jit(solution)/shard_map/reduce_sum | solution.py:258
  455.0 9.2 multiply_convert_fusion.6
  464.2 12.3 %convert_reduce_fusion.8 = (f32[4,32]{1,0:T(4,128)S(1)}, bf16[128,4,32,49]{3,2,1,0:T(8,128)(2,1)}) fusion(bf16[128,49,4,32]{1,3,2,0:T(8,128)(2,1)} %copy.191, f32[128,4,49,49]{2,3,1,0:T(8,128)} %get-tuple-element.126, f32[128,4,49]{2,1,0:T(4,128)S(1)} %log_add_fusion), kind=kOutput, calls=%fused_computation.59 | convolution fusion | flops 83542912 | bytes 8229376 | tf_op jit(solution)/shard_map/whij,wihd->wjhd/dot_general | solution.py:253
  476.5 10.6 %copy.195 = bf16[128,49,4,32]{3,2,0,1:T(4,128)(2,1)} copy(bf16[128,49,4,32]{1,3,2,0:T(8,128)(2,1)} %bitcast.405) | data formatting | bytes 3211264 | tf_op jit(solution)/shard_map/convert_element_type | solution.py:267
  487.1 7.9 concatenate.62
  495.5 10.6 %copy.198 = bf16[128,49,4,32]{3,2,0,1:T(4,128)(2,1)} copy(bf16[128,49,4,32]{1,3,2,0:T(8,128)(2,1)} %bitcast.407) | data formatting | bytes 3211264 | tf_op jit(solution)/shard_map/convert_element_type | solution.py:273
  506.1 7.9 concatenate.63
  515.6 10.6 %copy.201 = bf16[128,49,4,32]{3,2,0,1:T(4,128)(2,1)} copy(bf16[128,49,4,32]{1,3,2,0:T(8,128)(2,1)} %bitcast.409) | data formatting | bytes 3211264 | tf_op jit(solution)/shard_map/convert_element_type | solution.py:255
  526.2 8.1 concatenate.64
  538.5 5.5 copy.233
  544.0 5.5 copy.234
  549.5 5.6 copy.235
  565.7 7.5 collective-permute-done.7
  573.1 5.9 fusion.60
  579.2 6.9 convert_reduce_fusion.16
  589.0 15.2 %convert_reduce_fusion.5 = (f32[512]{0:T(512)S(1)}, bf16[8,28,28,512]{3,2,1,0:T(8,128)(2,1)}) fusion(f32[8,28,28,512]{3,2,1,0:T(8,128)} %get-tuple-element.90, bf16[2,512,128]{2,1,0:T(8,128)(2,1)S(1)} %copy-done.49, f32[8,28,28,128]{3,2,1,0:T(8,128)S(1)} %get-tuple-element.80, f32[8,28,28,512]{3,2,1,0:T(8,128)} %copy-done.17, f32[512]{0:T(512)S(1)} %bitcast.445), kind=kOutput, calls=%fused_computation.14 | convolution fusion | flops 877477376 | bytes 35917824 | tf_op jit(solution)/shard_map/bhwd,fd->bhwf/dot_general | solution.py:221
  604.2 7.1 fusion.112
  615.6 6.0 convert_reduce_fusion.17
  630.8 10.8 %copy.210 = bf16[128,49,4,32]{1,3,2,0:T(8,128)(2,1)} copy(bf16[128,49,4,32]{3,2,0,1:T(4,128)(2,1)} %reshape_reshape.7) | data formatting | bytes 3211264 | tf_op jit(solution)/shard_map/reshape;reshape | solution.py:246
  641.6 13.8 %multiply_reduce_fusion = (f32[128,4,49]{2,1,0:T(4,128)S(1)}, f32[128,4,49,49]{2,3,1,0:T(8,128)}) fusion(f32[128,4,49,49]{2,3,1,0:T(8,128)} %get-tuple-element.119, f32[128,4,49]{2,1,0:T(4,128)S(1)} %copy-done.23, f32[4,49,49]{1,2,0:T(8,128)S(1)} %copy-done.29, bf16[128,49,4,32]{1,3,2,0:T(8,128)(2,1)} %copy.210, bf16[128,49,4,32]{1,3,2,0:T(8,128)(2,1)} %bitcast.394), kind=kOutput, calls=%fused_computation.18 | convolution fusion | flops 84797440 | bytes 13284880 | tf_op jit(solution)/shard_map/wihd,wjhd->whij/dot_general | solution.py:250
  655.3 12.0 %convert_reduce_fusion.7 = (f32[4,49,49]{1,2,0:T(8,128)S(1)}, bf16[128,4,49,49]{2,3,1,0:T(8,128)(2,1)S(1)}) fusion(f32[128,4,49,49]{2,3,1,0:T(8,128)} %get-tuple-element.135, f32[128,4,49]{2,1,0:T(4,128)S(1)} %get-tuple-element.134, f32[128,4,49]{2,1,0:T(4,128)S(1)} %copy-done.23, f32[4,49,49]{1,2,0:T(8,128)S(1)} %copy-done.29, ...), kind=kLoop, calls=%fused_computation.16 | loop fusion | flops 9824892 | bytes 12570656 | tf_op jit(solution)/shard_map/reduce_sum | solution.py:258
  674.2 9.1 multiply_convert_fusion.4
  683.3 12.6 %convert_reduce_fusion.10 = (f32[4,32]{1,0:T(4,128)S(1)}, bf16[128,4,32,49]{3,2,1,0:T(8,128)(2,1)}) fusion(bf16[128,49,4,32]{1,3,2,0:T(8,128)(2,1)} %copy.210, f32[128,4,49,49]{2,3,1,0:T(8,128)} %get-tuple-element.119, f32[128,4,49]{2,1,0:T(4,128)S(1)} %copy-done.23, f32[4,49,49]{1,2,0:T(8,128)S(1)} %copy-done.29), kind=kOutput, calls=%fused_computation.61 | convolution fusion | flops 86001536 | bytes 8267792 | tf_op jit(solution)/shard_map/whij,wihd->wjhd/dot_general | solution.py:253
  696.7 5.7 copy.229
  702.4 5.5 copy.230
  707.9 5.5 copy.231
  713.4 10.7 %copy.214 = bf16[128,49,4,32]{3,2,0,1:T(4,128)(2,1)} copy(bf16[128,49,4,32]{1,3,2,0:T(8,128)(2,1)} %bitcast.416) | data formatting | bytes 3211264 | tf_op jit(solution)/shard_map/convert_element_type | solution.py:267
  724.0 7.9 concatenate.68
  733.5 10.7 %copy.217 = bf16[128,49,4,32]{3,2,0,1:T(4,128)(2,1)} copy(bf16[128,49,4,32]{1,3,2,0:T(8,128)(2,1)} %bitcast.414) | data formatting | bytes 3211264 | tf_op jit(solution)/shard_map/convert_element_type | solution.py:273
  744.2 7.9 concatenate.69
  753.7 10.7 %copy.220 = bf16[128,49,4,32]{3,2,0,1:T(4,128)(2,1)} copy(bf16[128,49,4,32]{1,3,2,0:T(8,128)(2,1)} %bitcast.412) | data formatting | bytes 3211264 | tf_op jit(solution)/shard_map/convert_element_type | solution.py:255
  764.4 8.1 concatenate.70
  796.5 9.0 fusion.53
  805.5 6.6 copy.242
  812.1 11.3 %reduce-scatter.11.cloned.1.call-done = bf16[2,128,128]{2,1,0:T(8,128)(2,1)} async-done(((bf16[2,512,128]{2,1,0:T(8,128)(2,1)}), bf16[2,128,128]{2,1,0:T(8,128)(2,1)}) %reduce-scatter.11.cloned.1.call-update) | async-done | bytes 65552 | tf_op jit(solution)/shard_map/reduce_scatter | solution.py:338
  823.4 20.2 %reduce-scatter.9.cloned.1.call-done = bf16[2,32,512]{2,1,0:T(8,128)(2,1)} async-done(((bf16[2,128,512]{2,1,0:T(8,128)(2,1)}), bf16[2,32,512]{2,1,0:T(8,128)(2,1)}) %reduce-scatter.9.cloned.1.call-update) | async-done | bytes 65552 | tf_op jit(solution)/shard_map/reduce_scatter | solution.py:335
  843.6 39.1 %all-reduce = (f32[2,2,128]{2,1,0:T(2,128)}, f32[2,2,128]{2,1,0:T(2,128)}, f32[2,2,128]{2,1,0:T(2,128)}, f32[2,169,4]{1,2,0:T(4,128)}, f32[2,2,128]{2,1,0:T(2,128)}, /*index=5*/f32[2,512]{1,0:T(2,128)}) all-reduce(f32[2,2,128]{2,1,0:T(2,128)S(1)} %pad_maximum_fusion.16, ...), channel_id=1, replica_groups=mesh['seq'=8,'wt'=4] {'seq','wt'}, use_global_device_ids=true, to_apply=%region_26.27 | all-reduce | flops 4424 | bytes 35392 | tf_op jit(solution)/shard_map/psum | solution.py:305
  882.7 14.8 %all-reduce.6.cloned.1.call-done = (bf16[2,32,384]{2,1,0:T(8,128)(2,1)}, bf16[2,32,128]{2,1,0:T(8,128)(2,1)}) async-done(((bf16[2,32,384]{2,1,0:T(8,128)(2,1)}, bf16[2,32,128]{2,1,0:T(8,128)(2,1)}), (bf16[2,32,384]{2,1,0:T(8,128)(2,1)}, bf16[2,32,128]{2,1,0:T(8,128)(2,1)})) %all-reduce.6.cloned.1.call-update) | async-done | bytes 65552 | tf_op jit(solution)/shard_map/psum | solution.py:323
  900.3 52.9 %all-reduce.8.cloned.1.call-done = (bf16[2,32,512]{2,1,0:T(8,128)(2,1)}, bf16[2,128,128]{2,1,0:T(8,128)(2,1)}) async-done(((bf16[2,32,512]{2,1,0:T(8,128)(2,1)}, bf16[2,128,128]{2,1,0:T(8,128)(2,1)}), (bf16[2,32,512]{2,1,0:T(8,128)(2,1)}, bf16[2,128,128]{2,1,0:T(8,128)(2,1)})) %all-reduce.8.cloned.1.call-update) | async-done | bytes 131088 | tf_op jit(solution)/shard_map/psum | solution.py:325
  (384 shorter events, 197.7 us)
Async XLA Ops:
  7.2 8.1 copy-start.6
  7.2 798.2 %reduce-scatter.7.cloned.1.call-start = ((), (), s32[]{:S(2)}) async-start(), calls=%async_computation.5 | async-start | bytes 81920 | tf_op jit(solution)/shard_map/reduce_scatter | solution.py:332
  8.1 10.5 %copy-start.75 = (f32[128]{0:T(128)}, f32[128]{0:T(128)S(1)}, u32[]{:S(2)}) copy-start(f32[128]{0:T(128)S(1)} %get-tuple-element.106) | copy-start | bytes 1540
  8.1 148.8 %copy-start.77 = (f32[128]{0:T(128)}, f32[128]{0:T(128)S(1)}, u32[]{:S(2)}) copy-start(f32[128]{0:T(128)S(1)} %get-tuple-element.105) | copy-start | bytes 1540
  8.1 195.2 %copy-start.79 = (f32[128]{0:T(128)}, f32[128]{0:T(128)S(1)}, u32[]{:S(2)}) copy-start(f32[128]{0:T(128)S(1)} %get-tuple-element.107) | copy-start | bytes 1540
  19.5 15.5 %copy-start.24 = (bf16[8,4,4,7,7,128]{5,2,1,0,4,3:T(4,128)(2,1)}, bf16[8,4,4,7,7,128]{5,2,1,0,4,3:T(4,128)(2,1)S(1)}, u32[]{:S(2)}) copy-start(bf16[8,4,4,7,7,128]{5,2,1,0,4,3:T(4,128)(2,1)S(1)} %copy.160) | copy-start | bytes 4816900
  52.8 12.9 %copy-start.28 = (f32[4,49,49]{1,2,0:T(8,128)}, f32[4,49,49]{1,2,0:T(8,128)S(1)}, u32[]{:S(2)}) copy-start(f32[4,49,49]{1,2,0:T(8,128)S(1)} %copy.166) | copy-start | bytes 115252
  75.7 15.9 %copy-start.22 = (f32[128,4,49]{2,1,0:T(4,128)}, f32[128,4,49]{2,1,0:T(4,128)S(1)}, u32[]{:S(2)}) copy-start(f32[128,4,49]{2,1,0:T(4,128)S(1)} %log_add_fusion.1) | copy-start | bytes 301060
  102.2 8.4 copy-start.73
  102.2 21.6 %copy-start.93 = (f32[2,2,128]{2,1,0:T(2,128)S(1)}, f32[2,2,128]{2,1,0:T(2,128)}, u32[]{:S(2)}) copy-start(f32[2,2,128]{2,1,0:T(2,128)} %param.23) | copy-start | bytes 6148
  110.6 17.2 %copy-start.20 = (bf16[8,4,7,4,7,128]{5,0,4,3,2,1:T(8,128)(2,1)}, bf16[8,4,7,4,7,128]{5,0,4,3,2,1:T(8,128)(2,1)S(1)}, u32[]{:S(2)}) copy-start(bf16[8,4,7,4,7,128]{5,0,4,3,2,1:T(8,128)(2,1)S(1)} %copy.170) | copy-start | bytes 4816900
  123.8 264.3 %copy-start.54 = (bf16[2,128,128]{2,1,0:T(8,128)(2,1)}, bf16[2,128,128]{2,1,0:T(8,128)(2,1)S(1)}, u32[]{:S(2)}) copy-start(bf16[2,128,128]{2,1,0:T(8,128)(2,1)S(1)} %all_gather.13) | copy-start | bytes 196612
  125.6 72.5 %copy-start.2 = (f32[8,28,28,128]{3,2,1,0:T(8,128)}, f32[8,28,28,128]{3,2,1,0:T(8,128)S(1)}, u32[]{:S(2)}) copy-start(f32[8,28,28,128]{3,2,1,0:T(8,128)S(1)} %get-tuple-element.121) | copy-start | bytes 9633796
  125.6 16.2 %copy-start.88 = (f32[2,512]{1,0:T(2,128)S(1)}, f32[2,512]{1,0:T(2,128)}, u32[]{:S(2)}) copy-start(f32[2,512]{1,0:T(2,128)} %param.25) | copy-start | bytes 12292
  125.7 16.8 %copy-start.67 = (bf16[2,128,128]{2,1,0:T(8,128)(2,1)S(1)}, bf16[2,128,128]{2,1,0:T(8,128)(2,1)}, u32[]{:S(2)}) copy-start(bf16[2,128,128]{2,1,0:T(8,128)(2,1)} %param.26) | copy-start | bytes 196612
  125.7 31.2 %copy-start.84 = (f32[128]{0:T(128)S(1)}, f32[128]{0:T(128)}, u32[]{:S(2)}) copy-start(f32[128]{0:T(128)} %get-tuple-element.109) | copy-start | bytes 1540
  125.7 37.5 %copy-start.36 = (f32[8,28,28]{2,1,0:T(8,128)}, f32[8,28,28]{2,1,0:T(8,128)S(1)}, u32[]{:S(2)}) copy-start(f32[8,28,28]{2,1,0:T(8,128)S(1)} %broadcast_multiply_fusion.10) | copy-start | bytes 75268
  127.9 35.3 %copy-start.42 = (f32[8,28,28]{2,1,0:T(8,128)}, f32[8,28,28]{2,1,0:T(8,128)S(1)}, u32[]{:S(2)}) copy-start(f32[8,28,28]{2,1,0:T(8,128)S(1)} %add_rsqrt_fusion.2) | copy-start | bytes 75268
  141.8 21.4 %copy-start.57 = (bf16[2,128,512]{2,1,0:T(8,128)(2,1)}, bf16[2,128,512]{2,1,0:T(8,128)(2,1)S(1)}, u32[]{:S(2)}) copy-start(bf16[2,128,512]{2,1,0:T(8,128)(2,1)S(1)} %all_gather.14) | copy-start | bytes 786436
  142.5 20.8 %copy-start.81 = (f32[1,512]{1,0:T(1,128)}, f32[1,512]{1,0:T(1,128)S(1)}, u32[]{:S(2)}) copy-start(f32[1,512]{1,0:T(1,128)S(1)} %get-tuple-element.99) | copy-start | bytes 6148
  156.9 234.8 %copy-start.48 = (bf16[2,512,128]{2,1,0:T(8,128)(2,1)}, bf16[2,512,128]{2,1,0:T(8,128)(2,1)S(1)}, u32[]{:S(2)}) copy-start(bf16[2,512,128]{2,1,0:T(8,128)(2,1)S(1)} %all_gather.15) | copy-start | bytes 786436
  163.2 34.8 %copy-start.17 = (f32[8,28,28,512]{3,2,1,0:T(8,128)}, f32[8,28,28,512]{3,2,1,0:T(8,128)S(1)}, u32[]{:S(2)}) copy-start(f32[8,28,28,512]{3,2,1,0:T(8,128)S(1)} %get-tuple-element.122) | copy-start | bytes 38535172
  205.6 4.0 collective-permute-start
  206.0 7.8 copy-start.98
  206.3 7.5 copy-start.71
  209.7 10.1 %collective-permute-start.1 = (bf16[8,28,3,128]{3,2,1,0:T(4,128)(2,1)S(1)}, bf16[8,28,3,128]{3,2,1,0:T(4,128)(2,1)S(1)}, u32[]{:S(2)}, u32[]{:S(2)}) collective-permute-start(bf16[8,28,3,128]{3,2,1,0:T(4,128)(2,1)S(1)} %pad_maximum_fusion.9), channel_id=1, source_target_pairs={{0,3},{1,0},{2,1},{3,2},{4,7},{5,4},{6,5},{7,6},{8,11},{9,8},{10,9... | collective-permute-start | bytes 516104 | tf_op jit(solution)/shard_map/ppermute | solution.py:20
  294.0 7.4 copy-start.72
  294.0 15.0 %copy-start.90 = (f32[128]{0:T(128)S(1)}, f32[128]{0:T(128)}, u32[]{:S(2)}) copy-start(f32[128]{0:T(128)} %get-tuple-element.103) | copy-start | bytes 1540
  294.1 6.0 collective-permute-start.2
  300.6 11.9 %copy-start.34 = (bf16[8,28,28,128]{3,2,1,0:T(8,128)(2,1)}, bf16[8,28,28,128]{3,2,1,0:T(8,128)(2,1)S(1)}, u32[]{:S(2)}) copy-start(bf16[8,28,28,128]{3,2,1,0:T(8,128)(2,1)S(1)} %copy_dynamic-update-slice_fusion.1) | copy-start | bytes 4816900
  300.7 8.3 collective-permute-start.3
  321.6 34.5 %copy-start.18 = (f32[8,28,28,512]{3,2,1,0:T(8,128)}, f32[8,28,28,512]{3,2,1,0:T(8,128)S(1)}, u32[]{:S(2)}) copy-start(f32[8,28,28,512]{3,2,1,0:T(8,128)S(1)} %get-tuple-element.129) | copy-start | bytes 38535172
  321.6 34.5 %copy-start.46 = (bf16[8,28,28,128]{3,0,2,1:T(8,128)(2,1)S(1)}, bf16[8,28,28,128]{3,0,2,1:T(8,128)(2,1)}, u32[]{:S(2)}) copy-start(bf16[8,28,28,128]{3,0,2,1:T(8,128)(2,1)} %param.27) | copy-start | bytes 4816900
  372.1 7.6 copy-start.16
  379.7 9.2 slice-start.2
  388.8 7.1 collective-permute-start.4
  396.0 8.2 collective-permute-start.5
  435.8 14.9 %copy-start.12 = (bf16[128,49,128]{1,2,0:T(8,128)(2,1)S(1)}, bf16[128,49,128]{1,2,0:T(8,128)(2,1)}, u32[]{:S(2)}) copy-start(bf16[128,49,128]{1,2,0:T(8,128)(2,1)} %copy.272) | copy-start | bytes 4816900
  526.2 8.5 copy-start.52
  538.5 22.0 %collective-permute-start.6 = (bf16[8,3,28,128]{3,2,1,0:T(8,128)(2,1)}, bf16[8,3,28,128]{3,2,1,0:T(8,128)(2,1)}, u32[]{:S(2)}, u32[]{:S(2)}) collective-permute-start(bf16[8,3,28,128]{3,2,1,0:T(8,128)(2,1)} %copy.283), channel_id=1, source_target_pairs={{0,4},{4,8},{8,12},{12,16},{16,20},{20,24},{24,28},{28,0},{1,5},{5... | collective-permute-start | bytes 516104 | tf_op jit(solution)/shard_map/ppermute | solution.py:20
  559.1 14.0 %copy-start.33 = (f32[8,28,28]{2,1,0:T(8,128)S(1)}, f32[8,28,28]{2,1,0:T(8,128)}, u32[]{:S(2)}) copy-start(f32[8,28,28]{2,1,0:T(8,128)} %copy-done.32) | copy-start | bytes 75268
  559.1 14.0 %copy-start.41 = (f32[8,28,28]{2,1,0:T(8,128)S(1)}, f32[8,28,28]{2,1,0:T(8,128)}, u32[]{:S(2)}) copy-start(f32[8,28,28]{2,1,0:T(8,128)} %copy-done.40) | copy-start | bytes 75268
  559.1 14.0 %copy-start.80 = (f32[128]{0:T(128)S(1)}, f32[128]{0:T(128)}, u32[]{:S(2)}) copy-start(f32[128]{0:T(128)} %copy-done.79) | copy-start | bytes 1540
  563.2 15.9 %copy-start.19 = (bf16[8,28,28,128]{3,2,1,0:T(8,128)(2,1)}, bf16[8,28,28,128]{3,2,1,0:T(8,128)(2,1)S(1)}, u32[]{:S(2)}) copy-start(bf16[8,28,28,128]{3,2,1,0:T(8,128)(2,1)S(1)} %copy_dynamic-update-slice_fusion) | copy-start | bytes 4816900
  563.4 9.7 %collective-permute-start.7 = (bf16[8,28,3,128]{3,2,1,0:T(4,128)(2,1)S(1)}, bf16[8,28,3,128]{3,2,1,0:T(4,128)(2,1)S(1)}, u32[]{:S(2)}, u32[]{:S(2)}) collective-permute-start(bf16[8,28,3,128]{3,2,1,0:T(4,128)(2,1)S(1)} %slice.240), channel_id=1, source_target_pairs={{0,1},{1,2},{2,3},{3,0},{4,5},{5,6},{6,7},{7,4},{8,9},{9,10},{10,1... | collective-permute-start | bytes 516104 | tf_op jit(solution)/shard_map/ppermute | solution.py:20
  564.7 14.4 %copy-start.1 = (f32[8,28,28,128]{3,2,1,0:T(8,128)S(1)}, f32[8,28,28,128]{3,2,1,0:T(8,128)}, u32[]{:S(2)}) copy-start(f32[8,28,28,128]{3,2,1,0:T(8,128)} %copy-done) | copy-start | bytes 9633796
  564.7 14.4 %copy-start.14 = (f32[8,28,28,128]{3,2,1,0:T(8,128)S(1)}, f32[8,28,28,128]{3,2,1,0:T(8,128)}, u32[]{:S(2)}) copy-start(f32[8,28,28,128]{3,2,1,0:T(8,128)} %copy-done.13) | copy-start | bytes 9633796
  573.1 12.9 %slice-start = ((s8[7340032]{0:T(1024)(128)(4,1)}), s8[4194304]{0:T(1024)(128)(4,1)S(1)}, s32[]{:S(2)}) async-start(s8[7340032]{0:T(1024)(128)(4,1)} %bitcast.389), calls=%async_computation.10 | async-start | bytes 8388608
  589.0 15.2 %copy-start.3 = (f32[8,28,28,128]{3,2,1,0:T(8,128)S(1)}, f32[8,28,28,128]{3,2,1,0:T(8,128)}, u32[]{:S(2)}) copy-start(f32[8,28,28,128]{3,2,1,0:T(8,128)} %copy-done.2) | copy-start | bytes 9633796
  589.0 15.2 %copy-start.37 = (f32[8,28,28]{2,1,0:T(8,128)S(1)}, f32[8,28,28]{2,1,0:T(8,128)}, u32[]{:S(2)}) copy-start(f32[8,28,28]{2,1,0:T(8,128)} %copy-done.36) | copy-start | bytes 75268
  589.0 15.2 %copy-start.43 = (f32[8,28,28]{2,1,0:T(8,128)S(1)}, f32[8,28,28]{2,1,0:T(8,128)}, u32[]{:S(2)}) copy-start(f32[8,28,28]{2,1,0:T(8,128)} %copy-done.42) | copy-start | bytes 75268
  589.0 15.2 %copy-start.78 = (f32[128]{0:T(128)S(1)}, f32[128]{0:T(128)}, u32[]{:S(2)}) copy-start(f32[128]{0:T(128)} %copy-done.77) | copy-start | bytes 1540
  589.0 15.2 %copy-start.85 = (f32[128]{0:T(128)S(1)}, f32[128]{0:T(128)}, u32[]{:S(2)}) copy-start(f32[128]{0:T(128)} %get-tuple-element.109) | copy-start | bytes 1540
  630.8 10.8 %copy-start.23 = (f32[128,4,49]{2,1,0:T(4,128)S(1)}, f32[128,4,49]{2,1,0:T(4,128)}, u32[]{:S(2)}) copy-start(f32[128,4,49]{2,1,0:T(4,128)} %copy-done.22) | copy-start | bytes 301060
  630.8 10.8 %copy-start.29 = (f32[4,49,49]{1,2,0:T(8,128)S(1)}, f32[4,49,49]{1,2,0:T(8,128)}, u32[]{:S(2)}) copy-start(f32[4,49,49]{1,2,0:T(8,128)} %copy-done.28) | copy-start | bytes 115252
  655.3 14.9 %copy-start.10 = (bf16[128,49,128]{1,2,0:T(8,128)(2,1)S(1)}, bf16[128,49,128]{1,2,0:T(8,128)(2,1)}, u32[]{:S(2)}) copy-start(bf16[128,49,128]{1,2,0:T(8,128)(2,1)} %copy.269) | copy-start | bytes 4816900
  683.3 12.6 %copy-start.69 = (bf16[1,128,128]{2,1,0:T(8,128)(2,1)S(1)}, bf16[1,128,128]{2,1,0:T(8,128)(2,1)}, u32[]{:S(2)}) copy-start(bf16[1,128,128]{2,1,0:T(8,128)(2,1)} %fusion.135) | copy-start | bytes 98308
  696.6 108.8 %reduce-scatter.5.cloned.1.call-start = ((), (), s32[]{:S(2)}) async-start(), calls=%async_computation.4 | async-start | bytes 245760 | tf_op jit(solution)/shard_map/reduce_scatter | solution.py:329
  764.3 8.5 copy-start.25
  785.1 38.4 %reduce-scatter.11.cloned.1.call-start = ((), (), s32[]{:S(2)}) async-start(), calls=%async_computation.7 | async-start | bytes 327680 | tf_op jit(solution)/shard_map/reduce_scatter | solution.py:338
  790.1 53.5 %reduce-scatter.9.cloned.1.call-start = ((), (), s32[]{:S(2)}) async-start(), calls=%async_computation.6 | async-start | bytes 327680 | tf_op jit(solution)/shard_map/reduce_scatter | solution.py:335
  796.2 101.3 %all-reduce.6.cloned.1.call-start = ((), (), s32[]{:S(2)}) async-start(), calls=%async_computation.8 | async-start | bytes 131072 | tf_op jit(solution)/shard_map/psum | solution.py:323
  796.4 9.0 copy-start.95
  805.4 147.7 %all-reduce.8.cloned.1.call-start = ((), (), s32[]{:S(2)}) async-start(), calls=%async_computation.9 | async-start | bytes 262144 | tf_op jit(solution)/shard_map/psum | solution.py:325
  (53 other events, 209.4 us)
Sparse Core Ops, SparseCore 0:
  696.8 17.6 reduce-scatter.6
  785.2 17.9 reduce-scatter.4
  805.5 17.8 reduce-scatter.10
  825.6 17.9 reduce-scatter.8
  846.5 50.8 all-reduce.5
  900.7 52.3 all-reduce.7
where the time goes:
time: 974 us; the launch traced here: 963 us
  local copies, waits for them, and re-layouts  298 us (31%)
  matrix products  235 us (24%)
  other arithmetic  185 us (19%)
  waiting for transfers between devices  125 us (13%)
  blocking collectives  96.1 us (10%)
  between operations  16.3 us (2%)
    convert_element_type x2, other arithmetic, per_device(): activated = gelu_exact(expanded).astype(jnp.bfloat16)  69.3 us
    concatenate x12, local copies, waits for them, and re-layouts, per_device(): jnp.concatenate([query_grad.reshape(flat_shape), key_grad.reshape(flat_sh...  53.9 us
    psum x1, waiting for transfers between devices, per_device(): lax.psum(large[2].astype(jnp.bfloat16), 'seq').astype(jnp.float32)  52.9 us
    psum x1, blocking collectives, per_device(): lax.psum((jnp.stack(gains), jnp.stack(shifts), jnp.stack(qv_sums), jnp.st...  39.1 us
    convert_element_type x4, local copies, waits for them, and re-layouts, per_device(): attended.reshape(window_count, WIN * WIN, depth).astype(jnp.bfloat16)  37.2 us
    another operation x4, local copies, waits for them, and re-layouts, per_device(): attended_grad = to_windows(attended_grad).reshape(heads_shape)  31.9 us
    dot_general x2, matrix products, per_device(): jnp.einsum('bhwd,fd->bhwf', out_low, whole_fc2[layer], preferred_element_...  31.1 us
    dot_general x2, matrix products, per_device(): jnp.einsum('wihd,wjhd->whij', attended_grad, value_heads, preferred_eleme...  26.9 us
  transfers between devices with their start and end apart: 14, of which 9 were waited for; matrix products, arithmetic and copies ran while one was open for 17% of the time, Pallas kernels for 0%

commit v1 on v0

v1 whole, which is shorter than its diff:
```python
import math

import jax
import jax.numpy as jnp
from jax import lax
from jax.experimental import pallas as pl
from jax.experimental.pallas import tpu as pltpu
from jax.sharding import PartitionSpec as P

HEADS = 4
WIN = 7
SHIFT = 3
HEAD_DIM = 32
EPSILON = 1e-05
POS = WIN * WIN
SLOT = 64
LOG2E = math.log2(math.e)
SCALE = 1.0 / math.sqrt(HEAD_DIM)
OFF = -1e30
BF = jnp.bfloat16
F32 = jnp.float32
VMEM_LIMIT = 56 * 1024 * 1024


def mm(left, right):
    return lax.dot_general(left, right, (((1,), (0,)), ((), ())), preferred_element_type=F32)


def mm_nt(left, right):
    return lax.dot_general(left, right, (((1,), (1,)), ((), ())), preferred_element_type=F32)


def mm_tn(left, right):
    return lax.dot_general(left, right, (((0,), (0,)), ((), ())), preferred_element_type=F32)


def norm_parts(field):
    centred = field - jnp.mean(field, -1, keepdims=True)
    inverse = lax.rsqrt(jnp.mean(centred * centred, -1, keepdims=True) + EPSILON)
    return centred * inverse, inverse


def norm_backward(upstream, normed, inverse, gain):
    scaled = upstream * gain
    return inverse * (
        scaled
        - jnp.mean(scaled, -1, keepdims=True)
        - normed * jnp.mean(scaled * normed, -1, keepdims=True)
    )


def fold_rows(field):
    rows, cols = field.shape
    return jnp.sum(field.reshape(rows // 8, 8, cols), 0)


def tokens_of(ref):
    block = ref[...].astype(F32)
    return block.reshape(-1, block.shape[-1])


def put_tokens(ref, field):
    ref[...] = field.reshape(ref.shape).astype(ref.dtype)


def head_blocks(field):
    head = lax.broadcasted_iota(jnp.int32, field.shape, 1) >> 5
    return jnp.concatenate(
        [jnp.where(head == h, field, 0.0).astype(BF) for h in range(HEADS)], 0
    )


def gather_heads(stacked):
    head = lax.broadcasted_iota(jnp.int32, (SLOT, stacked.shape[1]), 1) >> 5
    total = stacked[:SLOT]
    for h in range(1, HEADS):
        total = jnp.where(head == h, stacked[h * SLOT : (h + 1) * SLOT], total)
    return total


def lane_segments():
    row = lax.broadcasted_iota(jnp.int32, (HEADS * SLOT, HEADS * SLOT), 0) >> 6
    col = lax.broadcasted_iota(jnp.int32, (HEADS * SLOT, HEADS * SLOT), 1) >> 6
    return jnp.where(row == col, 1.0, 0.0).astype(BF)


def head_lanes():
    row = lax.broadcasted_iota(jnp.int32, (HEADS * SLOT, HEADS * HEAD_DIM), 0) >> 6
    col = lax.broadcasted_iota(jnp.int32, (HEADS * SLOT, HEADS * HEAD_DIM), 1) >> 5
    return jnp.where(row == col, 1.0, 0.0).astype(BF)


def segment_max(scores):
    low = lax.broadcasted_iota(jnp.int32, (SLOT, 2 * SLOT), 1) < SLOT
    parts = []
    for start in (0, 2 * SLOT):
        pair = scores[:, start : start + 2 * SLOT]
        first = jnp.max(jnp.where(low, pair, OFF), 1, keepdims=True)
        second = jnp.max(jnp.where(low, OFF, pair), 1, keepdims=True)
        parts.append(jnp.where(low, first, second))
    return jnp.concatenate(parts, 1)


def zero_tails(first_step, count, *refs):
    @pl.when(first_step)
    def _():
        for ref in refs:
            ref[count:, :] = jnp.zeros((ref.shape[0] - count, ref.shape[1]), F32)


def first_of_grid():
    return (pl.program_id(0) == 0) & (pl.program_id(1) == 0)


def window(ref, image, images):
    return ref[pl.ds(image, SLOT, stride=images), :]


def attention_forward(images, parts, bias, masks, probs_ref, out_ref):
    sc_q, sc_k, sc_v = parts
    segments = lane_segments()
    everything = range(images)
    scores = [
        mm_nt(window(sc_q, i, images).astype(BF), head_blocks(window(sc_k, i, images)))
        * (SCALE * LOG2E)
        + bias
        for i in everything
    ]
    if masks is not None:
        apart = [masks[0, 0, i].astype(F32) * (-100.0 * LOG2E) for i in everything]
        scores = [scores[i] + jnp.concatenate([apart[i], apart[i]], 1) for i in everything]
    powers = [jnp.exp2(s - segment_max(s)) for s in scores]
    sums = [mm(p.astype(BF), segments) for p in powers]
    probs = [(p / s).astype(BF) for p, s in zip(powers, sums)]
    for i in everything:
        probs_ref[0, 0, i] = probs[i]
        out_ref[pl.ds(i, SLOT, stride=images), :] = mm(
            probs[i], head_blocks(window(sc_v, i, images))
        )


def attention_backward(images, parts, sc_grad, sc_out, probs_ref, grads, bias_acc):
    sc_q, sc_k, sc_v = parts
    sc_dq, sc_dk, sc_dv = grads
    lanes = head_lanes()
    everything = range(images)
    upstream = [window(sc_grad, i, images) for i in everything]
    centred = [
        mm_nt(
            jnp.concatenate(
                [
                    upstream[i].astype(BF),
                    (-(upstream[i] * window(sc_out, i, images))).astype(BF),
                ],
                1,
            ),
            jnp.concatenate([head_blocks(window(sc_v, i, images)), lanes], 1),
        )
        for i in everything
    ]
    probs = [probs_ref[0, 0, i] for i in everything]
    score_grads = [(probs[i].astype(F32) * centred[i]).astype(BF) for i in everything]
    total = score_grads[0].astype(F32)
    for i in everything[1:]:
        total = total + score_grads[i].astype(F32)
    bias_acc[...] += total
    for i in everything:
        place = pl.ds(i, SLOT, stride=images)
        sc_dq[place, :] = mm(score_grads[i], head_blocks(window(sc_k, i, images))) * SCALE
        sc_dk[place, :] = (
            gather_heads(mm_tn(score_grads[i], window(sc_q, i, images).astype(BF))) * SCALE
        )
        sc_dv[place, :] = gather_heads(mm_tn(probs[i], upstream[i].astype(BF)))


def split_projection(hidden, w_qkv, qkv_bias, parts, count):
    projected = mm(hidden, w_qkv) + qkv_bias
    projected = projected.astype(BF).astype(F32)
    depth = hidden.shape[1]
    for n, ref in enumerate(parts):
        ref[:count, :] = projected[:, n * depth : (n + 1) * depth]


def gelu_parts(expanded):
    cumulative = 0.5 + 0.5 * lax.erf(expanded * (1.0 / math.sqrt(2.0)))
    density = jnp.exp(expanded * expanded * -0.5) * (1.0 / math.sqrt(2.0 * math.pi))
    return expanded * cumulative, cumulative + expanded * density


def kernel_first_layer(
    images, x_ref, w_qkv, w_proj, w_fc1, w_fc2, vecs, qkv_bias, fc1_bias, bias,
    stream_out, hidden_out, middle_out, out_out, probs_out, act_out, slope_out,
    sc_q, sc_k, sc_v, sc_out,
):
    count = POS * images
    zero_tails(first_of_grid(), count, sc_q, sc_k, sc_v)
    stream = tokens_of(x_ref)
    normed, _ = norm_parts(stream)
    hidden = (normed * vecs[0:1] + vecs[1:2]).astype(BF)
    split_projection(hidden, w_qkv[...], qkv_bias[...], (sc_q, sc_k, sc_v), count)
    attention_forward(images, (sc_q, sc_k, sc_v), bias[...], None, probs_out, sc_out)
    attended = sc_out[:count, :].astype(BF)
    out_out[0, 0] = attended
    middle = stream + (mm(attended, w_proj[...]) + vecs[4:5])
    middle_out[0, 0] = middle
    normed, _ = norm_parts(middle)
    inner = (normed * vecs[2:3] + vecs[3:4]).astype(BF)
    activated, slope = gelu_parts(mm(inner, w_fc1[...]) + fc1_bias[...])
    activated = activated.astype(BF)
    act_out[0, 0] = activated
    slope_out[0, 0] = slope.astype(BF)
    stream = middle + mm(activated, w_fc2[...]) + vecs[5:6]
    stream_out[0, 0] = stream
    normed, _ = norm_parts(stream)
    put_tokens(hidden_out, normed * vecs[6:7] + vecs[7:8])


def kernel_shifted_forward(
    images, hidden_ref, w_qkv, qkv_bias, bias, masks, out_out, probs_out, sc_q, sc_k, sc_v, sc_out
):
    count = POS * images
    zero_tails(first_of_grid(), count, sc_q, sc_k, sc_v)
    hidden = tokens_of(hidden_ref).astype(BF)
    split_projection(hidden, w_qkv[...], qkv_bias[...], (sc_q, sc_k, sc_v), count)
    attention_forward(images, (sc_q, sc_k, sc_v), bias[...], masks, probs_out, sc_out)
    put_tokens(out_out, sc_out[:count, :])


def feed_forward_backward(out_low, inner, activated, slope, w_fc1, w_fc2):
    expanded_low = (slope * mm_nt(out_low, w_fc2)).astype(BF)
    inner_grad = mm_nt(expanded_low, w_fc1)
    return expanded_low, inner_grad


def start_sums(refs):
    @pl.when(first_of_grid())
    def _():
        for ref in refs:
            ref[...] = jnp.zeros_like(ref)


def kernel_middle(
    images, stream_ref, out_ref, cot_ref, w_proj, w_fc1, w_fc2, vecs, fc1_bias,
    mixed_out, grad_out, low_out, g_proj, g_fc1, g_fc2, sums, fc1_sums,
):
    start_sums((g_proj, g_fc1, g_fc2, sums, fc1_sums))
    stream = stream_ref[0, 0]
    attended = tokens_of(out_ref).astype(BF)
    middle = stream + (mm(attended, w_proj[...]) + vecs[4:5])
    normed, inverse = norm_parts(middle)
    inner = (normed * vecs[2:3] + vecs[3:4]).astype(BF)
    activated, slope = gelu_parts(mm(inner, w_fc1[...]) + fc1_bias[...])
    activated = activated.astype(BF)
    put_tokens(mixed_out, middle + mm(activated, w_fc2[...]) + vecs[5:6])
    gradient = tokens_of(cot_ref)
    out_low = gradient.astype(BF)
    expanded_low, inner_grad = feed_forward_backward(
        out_low, inner, activated, slope, w_fc1[...], w_fc2[...]
    )
    g_fc2[...] += mm_tn(out_low, activated)
    g_fc1[...] += mm_tn(inner, expanded_low)
    fc1_sums[...] += fold_rows(expanded_low.astype(F32))
    norm_term = norm_backward(inner_grad, normed, inverse, vecs[2:3])
    updated = gradient + norm_term
    grad_out[0, 0] = updated
    branch_low = updated.astype(BF)
    g_proj[...] += mm_tn(attended, branch_low)
    put_tokens(low_out, mm_nt(branch_low, w_proj[...]))
    sums[0] += fold_rows(gradient)
    sums[1] += fold_rows(inner_grad * normed)
    sums[2] += fold_rows(inner_grad)
    sums[3] += fold_rows(branch_low.astype(F32))


def joined_gradients(count, grads, qv_sums):
    pieces = [ref[:count, :].astype(BF) for ref in grads]
    qv_sums[0] += fold_rows(pieces[0].astype(F32))
    qv_sums[1] += fold_rows(pieces[2].astype(F32))
    return jnp.concatenate(pieces, 1)


def kernel_shifted_backward(
    images, hidden_ref, out_ref, low_ref, probs_ref, w_qkv, qkv_bias,
    hidden_grad_out, g_qkv, qv_sums, bias_acc,
    sc_q, sc_k, sc_v, sc_out, sc_grad, sc_dq, sc_dk, sc_dv,
):
    count = POS * images
    start_sums((g_qkv, qv_sums, bias_acc))
    zero_tails(first_of_grid(), count, sc_q, sc_k, sc_v, sc_out, sc_grad)
    hidden = tokens_of(hidden_ref).astype(BF)
    split_projection(hidden, w_qkv[...], qkv_bias[...], (sc_q, sc_k, sc_v), count)
    sc_out[:count, :] = tokens_of(out_ref)
    sc_grad[:count, :] = tokens_of(low_ref)
    grads = (sc_dq, sc_dk, sc_dv)
    attention_backward(images, (sc_q, sc_k, sc_v), sc_grad, sc_out, probs_ref, grads, bias_acc)
    joined = joined_gradients(count, grads, qv_sums)
    g_qkv[...] += mm_tn(hidden, joined)
    put_tokens(hidden_grad_out, mm_nt(joined, w_qkv[...]))


def kernel_first_feed_backward(
    images, hidden_grad_ref, stream_ref, grad_ref, middle_ref, act_ref, slope_ref, att_ref,
    w_proj, w_fc1, w_fc2, vecs,
    grad_out, low_out, g_proj, g_fc1, g_fc2, sums, fc1_sums,
):
    start_sums((g_proj, g_fc1, g_fc2, sums, fc1_sums))
    upstream = tokens_of(hidden_grad_ref)
    normed, inverse = norm_parts(stream_ref[0, 0])
    gradient = grad_ref[0, 0] + norm_backward(upstream, normed, inverse, vecs[6:7])
    sums[4] += fold_rows(upstream * normed)
    sums[5] += fold_rows(upstream)
    out_low = gradient.astype(BF)
    normed, inverse = norm_parts(middle_ref[0, 0])
    inner = (normed * vecs[2:3] + vecs[3:4]).astype(BF)
    activated = act_ref[0, 0]
    expanded_low, inner_grad = feed_forward_backward(
        out_low, inner, activated, slope_ref[0, 0].astype(F32), w_fc1[...], w_fc2[...]
    )
    g_fc2[...] += mm_tn(out_low, activated)
    g_fc1[...] += mm_tn(inner, expanded_low)
    fc1_sums[...] += fold_rows(expanded_low.astype(F32))
    updated = gradient + norm_backward(inner_grad, normed, inverse, vecs[2:3])
    grad_out[0, 0] = updated
    branch_low = updated.astype(BF)
    g_proj[...] += mm_tn(att_ref[0, 0], branch_low)
    low_out[0, 0] = mm_nt(branch_low, w_proj[...]).astype(BF)
    sums[0] += fold_rows(out_low.astype(F32))
    sums[1] += fold_rows(inner_grad * normed)
    sums[2] += fold_rows(inner_grad)
    sums[3] += fold_rows(branch_low.astype(F32))


def kernel_first_attention_backward(
    images, x_ref, grad_ref, low_ref, att_ref, probs_ref, w_qkv, vecs, qkv_bias,
    tokens_grad_out, g_qkv, qv_sums, bias_acc, sums,
    sc_q, sc_k, sc_v, sc_out, sc_grad, sc_dq, sc_dk, sc_dv,
):
    count = POS * images
    start_sums((g_qkv, qv_sums, bias_acc, sums))
    zero_tails(first_of_grid(), count, sc_q, sc_k, sc_v, sc_out, sc_grad)
    normed, inverse = norm_parts(tokens_of(x_ref))
    hidden = (normed * vecs[0:1] + vecs[1:2]).astype(BF)
    split_projection(hidden, w_qkv[...], qkv_bias[...], (sc_q, sc_k, sc_v), count)
    sc_out[:count, :] = att_ref[0, 0].astype(F32)
    sc_grad[:count, :] = low_ref[0, 0].astype(F32)
    grads = (sc_dq, sc_dk, sc_dv)
    attention_backward(images, (sc_q, sc_k, sc_v), sc_grad, sc_out, probs_ref, grads, bias_acc)
    joined = joined_gradients(count, grads, qv_sums)
    g_qkv[...] += mm_tn(hidden, joined)
    upstream = mm_nt(joined, w_qkv[...])
    put_tokens(tokens_grad_out, grad_ref[0, 0] + norm_backward(upstream, normed, inverse, vecs[0:1]))
    sums[0] += fold_rows(upstream * normed)
    sums[1] += fold_rows(upstream)


def shift_by(array, axis, by):
    count = lax.axis_size(axis)
    return lax.ppermute(array, axis, [(i, (i + by) % count) for i in range(count)])


def shift_both(array, by):
    rows, cols = lax.axis_size("seq"), lax.axis_size("wt")
    pairs = [
        (r * cols + c, ((r + by) % rows) * cols + (c + by) % cols)
        for r in range(rows)
        for c in range(cols)
    ]
    return lax.ppermute(array, ("seq", "wt"), pairs)


def roll_ahead(field):
    rim_rows = shift_by(field[:SHIFT], "seq", -1)
    rim_cols = shift_by(field[:, :SHIFT], "wt", -1)
    corner = shift_both(field[:SHIFT, :SHIFT], -1)
    upper = jnp.concatenate([field[SHIFT:, SHIFT:], rim_cols[SHIFT:]], 1)
    lower = jnp.concatenate([rim_rows[:, SHIFT:], corner], 1)
    return jnp.concatenate([upper, lower], 0)


def roll_behind(field):
    rim_rows = shift_by(field[-SHIFT:], "seq", 1)
    rim_cols = shift_by(field[:, -SHIFT:], "wt", 1)
    corner = shift_both(field[-SHIFT:, -SHIFT:], 1)
    upper = jnp.concatenate([corner, rim_rows[:, :-SHIFT]], 1)
    lower = jnp.concatenate([rim_cols[:-SHIFT], field[:-SHIFT, :-SHIFT]], 1)
    return jnp.concatenate([upper, lower], 0)


def pack_second(w_fc2):
    rows, depth = w_fc2.shape
    blocks = w_fc2.reshape(4, rows // 4, depth)
    return blocks.transpose(1, 0, 2).reshape(rows // 4, 4 * depth)


def unpack_second(packed, parts):
    rows, wide = packed.shape
    depth = wide // 4
    blocks = packed.reshape(parts, rows // parts, 4, depth)
    return blocks.transpose(0, 2, 1, 3).reshape(rows * 4, depth)


def per_device(
    tokens, region, rel_index, norm_gain, norm_bias, w_qkv, qv_bias, pos_table, w_proj, out_bias,
    w_fc1, fc1_bias, w_fc2, cotangent,
):
    images, height, width, depth = tokens.shape
    wide = w_fc1.shape[-1]
    parts = lax.axis_size("wt")
    rows, cols = height // WIN, width // WIN
    count = POS * images
    table_size = pos_table.shape[1]

    weights = []
    for layer in range(2):
        packed = jnp.concatenate(
            [w_qkv[layer], w_proj[layer], w_fc1[layer], pack_second(w_fc2[layer])], 1
        )
        whole = lax.all_gather(packed, "wt", axis=0, tiled=True)
        cuts = [3 * depth, 4 * depth, 4 * depth + wide]
        qkv, proj, fc1, fc2 = jnp.split(whole, cuts, 1)
        weights.append((qkv, proj, fc1, unpack_second(fc2, parts)))

    x = tokens.transpose(1, 2, 0, 3)
    cot = cotangent.transpose(1, 2, 0, 3)
    selector = (
        rel_index.reshape(-1)[:, None] == jnp.arange(table_size, dtype=jnp.int32)[None, :]
    ).astype(F32)
    tables = jnp.dot(
        selector,
        pos_table.transpose(1, 0, 2).reshape(table_size, 2 * HEADS) * LOG2E,
        precision=lax.Precision.HIGHEST,
    ).reshape(POS, POS, 2, HEADS)
    padded = jnp.pad(
        jnp.pad(tables.transpose(2, 0, 3, 1), ((0, 0), (0, SLOT - POS), (0, 0), (0, 0))),
        ((0, 0), (0, 0), (0, 0), (0, SLOT - POS)),
        constant_values=OFF,
    )
    biases = padded.reshape(2, SLOT, HEADS * SLOT)
    ids = region.reshape(images, rows, WIN, cols, WIN).transpose(1, 3, 0, 2, 4)
    ids = ids.reshape(rows, cols, images, POS)
    apart = (ids[..., :, None] != ids[..., None, :]).astype(BF)
    apart = jnp.pad(apart, [(0, 0)] * 3 + [(0, SLOT - POS)] * 2)
    masks = jnp.concatenate([apart, apart], -1)

    zeros = jnp.zeros((depth,), F32)
    qkv_biases = [
        jnp.concatenate([qv_bias[l, 0], zeros, qv_bias[l, 1]])[None] for l in range(2)
    ]

    def vectors(layer):
        after = norm_gain[1, 0], norm_bias[1, 0]
        return jnp.stack(
            [
                norm_gain[layer, 0], norm_bias[layer, 0], norm_gain[layer, 1], norm_bias[layer, 1],
                out_bias[layer, 0], out_bias[layer, 1], *after,
            ]
        )

    vecs = [vectors(0), vectors(1)]

    field = pl.BlockSpec((WIN, WIN, images, depth), lambda r, c: (r, c, 0, 0))
    probs_spec = pl.BlockSpec((1, 1, images, SLOT, HEADS * SLOT), lambda r, c: (r, c, 0, 0, 0))
    mask_spec = pl.BlockSpec((1, 1, images, SLOT, 2 * SLOT), lambda r, c: (r, c, 0, 0, 0))

    def flat(columns):
        return pl.BlockSpec((1, 1, count, columns), lambda r, c: (r, c, 0, 0))

    def whole_of(shape):
        return pl.BlockSpec(tuple(shape), lambda r, c: (0,) * len(shape))

    field_shape = (height, width, images, depth)

    def flat_type(columns, dtype):
        return jax.ShapeDtypeStruct((rows, cols, count, columns), dtype)

    probs_type = jax.ShapeDtypeStruct((rows, cols, images, SLOT, HEADS * SLOT), BF)

    def run(kernel, inputs, outputs, slots):
        def body(*refs):
            kernel(images, *refs)

        return pl.pallas_call(
            body,
            grid=(rows, cols),
            in_specs=[spec if spec is not None else whole_of(a.shape) for a, spec in inputs],
            out_specs=[spec if spec is not None else whole_of(t.shape) for t, spec in outputs],
            out_shape=[t for t, _ in outputs],
            scratch_shapes=[pltpu.VMEM((SLOT * images, depth), F32)] * slots,
            compiler_params=pltpu.CompilerParams(vmem_limit_bytes=VMEM_LIMIT),
        )(*[a for a, _ in inputs])

    def total(*shape):
        return (jax.ShapeDtypeStruct(shape, F32), None)

    qkv0, proj0, fc10, fc20 = weights[0]
    qkv1, proj1, fc11, fc21 = weights[1]
    stream1, hidden1, middle0, att0, probs0, act0, slope0 = run(
        kernel_first_layer,
        [
            (x, field), (qkv0, None), (proj0, None), (fc10, None), (fc20, None), (vecs[0], None),
            (qkv_biases[0], None), (fc1_bias[0:1], None), (biases[0], None),
        ],
        [
            (flat_type(depth, F32), flat(depth)),
            (jax.ShapeDtypeStruct(field_shape, BF), field),
            (flat_type(depth, F32), flat(depth)),
            (flat_type(depth, BF), flat(depth)),
            (probs_type, probs_spec),
            (flat_type(wide, BF), flat(wide)),
            (flat_type(wide, BF), flat(wide)),
        ],
        4,
    )
    hidden1 = roll_ahead(hidden1)
    att1, probs1 = run(
        kernel_shifted_forward,
        [
            (hidden1, field), (qkv1, None), (qkv_biases[1], None), (biases[1], None),
            (masks, mask_spec),
        ],
        [(jax.ShapeDtypeStruct(field_shape, BF), field), (probs_type, probs_spec)],
        4,
    )
    mixed, grad1, low1, g_proj1, g_fc11, g_fc21, sums1, fc1_sums1 = run(
        kernel_middle,
        [
            (stream1, flat(depth)), (roll_behind(att1), field), (cot, field), (proj1, None),
            (fc11, None), (fc21, None), (vecs[1], None), (fc1_bias[1:2], None),
        ],
        [
            (jax.ShapeDtypeStruct(field_shape, BF), field),
            (flat_type(depth, F32), flat(depth)),
            (jax.ShapeDtypeStruct(field_shape, BF), field),
            total(depth, depth), total(depth, wide), total(depth, wide), total(4, 8, depth),
            total(8, wide),
        ],
        0,
    )
    hidden_grad1, g_qkv1, qv_sums1, bias_sums1 = run(
        kernel_shifted_backward,
        [
            (hidden1, field), (att1, field), (roll_ahead(low1), field), (probs1, probs_spec),
            (qkv1, None), (qkv_biases[1], None),
        ],
        [
            (jax.ShapeDtypeStruct(field_shape, BF), field),
            total(depth, 3 * depth), total(2, 8, depth), total(SLOT, HEADS * SLOT),
        ],
        8,
    )
    grad0, low0, g_proj0, g_fc10, g_fc20, sums0, fc1_sums0 = run(
        kernel_first_feed_backward,
        [
            (roll_behind(hidden_grad1), field), (stream1, flat(depth)), (grad1, flat(depth)),
            (middle0, flat(depth)), (act0, flat(wide)), (slope0, flat(wide)), (att0, flat(depth)),
            (proj0, None), (fc10, None), (fc20, None), (vecs[0], None),
        ],
        [
            (flat_type(depth, F32), flat(depth)), (flat_type(depth, BF), flat(depth)),
            total(depth, depth), total(depth, wide), total(depth, wide), total(6, 8, depth),
            total(8, wide),
        ],
        0,
    )
    tokens_grad, g_qkv0, qv_sums0, bias_sums0, sums00 = run(
        kernel_first_attention_backward,
        [
            (x, field), (grad0, flat(depth)), (low0, flat(depth)), (att0, flat(depth)),
            (probs0, probs_spec), (qkv0, None), (vecs[0], None), (qkv_biases[0], None),
        ],
        [
            (jax.ShapeDtypeStruct(field_shape, F32), field),
            total(depth, 3 * depth), total(2, 8, depth), total(SLOT, HEADS * SLOT),
            total(2, 8, depth),
        ],
        8,
    )

    owned = []
    for g_qkv, g_proj, g_fc1, g_fc2 in (
        (g_qkv0, g_proj0, g_fc10, g_fc20), (g_qkv1, g_proj1, g_fc11, g_fc21)
    ):
        packed = jnp.concatenate(
            [g_qkv, g_proj, g_fc1, g_fc2.reshape(depth, parts, -1).transpose(1, 2, 0).reshape(parts, wide // parts, depth).reshape(parts, 4, -1, depth).transpose(0, 2, 1, 3).reshape(depth, wide)], 1
        ).astype(BF)
        mine = lax.psum_scatter(packed, "wt", scatter_dimension=0, tiled=True)
        mine = lax.psum(mine, "seq").astype(F32)
        a, b, c, d = jnp.split(mine, [3 * depth, 4 * depth, 4 * depth + wide], 1)
        owned.append((a, b, c, unpack_second(d, 1)))

    def one(sums):
        return jnp.sum(sums, -2)

    sums0, sums1, sums00 = one(sums0), one(sums1), one(sums00)
    bias_sums = jnp.stack([bias_sums0, bias_sums1]).reshape(2, SLOT, HEADS, SLOT)
    bias_sums = bias_sums[:, :POS, :, :POS].transpose(1, 3, 0, 2).reshape(POS * POS, 2 * HEADS)
    table_grads = jnp.dot(selector.T, bias_sums, precision=lax.Precision.HIGHEST)
    table_grads = table_grads.reshape(table_size, 2, HEADS).transpose(1, 0, 2)
    small = lax.psum(
        (
            jnp.stack([jnp.stack([sums00[0], sums0[1]]), jnp.stack([sums0[4], sums1[1]])]),
            jnp.stack([jnp.stack([sums00[1], sums0[2]]), jnp.stack([sums0[5], sums1[2]])]),
            jnp.stack([one(qv_sums0), one(qv_sums1)]),
            table_grads,
            jnp.stack([jnp.stack([sums0[3], sums0[0]]), jnp.stack([sums1[3], sums1[0]])]),
            jnp.stack([one(fc1_sums0), one(fc1_sums1)]),
        ),
        ("seq", "wt"),
    )

    def both(index):
        return jnp.stack([owned[0][index], owned[1][index]])

    return (
        mixed.transpose(2, 0, 1, 3),
        tokens_grad.transpose(2, 0, 1, 3),
        small[0],
        small[1],
        both(0),
        small[2],
        small[3],
        both(1),
        small[4],
        both(2),
        small[5],
        both(3),
    )


def solution(mesh):
    field = P(None, "seq", "wt", None)
    shared = P(None, "wt", None)
    return jax.shard_map(
        per_device,
        mesh=mesh,
        in_specs=(
            field, P(None, "seq", "wt"), P(), P(), P(), shared, P(), P(), shared, P(), shared, P(),
            shared, field,
        ),
        out_specs=(
            field, field, P(), P(), shared, P(), P(), shared, P(), shared, P(), shared,
        ),
        check_vma=False,
    )
```

time: 974 us -> 362 us (0.37)
  local copies, waits for them, and re-layouts: 298 us -> 33.6 us
  matrix products: 235 us -> 2.85 us
  Pallas kernels: 0 us -> 167 us
  other arithmetic: 185 us -> 18.2 us
  waiting for transfers between devices: 125 us -> 42.4 us
  blocking collectives: 96.1 us -> 70.4 us
    dot_general x40 -> x2, matrix products: 235 us -> 2.85 us  [the longest x1 1.96 us: per_device(): jnp.dot(selector, pos_table.transpose(1, 0, 2).reshape(table_size, 2 * HE...]
    pallas_call x0 -> x6, Pallas kernels: none -> 167 us  [run(): pl.pallas_call(body, grid=(rows, cols), in_specs=[spec if spec is not Non...]
    convert_element_type x13 -> x0, local copies, waits for them, and re-layouts: 103 us -> none  [the longest x4 37.2 us: per_device(): attended.reshape(window_count, WIN * WIN, depth).astype(jnp.bfloat16)]
    reduce_sum x15 -> x7, other arithmetic: 86.7 us -> 0.84 us  [one(): return jnp.sum(sums, -2)]
    convert_element_type x8 -> x2, other arithmetic: 79.6 us -> 1.81 us  [per_device(): mine = lax.psum(mine, 'seq').astype(F32)]
    reshape x14 -> x8, local copies, waits for them, and re-layouts: 61 us -> 0.71 us  [the longest x2 0.24 us: per_device(): g_fc2.reshape(depth, parts, -1).transpose(1, 2, 0)]
    concatenate x16 -> x0, local copies, waits for them, and re-layouts: 58.1 us -> none  [the longest x12 53.9 us: per_device(): jnp.concatenate([query_grad.reshape(flat_shape), key_grad.reshape(flat_sh...]
    psum x2 -> x1, waiting for transfers between devices: 67.7 us -> 15.8 us  [per_device(): mine = lax.psum(mine, 'seq').astype(F32)]
  transfers between devices with their start and end apart: 14 -> 15, of which waited for: 9 -> 9; matrix products, arithmetic and copies ran while one was open for 17% -> 7% of each run, Pallas kernels for 0% -> 15%
where the time goes in v1:
time: 362 us; the launch traced here: 360 us
  Pallas kernels  167 us (46%)
  blocking collectives  70.4 us (19%)
  waiting for transfers between devices  42.4 us (12%)
  local copies, waits for them, and re-layouts  33.6 us (9%)
  other arithmetic  18.2 us (5%)
  between operations  14.7 us (4%)
  starting transfers between devices  11.3 us (3%)
    pallas_call x6, Pallas kernels, run(): pl.pallas_call(body, grid=(rows, cols), in_specs=[spec if spec is not Non...  167 us
    psum x1, blocking collectives, per_device(): lax.psum((jnp.stack([jnp.stack([sums00[0], sums0[1]]), jnp.stack([sums0[4...  39 us
    all_gather x2, blocking collectives, per_device(): whole = lax.all_gather(packed, 'wt', axis=0, tiled=True)  31.3 us
    reduce_scatter x2, waiting for transfers between devices, per_device(): mine = lax.psum_scatter(packed, 'wt', scatter_dimension=0, tiled=True)  17.1 us
    psum x1, waiting for transfers between devices, per_device(): mine = lax.psum(mine, 'seq').astype(F32)  15.8 us
  transfers between devices with their start and end apart: 15, of which 9 were waited for; matrix products, arithmetic and copies ran while one was open for 7% of the time, Pallas kernels for 15%

profile of v1, /device:TPU:0, one launch (start us, length us, event | category | flops | bytes accessed | tf_op | source)
XLA Modules:
  0.0 360.1 jit_solution(2455638090418632031)
XLA Ops:
  7.3 0.8 fusion.20
  8.1 0.8 slice_bitcast_fusion.4
  8.9 0.8 slice_bitcast_fusion.6
  9.6 0.7 slice_bitcast_fusion.10
  10.4 16.2 %all_gather.6 = bf16[128,1536]{1,0:T(8,128)(2,1)S(1)} all-gather(bf16[32,1536]{1,0:T(8,128)(2,1)S(1)} %pad_maximum_fusion.5), channel_id=1, replica_groups=mesh['seq'=8,'wt'=4] {'wt'}, dimensions={0}, use_global_device_ids=true | all-gather | bytes 491520 | tf_op jit(solution)/shard_map/all_gather | solution.py:418
  26.6 0.7 fusion.18
  29.2 0.7 copy.35
  29.9 2.0 fusion.7
  32.0 0.8 squeeze.41.refs_8_
  34.0 40.2 %shard_map.229 = (f32[4,4,392,128]{3,2,1,0:T(8,128)}, bf16[28,28,8,128]{3,2,1,0:T(8,128)(2,1)}, f32[4,4,392,128]{3,2,1,0:T(8,128)}, bf16[4,4,392,128]{3,2,1,0:T(...) custom-call(bf16[28,28,8,128]{3,2,1,0:T(8,128)(2,1)} %bitcast.156, ...), custom_call_target="tpu_custom_call" | custom-call | tf_op jit(solution)/shard_map/pallas_call | solution.py:482
  74.2 0.9 slice.218
  75.2 4.2 %collective-permute-start = (bf16[28,3,8,128]{3,2,1,0:T(8,128)(2,1)S(1)}, bf16[28,3,8,128]{3,2,1,0:T(8,128)(2,1)S(1)}, u32[]{:S(2)}, u32[]{:S(2)}) collective-permute-start(bf16[28,3,8,128]{3,2,1,0:T(8,128)(2,1)S(1)} %slice.218), channel_id=1, source_target_pairs={{0,3},{1,0},{2,1},{3,2},{4,7},{5,4},{6,5},{7,6},{8,11},{9,8},{10,9... | collective-permute-start | bytes 516104 | tf_op jit(solution)/shard_map/ppermute | solution.py:358
  79.3 0.9 slice.220
  80.3 0.7 slice.222
  81.0 2.0 collective-permute-start.2
  83.8 1.3 broadcast_compare_fusion
  85.7 2.6 add_convert_fusion.refs_4_
  88.3 15.1 %all_gather.7 = bf16[128,1536]{1,0:T(8,128)(2,1)S(1)} all-gather(bf16[32,1536]{1,0:T(8,128)(2,1)S(1)} %pad_maximum_fusion.6), channel_id=1, replica_groups=mesh['seq'=8,'wt'=4] {'wt'}, dimensions={0}, use_global_device_ids=true | all-gather | bytes 491520 | tf_op jit(solution)/shard_map/all_gather | solution.py:418
  104.7 0.8 squeeze.47.refs_3_
  105.5 1.3 maximum_maximum_fusion.refs_0_
  106.8 19.7 %shard_map.230 = (bf16[28,28,8,128]{3,2,1,0:T(8,128)(2,1)}, bf16[4,4,8,64,256]{4,3,2,1,0:T(8,128)(2,1)}) custom-call(bf16[28,28,8,128]{3,2,1,0:T(8,128)(2,1)} %maximum_maximum_fusion.refs_0_, bf16[128,384]{1,0:T(8,128)(2,1)} %split.68.refs_1_.refs_4_, f32[1,384]{1,0:T(1,128)} %broadcast_in_dim.12.refs_2_.refs_5_, f32[64,256]{1,0:T(8,128)} %squeeze.47.refs_3_, ...), custom_call_target="tpu_custom_call" | custom-call | tf_op jit(solution)/shard_map/pallas_call | solution.py:482
  126.5 1.1 slice.231
  127.6 0.9 slice.233
  128.5 0.7 slice.230
  129.5 0.7 fusion.17
  130.8 0.7 eq.41
  131.6 0.7 copy.38
  132.9 2.0 collective-permute-done.4
  135.0 2.2 collective-permute-done.5
  137.2 1.4 collective-permute-done.3
  138.6 1.3 maximum_maximum_fusion.1.refs_1_
  139.9 27.1 %shard_map.231 = (bf16[28,28,8,128]{3,2,1,0:T(8,128)(2,1)}, f32[4,4,392,128]{3,2,1,0:T(8,128)}, bf16[28,28,8,128]{3,2,1,0:T(8,128)(2,1)}, f32[128,128]{1,0:T(8,1...) custom-call(f32[4,4,392,128]{3,2,1,0:T(8,128)} %get-tuple-element.45.refs_0_.refs_1_, ...), custom_call_target="tpu_custom_call" | custom-call | tf_op jit(solution)/shard_map/pallas_call | solution.py:482
  167.1 1.0 slice.242
  168.1 0.9 slice.244
  169.0 0.7 slice.246
  169.9 1.8 collective-permute-start.8
  171.6 0.7 reduce_sum.65
  172.9 1.4 slice.241
  175.2 1.3 maximum_maximum_fusion.2.refs_2_
  176.6 25.9 %shard_map.232 = (bf16[28,28,8,128]{3,2,1,0:T(8,128)(2,1)}, f32[128,384]{1,0:T(8,128)}, f32[2,8,128]{2,1,0:T(8,128)}, f32[64,256]{1,0:T(8,128)}) custom-call(bf16[28,28,8,128]{3,2,1,0:T(8,128)(2,1)} %maximum_maximum_fusion.refs_0_, bf16[28,28,8,128]{3,2,1,0:T(8,128)(2,1)} %get-tuple-element.47.refs_1_, ...), custom_call_target="tpu_custom_call" | custom-call | tf_op jit(solution)/shard_map/pallas_call | solution.py:482
  202.4 1.1 slice.248
  203.5 0.9 slice.250
  204.5 1.3 slice.247
  205.8 1.1 collective-permute-start.11
  206.9 1.6 collective-permute-start.9
  208.5 0.9 convert.41
  209.5 0.8 pad_maximum_fusion.1
  211.6 0.9 slice.274
  212.5 2.1 collective-permute-done.11
  214.6 0.9 slice.275
  215.5 0.9 collective-permute-done.9
  216.5 1.3 maximum_maximum_fusion.3.refs_0_
  217.8 22.2 %shard_map.233 = (f32[4,4,392,128]{3,2,1,0:T(8,128)}, bf16[4,4,392,128]{3,2,1,0:T(8,128)(2,1)}, f32[128,128]{1,0:T(8,128)}, f32[128,512]{1,0:T(8,128)}, f32[128,...) custom-call(bf16[28,28,8,128]{3,2,1,0:T(8,128)(2,1)} %maximum_maximum_fusion.3.refs_0_, ...), custom_call_target="tpu_custom_call" | custom-call | tf_op jit(solution)/shard_map/pallas_call | solution.py:482
  240.0 31.7 %shard_map.234 = (f32[28,28,8,128]{3,2,1,0:T(8,128)}, f32[128,384]{1,0:T(8,128)}, f32[2,8,128]{2,1,0:T(8,128)}, f32[64,256]{1,0:T(8,128)}, f32[2,8,128]{2,1,0:T(8,128)}) custom-call(bf16[28,28,8,128]{3,2,1,0:T(8,128)(2,1)} %bitcast.157, f32[4,4,392,128]{3,2,1,0:T(8,128)} %get-tuple-element.57.refs_1_, bf16[4,4,392,128]{3,2,1,0:T(8,128)(2,1)} %get-tuple-element.58.refs_2_, ...), custom_call_target="tpu_custom_call" | custom-call | tf_op jit(solution)/shard_map/pallas_call | solution.py:482
  271.7 1.0 convert.37
  273.5 0.8 pad_maximum_fusion
  274.6 0.9 fusion.10
  275.5 17.1 %reduce-scatter.3.cloned.1.call-done = bf16[32,1536]{1,0:T(8,128)(2,1)} async-done(((bf16[128,1536]{1,0:T(8,128)(2,1)}), bf16[32,1536]{1,0:T(8,128)(2,1)}) %reduce-scatter.3.cloned.1.call-update) | async-done | bytes 98320 | tf_op jit(solution)/shard_map/reduce_scatter | solution.py:586
  292.6 39.0 %all-reduce.3 = (f32[2,2,128]{2,1,0:T(2,128)}, f32[2,2,128]{2,1,0:T(2,128)}, f32[2,2,128]{2,1,0:T(2,128)}, f32[2,169,4]{1,2,0:T(4,128)}, f32[2,2,128]{2,1,0:T(2,128)}, /*index=5*/f32[2,512]{1,0:T(2,128)}) all-reduce(f32[2,2,128]{2,1,0:T(2,128)S(1)} %pad_maximum_fusion.12, ...), channel_id=1, replica_groups=mesh['seq'=8,'wt'=4] {'seq','wt'}, use_global_device_ids=true, to_apply=%region_3.4 | all-reduce | flops 4424 | bytes 35392 | tf_op jit(solution)/shard_map/psum | solution.py:599
  331.6 15.8 %all-reduce.7.cloned.1.call-done = (bf16[32,1536]{1,0:T(8,128)(2,1)}, bf16[32,1536]{1,0:T(8,128)(2,1)}) async-done(((bf16[32,1536]{1,0:T(8,128)(2,1)}, bf16[32,1536]{1,0:T(8,128)(2,1)}), (bf16[32,1536]{1,0:T(8,128)(2,1)}, bf16[32,1536]{1,0:T(8,128)(2,1)})) %all-reduce.7.cloned.1.call-update) | async-done | bytes 196624 | tf_op jit(solution)/shard_map/psum | solution.py:587
  347.4 0.8 split.79
  348.2 0.9 convert_element_type.9
  349.1 0.8 split.78
  349.9 0.9 convert_element_type.8
  (170 shorter events, 14.0 us)
Async XLA Ops:
  7.2 21.4 %copy-start.22 = (f32[2,2,128]{2,1,0:T(2,128)S(1)}, f32[2,2,128]{2,1,0:T(2,128)}, u32[]{:S(2)}) copy-start(f32[2,2,128]{2,1,0:T(2,128)} %param.17) | copy-start | bytes 6148
  7.2 21.4 %copy-start.23 = (f32[2,2,128]{2,1,0:T(2,128)S(1)}, f32[2,2,128]{2,1,0:T(2,128)}, u32[]{:S(2)}) copy-start(f32[2,2,128]{2,1,0:T(2,128)} %param.20) | copy-start | bytes 6148
  7.2 22.7 %copy-start.20 = (f32[2,169,4]{1,2,0:T(4,128)S(1)}, f32[2,169,4]{1,2,0:T(4,128)}, u32[]{:S(2)}) copy-start(f32[2,169,4]{1,2,0:T(4,128)} %param.21) | copy-start | bytes 16228
  7.2 22.7 %copy-start.12 = (s32[49,49]{1,0:T(8,128)S(1)}, s32[49,49]{1,0:T(8,128)}, u32[]{:S(2)}) copy-start(s32[49,49]{1,0:T(8,128)} %param.16) | copy-start | bytes 28816
  7.2 268.2 %reduce-scatter.5.cloned.1.call-start = ((), (), s32[]{:S(2)}) async-start(), calls=%async_computation.3 | async-start | bytes 491520 | tf_op jit(solution)/shard_map/reduce_scatter | solution.py:586
  26.6 6.2 %copy-start.21 = (f32[2,512]{1,0:T(2,128)S(1)}, f32[2,512]{1,0:T(2,128)}, u32[]{:S(2)}) copy-start(f32[2,512]{1,0:T(2,128)} %param.25) | copy-start | bytes 12292
  26.6 6.8 %copy-start.24 = (f32[2,2,128]{2,1,0:T(2,128)S(1)}, f32[2,2,128]{2,1,0:T(2,128)}, u32[]{:S(2)}) copy-start(f32[2,2,128]{2,1,0:T(2,128)} %param.23) | copy-start | bytes 6148
  26.6 6.8 %copy-start.25 = (f32[2,2,128]{2,1,0:T(2,128)S(1)}, f32[2,2,128]{2,1,0:T(2,128)}, u32[]{:S(2)}) copy-start(f32[2,2,128]{2,1,0:T(2,128)} %param.18) | copy-start | bytes 6148
  32.0 51.1 %copy-start.7 = (s32[8,28,28]{2,0,1:T(8,128)S(1)}, s32[8,28,28]{2,0,1:T(8,128)}, u32[]{:S(2)}) copy-start(s32[8,28,28]{2,0,1:T(8,128)} %param.15) | copy-start | bytes 75268
  75.2 30.3 %collective-permute-start = (bf16[28,3,8,128]{3,2,1,0:T(8,128)(2,1)S(1)}, bf16[28,3,8,128]{3,2,1,0:T(8,128)(2,1)S(1)}, u32[]{:S(2)}, u32[]{:S(2)}) collective-permute-start(bf16[28,3,8,128]{3,2,1,0:T(8,128)(2,1)S(1)} %slice.218), channel_id=1, source_target_pairs={{0,3},{1,0},{2,1},{3,2},{4,7},{5,4},{6,5},{7,6},{8,11},{9,8},{10,9... | collective-permute-start | bytes 516104 | tf_op jit(solution)/shard_map/ppermute | solution.py:358
  80.2 25.2 %collective-permute-start.1 = (bf16[3,28,8,128]{3,2,1,0:T(8,128)(2,1)S(1)}, bf16[3,28,8,128]{3,2,1,0:T(8,128)(2,1)S(1)}, u32[]{:S(2)}, u32[]{:S(2)}) collective-permute-start(bf16[3,28,8,128]{3,2,1,0:T(8,128)(2,1)S(1)} %slice.220), channel_id=1, source_target_pairs={{0,28},{4,0},{8,4},{12,8},{16,12},{20,16},{24,20},{28,24},{1,29},{... | collective-permute-start | bytes 516104 | tf_op jit(solution)/shard_map/ppermute | solution.py:358
  81.0 24.5 %collective-permute-start.2 = (bf16[3,3,8,128]{3,2,1,0:T(8,128)(2,1)S(1)}, bf16[3,3,8,128]{3,2,1,0:T(8,128)(2,1)S(1)}, u32[]{:S(2)}, u32[]{:S(2)}) collective-permute-start(bf16[3,3,8,128]{3,2,1,0:T(8,128)(2,1)S(1)} %slice.222), channel_id=1, source_target_pairs={{0,31},{1,28},{2,29},{3,30},{4,3},{5,0},{6,1},{7,2},{8,7},{9,4},{1... | collective-permute-start | bytes 55304 | tf_op jit(solution)/shard_map/ppermute | solution.py:368
  85.7 17.7 %copy-start.1 = (bf16[28,28,8,128]{3,2,1,0:T(8,128)(2,1)S(1)}, bf16[28,28,8,128]{3,2,1,0:T(8,128)(2,1)}, u32[]{:S(2)}) copy-start(bf16[28,28,8,128]{3,2,1,0:T(8,128)(2,1)} %get-tuple-element.46) | copy-start | bytes 4816900
  126.5 6.3 %copy-start = (bf16[28,28,8,128]{3,2,1,0:T(8,128)(2,1)S(1)}, bf16[28,28,8,128]{3,2,1,0:T(8,128)(2,1)}, u32[]{:S(2)}) copy-start(bf16[28,28,8,128]{3,2,1,0:T(8,128)(2,1)} %get-tuple-element.47.refs_1_) | copy-start | bytes 4816900
  129.3 5.7 %collective-permute-start.4 = (bf16[3,28,8,128]{3,2,1,0:T(8,128)(2,1)S(1)}, bf16[3,28,8,128]{3,2,1,0:T(8,128)(2,1)S(1)}, u32[]{:S(2)}, u32[]{:S(2)}) collective-permute-start(bf16[3,28,8,128]{3,2,1,0:T(8,128)(2,1)S(1)} %slice.231), channel_id=1, source_target_pairs={{0,4},{4,8},{8,12},{12,16},{16,20},{20,24},{24,28},{28,0},{1,5},{5... | collective-permute-start | bytes 516104 | tf_op jit(solution)/shard_map/ppermute | solution.py:358
  129.3 7.9 %collective-permute-start.5 = (bf16[28,3,8,128]{3,2,1,0:T(8,128)(2,1)S(1)}, bf16[28,3,8,128]{3,2,1,0:T(8,128)(2,1)S(1)}, u32[]{:S(2)}, u32[]{:S(2)}) collective-permute-start(bf16[28,3,8,128]{3,2,1,0:T(8,128)(2,1)S(1)} %slice.233), channel_id=1, source_target_pairs={{0,1},{1,2},{2,3},{3,0},{4,5},{5,6},{6,7},{7,4},{8,9},{9,10},{10,1... | collective-permute-start | bytes 516104 | tf_op jit(solution)/shard_map/ppermute | solution.py:358
  129.5 9.1 %collective-permute-start.3 = (bf16[3,3,8,128]{3,2,1,0:T(8,128)(2,1)S(1)}, bf16[3,3,8,128]{3,2,1,0:T(8,128)(2,1)S(1)}, u32[]{:S(2)}, u32[]{:S(2)}) collective-permute-start(bf16[3,3,8,128]{3,2,1,0:T(8,128)(2,1)S(1)} %slice.230), channel_id=1, source_target_pairs={{0,5},{1,6},{2,7},{3,4},{4,9},{5,10},{6,11},{7,8},{8,13},{9,14},{1... | collective-permute-start | bytes 55304 | tf_op jit(solution)/shard_map/ppermute | solution.py:368
  167.1 7.3 %copy-start.4 = (f32[128,512]{1,0:T(8,128)S(1)}, f32[128,512]{1,0:T(8,128)}, u32[]{:S(2)}) copy-start(f32[128,512]{1,0:T(8,128)} %get-tuple-element.71) | copy-start | bytes 786436
  169.7 5.4 %collective-permute-start.6 = (bf16[28,3,8,128]{3,2,1,0:T(8,128)(2,1)S(1)}, bf16[28,3,8,128]{3,2,1,0:T(8,128)(2,1)S(1)}, u32[]{:S(2)}, u32[]{:S(2)}) collective-permute-start(bf16[28,3,8,128]{3,2,1,0:T(8,128)(2,1)S(1)} %slice.242), channel_id=1, source_target_pairs={{0,3},{1,0},{2,1},{3,2},{4,7},{5,4},{6,5},{7,6},{8,11},{9,8},{10,9... | collective-permute-start | bytes 516104 | tf_op jit(solution)/shard_map/ppermute | solution.py:358
  169.8 5.4 %collective-permute-start.7 = (bf16[3,28,8,128]{3,2,1,0:T(8,128)(2,1)S(1)}, bf16[3,28,8,128]{3,2,1,0:T(8,128)(2,1)S(1)}, u32[]{:S(2)}, u32[]{:S(2)}) collective-permute-start(bf16[3,28,8,128]{3,2,1,0:T(8,128)(2,1)S(1)} %slice.244), channel_id=1, source_target_pairs={{0,28},{4,0},{8,4},{12,8},{16,12},{20,16},{24,20},{28,24},{1,29},{... | collective-permute-start | bytes 516104 | tf_op jit(solution)/shard_map/ppermute | solution.py:358
  169.9 5.4 %collective-permute-start.8 = (bf16[3,3,8,128]{3,2,1,0:T(8,128)(2,1)S(1)}, bf16[3,3,8,128]{3,2,1,0:T(8,128)(2,1)S(1)}, u32[]{:S(2)}, u32[]{:S(2)}) collective-permute-start(bf16[3,3,8,128]{3,2,1,0:T(8,128)(2,1)S(1)} %slice.246), channel_id=1, source_target_pairs={{0,31},{1,28},{2,29},{3,30},{4,3},{5,0},{6,1},{7,2},{8,7},{9,4},{1... | collective-permute-start | bytes 55304 | tf_op jit(solution)/shard_map/ppermute | solution.py:368
  172.9 1.8 copy-start.3
  172.9 1.8 copy-start.10
  172.9 1.8 copy-start.14
  202.4 7.8 %copy-start.2 = (bf16[28,28,8,128]{3,2,1,0:T(8,128)(2,1)S(1)}, bf16[28,28,8,128]{3,2,1,0:T(8,128)(2,1)}, u32[]{:S(2)}) copy-start(bf16[28,28,8,128]{3,2,1,0:T(8,128)(2,1)} %get-tuple-element.51) | copy-start | bytes 4816900
  205.8 5.8 %collective-permute-start.10 = (bf16[3,28,8,128]{3,2,1,0:T(8,128)(2,1)S(1)}, bf16[3,28,8,128]{3,2,1,0:T(8,128)(2,1)}, u32[]{:S(2)}, u32[]{:S(2)}) collective-permute-start(bf16[3,28,8,128]{3,2,1,0:T(8,128)(2,1)S(1)} %slice.248), channel_id=1, source_target_pairs={{0,4},{4,8},{8,12},{12,16},{16,20},{20,24},{24,28},{28,0},{1,5},{5... | collective-permute-start | bytes 516104 | tf_op jit(solution)/shard_map/ppermute | solution.py:358
  205.8 8.8 %collective-permute-start.11 = (bf16[28,3,8,128]{3,2,1,0:T(8,128)(2,1)S(1)}, bf16[28,3,8,128]{3,2,1,0:T(8,128)(2,1)}, u32[]{:S(2)}, u32[]{:S(2)}) collective-permute-start(bf16[28,3,8,128]{3,2,1,0:T(8,128)(2,1)S(1)} %slice.250), channel_id=1, source_target_pairs={{0,1},{1,2},{2,3},{3,0},{4,5},{5,6},{6,7},{7,4},{8,9},{9,10},{10,1... | collective-permute-start | bytes 516104 | tf_op jit(solution)/shard_map/ppermute | solution.py:358
  206.9 9.6 %collective-permute-start.9 = (bf16[3,3,8,128]{3,2,1,0:T(8,128)(2,1)}, bf16[3,3,8,128]{3,2,1,0:T(8,128)(2,1)S(1)}, u32[]{:S(2)}, u32[]{:S(2)}) collective-permute-start(bf16[3,3,8,128]{3,2,1,0:T(8,128)(2,1)} %slice.247), channel_id=1, source_target_pairs={{0,5},{1,6},{2,7},{3,4},{4,9},{5,10},{6,11},{7,8},{8,13},{9,14},{1... | collective-permute-start | bytes 55304 | tf_op jit(solution)/shard_map/ppermute | solution.py:368
  210.3 0.8 copy-start.8
  210.3 1.0 copy-start.17
  210.4 82.2 %reduce-scatter.3.cloned.1.call-start = ((), (), s32[]{:S(2)}) async-start(), calls=%async_computation.2 | async-start | bytes 491520 | tf_op jit(solution)/shard_map/reduce_scatter | solution.py:586
  240.0 32.8 %copy-start.6 = (f32[128,512]{1,0:T(8,128)S(1)}, f32[128,512]{1,0:T(8,128)}, u32[]{:S(2)}) copy-start(f32[128,512]{1,0:T(8,128)} %get-tuple-element.67) | copy-start | bytes 786436
  271.6 1.4 copy-start.5
  271.7 1.4 copy-start.11
  271.7 1.4 copy-start.15
  271.7 1.4 copy-start.13
  271.7 1.4 copy-start.9
  272.7 0.8 copy-start.19
  272.7 0.8 copy-start.18
  273.0 1.4 copy-start.27
  273.0 1.5 copy-start.26
  273.0 1.5 copy-start.16
  274.3 73.1 %all-reduce.7.cloned.1.call-start = ((), (), s32[]{:S(2)}) async-start(), calls=%async_computation.4 | async-start | bytes 393216 | tf_op jit(solution)/shard_map/psum | solution.py:587
Sparse Core Ops, SparseCore 0:
  210.5 20.1 reduce-scatter.4
  274.5 18.0 reduce-scatter.2
  295.6 51.7 all-reduce.6

commit v2 on v1

--- a/solution.py
+++ b/solution.py
@@ -54,13 +54,18 @@
     return jnp.sum(field.reshape(rows // 8, 8, cols), 0)
 
 
+def tokens_of_block(block):
+    return block.astype(F32).reshape(-1, block.shape[-1])
+
+
 def tokens_of(ref):
-    block = ref[...].astype(F32)
-    return block.reshape(-1, block.shape[-1])
+    return tokens_of_block(ref[...])
 
 
 def put_tokens(ref, field):
-    ref[...] = field.reshape(ref.shape).astype(ref.dtype)
+    block = field.reshape(ref.shape).astype(ref.dtype)
+    ref[...] = block
+    return block
 
 
 def head_blocks(field):
@@ -109,7 +114,7 @@
 
 
 def first_of_grid():
-    return (pl.program_id(0) == 0) & (pl.program_id(1) == 0)
+    return pl.program_id(0) == 0
 
 
 def window(ref, image, images):
@@ -188,7 +193,7 @@
 
 
 def kernel_first_layer(
-    images, x_ref, w_qkv, w_proj, w_fc1, w_fc2, vecs, qkv_bias, fc1_bias, bias,
+    images, place, rims, x_ref, w_qkv, w_proj, w_fc1, w_fc2, vecs, qkv_bias, fc1_bias, bias,
     stream_out, hidden_out, middle_out, out_out, probs_out, act_out, slope_out,
     sc_q, sc_k, sc_v, sc_out,
 ):
@@ -212,18 +217,24 @@
     stream = middle + mm(activated, w_fc2[...]) + vecs[5:6]
     stream_out[0, 0] = stream
     normed, _ = norm_parts(stream)
-    put_tokens(hidden_out, normed * vecs[6:7] + vecs[7:8])
+    block = put_tokens(hidden_out, normed * vecs[6:7] + vecs[7:8])
+    if rims is not None:
+        put_rims(block, rims, place, "first")
 
 
 def kernel_shifted_forward(
-    images, hidden_ref, w_qkv, qkv_bias, bias, masks, out_out, probs_out, sc_q, sc_k, sc_v, sc_out
+    images, place, rims, hidden_ref, *refs
 ):
+    halo, refs = (None, refs) if rims is None else (refs[:3], refs[3:])
+    w_qkv, qkv_bias, bias, masks, out_out, probs_out, held, sc_q, sc_k, sc_v, sc_out = refs
     count = POS * images
     zero_tails(first_of_grid(), count, sc_q, sc_k, sc_v)
-    hidden = tokens_of(hidden_ref).astype(BF)
+    hidden = ahead_window(hidden_ref, halo, held, place).astype(BF)
     split_projection(hidden, w_qkv[...], qkv_bias[...], (sc_q, sc_k, sc_v), count)
     attention_forward(images, (sc_q, sc_k, sc_v), bias[...], masks, probs_out, sc_out)
-    put_tokens(out_out, sc_out[:count, :])
+    block = put_tokens(out_out, sc_out[:count, :])
+    if rims is not None:
+        put_rims(block, rims, place, "last")
 
 
 def feed_forward_backward(out_low, inner, activated, slope, w_fc1, w_fc2):
@@ -232,20 +243,121 @@
     return expanded_low, inner_grad
 
 
-def start_sums(refs):
-    @pl.when(first_of_grid())
-    def _():
-        for ref in refs:
-            ref[...] = jnp.zeros_like(ref)
-
-
-def kernel_middle(
-    images, stream_ref, out_ref, cot_ref, w_proj, w_fc1, w_fc2, vecs, fc1_bias,
-    mixed_out, grad_out, low_out, g_proj, g_fc1, g_fc2, sums, fc1_sums,
-):
-    start_sums((g_proj, g_fc1, g_fc2, sums, fc1_sums))
+def put_rims(block, rims, place, edge):
+    rim_rows, rim_cols, corner = rims
+    row, col, rows, cols = place
+    start = 0 if edge == "first" else WIN - SHIFT
+    keep = slice(start, start + SHIFT)
+    row_rim = row == (0 if edge == "first" else rows - 1)
+    col_rim = col == (0 if edge == "first" else cols - 1)
+
+    @pl.when(row_rim)
+    def _():
+        rim_rows[:, pl.ds(col * WIN, WIN)] = block[keep]
+
+    @pl.when(col_rim)
+    def _():
+        rim_cols[pl.ds(row * WIN, WIN)] = block[:, keep]
+
+    @pl.when(row_rim & col_rim)
+    def _():
+        corner[...] = block[keep, keep]
+
+
+def ahead_window(field, rims, held, place):
+    row, col, rows, cols = place
+    top, left = row * WIN + SHIFT, col * WIN + SHIFT
+    if rims is None:
+        return tokens_of_block(field[pl.ds(top, WIN), pl.ds(left, WIN)])
+    rim_rows, rim_cols, corner = rims
+    own = WIN - SHIFT
+    low, far = row == rows - 1, col == cols - 1
+    held[:own, :own] = field[pl.ds(top, own), pl.ds(left, own)]
+
+    @pl.when(low)
+    def _():
+        held[own:, :own] = rim_rows[:, pl.ds(left, own)]
+
+    @pl.when(jnp.logical_not(low))
+    def _():
+        held[own:, :own] = field[pl.ds(top + own, SHIFT), pl.ds(left, own)]
+
+    @pl.when(far)
+    def _():
+        held[:own, own:] = rim_cols[pl.ds(top, own)]
+
+    @pl.when(jnp.logical_not(far))
+    def _():
+        held[:own, own:] = field[pl.ds(top, own), pl.ds(left + own, SHIFT)]
+
+    @pl.when(low & far)
+    def _():
+        held[own:, own:] = corner[...]
+
+    @pl.when(low & jnp.logical_not(far))
+    def _():
+        held[own:, own:] = rim_rows[:, pl.ds(left + own, SHIFT)]
+
+    @pl.when(jnp.logical_not(low) & far)
+    def _():
+        held[own:, own:] = rim_cols[pl.ds(top + own, SHIFT)]
+
+    return tokens_of_block(held[...])
+
+
+def behind_window(field, rims, held, place):
+    row, col, _, _ = place
+    top, left = row * WIN, col * WIN
+    if rims is None:
+        return tokens_of_block(field[pl.ds(top - SHIFT, WIN), pl.ds(left - SHIFT, WIN)])
+    rim_rows, rim_cols, corner = rims
+    own = WIN - SHIFT
+    high, near = row == 0, col == 0
+    held[SHIFT:, SHIFT:] = field[pl.ds(top, own), pl.ds(left, own)]
+
+    @pl.when(high)
+    def _():
+        held[:SHIFT, SHIFT:] = rim_rows[:, pl.ds(left, own)]
+
+    @pl.when(jnp.logical_not(high))
+    def _():
+        held[:SHIFT, SHIFT:] = field[pl.ds(top - SHIFT, SHIFT), pl.ds(left, own)]
+
+    @pl.when(near)
+    def _():
+        held[SHIFT:, :SHIFT] = rim_cols[pl.ds(top, own)]
+
+    @pl.when(jnp.logical_not(near))
+    def _():
+        held[SHIFT:, :SHIFT] = field[pl.ds(top, own), pl.ds(left - SHIFT, SHIFT)]
+
+    @pl.when(high & near)
+    def _():
+        held[:SHIFT, :SHIFT] = corner[...]
+
+    @pl.when(high & jnp.logical_not(near))
+    def _():
+        held[:SHIFT, :SHIFT] = rim_rows[:, pl.ds(left - SHIFT, SHIFT)]
+
+    @pl.when(jnp.logical_not(high) & near)
+    def _():
+        held[:SHIFT, :SHIFT] = rim_cols[pl.ds(top - SHIFT, SHIFT)]
+
+    @pl.when(jnp.logical_not(high) & jnp.logical_not(near))
+    def _():
+        held[:SHIFT, :SHIFT] = field[pl.ds(top - SHIFT, SHIFT), pl.ds(left - SHIFT, SHIFT)]
+
+    return tokens_of_block(held[...])
+
+
+def kernel_middle(images, place, rims, out_ref, *refs):
+    halo, refs = (None, refs) if rims is None else (refs[:3], refs[3:])
+    (
+        stream_ref, cot_ref, w_proj, w_fc1, w_fc2, vecs, fc1_bias,
+        mixed_out, grad_out, low_out, g_proj, g_fc1, g_fc2, sums, fc1_sums, held,
+    ) = refs
     stream = stream_ref[0, 0]
-    attended = tokens_of(out_ref).astype(BF)
+    attended = behind_window(out_ref, halo, held, place).astype(BF)
     middle = stream + (mm(attended, w_proj[...]) + vecs[4:5])
     normed, inverse = norm_parts(middle)
     inner = (normed * vecs[2:3] + vecs[3:4]).astype(BF)
@@ -265,7 +377,9 @@
     grad_out[0, 0] = updated
     branch_low = updated.astype(BF)
     g_proj[...] += mm_tn(attended, branch_low)
-    put_tokens(low_out, mm_nt(branch_low, w_proj[...]))
+    block = put_tokens(low_out, mm_nt(branch_low, w_proj[...]))
+    if rims is not None:
+        put_rims(block, rims, place, "first")
     sums[0] += fold_rows(gradient)
     sums[1] += fold_rows(inner_grad * normed)
     sums[2] += fold_rows(inner_grad)
@@ -279,32 +393,35 @@
     return jnp.concatenate(pieces, 1)
 
 
-def kernel_shifted_backward(
-    images, hidden_ref, out_ref, low_ref, probs_ref, w_qkv, qkv_bias,
-    hidden_grad_out, g_qkv, qv_sums, bias_acc,
-    sc_q, sc_k, sc_v, sc_out, sc_grad, sc_dq, sc_dk, sc_dv,
-):
+def kernel_shifted_backward(images, place, rims, hidden_ref, low_ref, *refs):
+    halo, low_halo, refs = (
+        (None, None, refs) if rims is None else (refs[:3], refs[3:6], refs[6:])
+    )
+    (
+        out_ref, probs_ref, w_qkv, qkv_bias, hidden_grad_out, g_qkv, qv_sums, bias_acc,
+        held, sc_q, sc_k, sc_v, sc_out, sc_grad, sc_dq, sc_dk, sc_dv,
+    ) = refs
     count = POS * images
-    start_sums((g_qkv, qv_sums, bias_acc))
     zero_tails(first_of_grid(), count, sc_q, sc_k, sc_v, sc_out, sc_grad)
-    hidden = tokens_of(hidden_ref).astype(BF)
+    hidden = ahead_window(hidden_ref, halo, held, place).astype(BF)
     split_projection(hidden, w_qkv[...], qkv_bias[...], (sc_q, sc_k, sc_v), count)
     sc_out[:count, :] = tokens_of(out_ref)
-    sc_grad[:count, :] = tokens_of(low_ref)
+    sc_grad[:count, :] = ahead_window(low_ref, low_halo, held, place)
     grads = (sc_dq, sc_dk, sc_dv)
     attention_backward(images, (sc_q, sc_k, sc_v), sc_grad, sc_out, probs_ref, grads, bias_acc)
     joined = joined_gradients(count, grads, qv_sums)
     g_qkv[...] += mm_tn(hidden, joined)
-    put_tokens(hidden_grad_out, mm_nt(joined, w_qkv[...]))
+    block = put_tokens(hidden_grad_out, mm_nt(joined, w_qkv[...]))
+    if rims is not None:
+        put_rims(block, rims, place, "last")
 
 
 def kernel_first_feed_backward(
-    images, hidden_grad_ref, stream_ref, grad_ref, middle_ref, act_ref, slope_ref, att_ref,
+    images, place, rims, hidden_grad_ref, rim_rows, rim_cols, corner, stream_ref, grad_ref, middle_ref, act_ref, slope_ref, att_ref,
     w_proj, w_fc1, w_fc2, vecs,
-    grad_out, low_out, g_proj, g_fc1, g_fc2, sums, fc1_sums,
+    grad_out, low_out, g_proj, g_fc1, g_fc2, sums, fc1_sums, held,
 ):
-    start_sums((g_proj, g_fc1, g_fc2, sums, fc1_sums))
-    upstream = tokens_of(hidden_grad_ref)
+    upstream = behind_window(hidden_grad_ref, (rim_rows, rim_cols, corner), held, place)
     normed, inverse = norm_parts(stream_ref[0, 0])
     gradient = grad_ref[0, 0] + norm_backward(upstream, normed, inverse, vecs[6:7])
     sums[4] += fold_rows(upstream * normed)
@@ -331,12 +448,11 @@
 
 
 def kernel_first_attention_backward(
-    images, x_ref, grad_ref, low_ref, att_ref, probs_ref, w_qkv, vecs, qkv_bias,
+    images, place, rims, x_ref, grad_ref, low_ref, att_ref, probs_ref, w_qkv, vecs, qkv_bias,
     tokens_grad_out, g_qkv, qv_sums, bias_acc, sums,
     sc_q, sc_k, sc_v, sc_out, sc_grad, sc_dq, sc_dk, sc_dv,
 ):
     count = POS * images
-    start_sums((g_qkv, qv_sums, bias_acc, sums))
     zero_tails(first_of_grid(), count, sc_q, sc_k, sc_v, sc_out, sc_grad)
     normed, inverse = norm_parts(tokens_of(x_ref))
     hidden = (normed * vecs[0:1] + vecs[1:2]).astype(BF)
@@ -368,35 +484,232 @@
     return lax.ppermute(array, ("seq", "wt"), pairs)
 
 
-def roll_ahead(field):
-    rim_rows = shift_by(field[:SHIFT], "seq", -1)
-    rim_cols = shift_by(field[:, :SHIFT], "wt", -1)
-    corner = shift_both(field[:SHIFT, :SHIFT], -1)
-    upper = jnp.concatenate([field[SHIFT:, SHIFT:], rim_cols[SHIFT:]], 1)
-    lower = jnp.concatenate([rim_rows[:, SHIFT:], corner], 1)
-    return jnp.concatenate([upper, lower], 0)
-
-
-def roll_behind(field):
-    rim_rows = shift_by(field[-SHIFT:], "seq", 1)
-    rim_cols = shift_by(field[:, -SHIFT:], "wt", 1)
-    corner = shift_both(field[-SHIFT:, -SHIFT:], 1)
-    upper = jnp.concatenate([corner, rim_rows[:, :-SHIFT]], 1)
-    lower = jnp.concatenate([rim_cols[:-SHIFT], field[:-SHIFT, :-SHIFT]], 1)
-    return jnp.concatenate([upper, lower], 0)
-
-
-def pack_second(w_fc2):
-    rows, depth = w_fc2.shape
-    blocks = w_fc2.reshape(4, rows // 4, depth)
-    return blocks.transpose(1, 0, 2).reshape(rows // 4, 4 * depth)
-
-
-def unpack_second(packed, parts):
-    rows, wide = packed.shape
-    depth = wide // 4
-    blocks = packed.reshape(parts, rows // parts, 4, depth)
-    return blocks.transpose(0, 2, 1, 3).reshape(rows * 4, depth)
+def send_rims(rims, by):
+    rim_rows, rim_cols, corner = rims
+    return (
+        shift_by(rim_rows, "seq", by),
+        shift_by(rim_cols, "wt", by),
+        shift_both(corner, by),
+    )
+
+
+def window_order(part, rows, cols):
+    if part == "all":
+        return rows * cols, lambda i: (i // cols, i % cols)
+    edge, rim = part
+    if rim:
+        base = 0 if edge == "first" else rows - 1
+        side = 0 if edge == "first" else cols - 1
+        skip = 1 if edge == "first" else 0
+        return rows + cols - 1, lambda i: (
+            jnp.where(i < cols, base, i - cols + skip),
+            jnp.where(i < cols, i, side),
+        )
+    skip = 1 if edge == "first" else 0
+    return (rows - 1) * (cols - 1), lambda i: (
+        i // (cols - 1) + skip,
+        i % (cols - 1) + skip,
+    )
+
+
+def axis_sizes():
+    return lax.axis_size("seq"), lax.axis_size("wt")
+
+
+def blocks_of(matrix):
+    return [matrix[:, i : i + 128] for i in range(0, matrix.shape[1], 128)]
+
+
+def pack_slices(w_qkv, w_proj, w_fc1, w_fc2):
+    return jnp.concatenate([*blocks_of(w_qkv), w_proj, *blocks_of(w_fc1), w_fc2], 0)
+
+
+def kernel_weights(parts, place_ref, *refs):
+    pieces, (qkv, proj, fc1, fc2), (s_qkv, s_proj, s_fc1, s_fc2) = (
+        refs[:parts], refs[parts : parts + 4], refs[parts + 4 :]
+    )
+    rows = s_qkv.shape[0] // parts
+    for k in range(parts):
+        owner = lax.rem(place_ref[0] + k, parts)
+        piece = pieces[k][...].astype(F32)
+        near = pl.ds(pl.multiple_of(owner * rows, rows), rows)
+        at = 0
+        for target in (s_qkv, s_proj, s_fc1):
+            for i in range(0, target.shape[1], 128):
+                target[near, i : i + 128] = piece[at : at + rows]
+                at += rows
+        far = s_fc2.shape[0] // parts
+        s_fc2[pl.ds(pl.multiple_of(owner * far, far), far), :] = piece[at : at + far]
+    for out, held in ((qkv, s_qkv), (proj, s_proj), (fc1, s_fc1), (fc2, s_fc2)):
+        out[...] = held[...].astype(BF)
+
+
+def whole_weights(place, packed, depth, wide):
+    parts = lax.axis_size("wt")
+    pieces = [packed] + [shift_by(packed, "wt", -k) for k in range(1, parts)]
+    shapes = [(depth, 3 * depth), (depth, depth), (depth, wide), (wide, depth)]
+
+    def body(*refs):
+        kernel_weights(parts, *refs)
+
+    full = pl.BlockSpec(memory_space=pltpu.VMEM)
+    return pl.pallas_call(
+        body,
+        in_specs=[pl.BlockSpec(memory_space=pltpu.SMEM)] + [full] * parts,
+        out_specs=[full] * 4,
+        out_shape=[jax.ShapeDtypeStruct(shape, BF) for shape in shapes],
+        scratch_shapes=[pltpu.VMEM(shape, F32) for shape in shapes],
+    )(place, *pieces)
+
+
+SMALL_ROWS = 8
+
+
+def split_high(field):
+    high = field.astype(BF)
+    return high, (field - high.astype(F32)).astype(BF)
+
+
+def small_rows(refs):
+    (sums00, sums0, sums1, qv0, qv1, fc1_0, fc1_1, table) = refs
+
+    def one(ref, k):
+        return jnp.sum(ref[k], 0, keepdims=True)
+
+    rows = [
+        one(sums00, 0), one(sums0, 1), one(sums0, 4), one(sums1, 1),
+        one(sums00, 1), one(sums0, 2), one(sums0, 5), one(sums1, 2),
+        one(qv0, 0), one(qv0, 1), one(qv1, 0), one(qv1, 1),
+        one(sums0, 3), one(sums0, 0), one(sums1, 3), one(sums1, 0),
+    ]
+    for ref in (fc1_0, fc1_1):
+        line = jnp.sum(ref[...], 0, keepdims=True)
+        rows += [line[:, i : i + 128] for i in range(0, line.shape[1], 128)]
+    return rows + [table[:, i : i + 128] for i in range(0, table.shape[1], 128)]
+
+
+def kernel_pack(seqs, parts, each, *refs):
+    grads, smalls, out, held, lines = refs[:8], refs[8:16], refs[16], refs[17], refs[18]
+    depth = grads[0].shape[0]
+    rows = depth // parts
+    lines[...] = jnp.zeros_like(lines)
+    at = 0
+    for row in small_rows(smalls):
+        lines[at : at + row.shape[0], :] = row
+        at += row.shape[0]
+    per = -(-at // seqs)
+    turned = [grads[3][...].T, grads[7][...].T]
+    for w in range(parts):
+        near = slice(w * rows, (w + 1) * rows)
+        at = 0
+        for layer in range(2):
+            for grad in grads[4 * layer : 4 * layer + 3]:
+                for i in range(0, grad.shape[1], 128):
+                    held[at : at + rows, :] = grad[near, i : i + 128]
+                    at += rows
+            far = turned[layer].shape[0] // parts
+            held[at : at + far, :] = turned[layer][w * far : (w + 1) * far]
+            at += far
+        for s in range(seqs):
+            mine = held[s * each : s * each + out.shape[1] - 2 * SMALL_ROWS, :]
+            high, low = split_high(lines[s * per : s * per + SMALL_ROWS, :])
+            out[s * parts + w] = jnp.concatenate(
+                [mine, high.astype(F32), low.astype(F32)], 0
+            ).astype(BF)
+
+
+def kernel_reduce(packet_ref, out_ref):
+    total = packet_ref[0].astype(F32)
+    for i in range(1, packet_ref.shape[0]):
+        total = total + packet_ref[i].astype(F32)
+    rows = total.shape[0] - 2 * SMALL_ROWS
+    high, low = split_high(total[rows : rows + SMALL_ROWS] + total[rows + SMALL_ROWS :])
+    out_ref[...] = jnp.concatenate(
+        [total[:rows], high.astype(F32), low.astype(F32)], 0
+    ).astype(BF)
+
+
+def kernel_unpack(each, per, packets, *refs):
+    (gains, shifts, qkv, qv, table, proj, outs, fc1, fc1_bias, fc2, held, lines) = refs
+    seqs, size, _ = packets.shape
+    for s in range(seqs):
+        packet = packets[s].astype(F32)
+        start = size - 2 * SMALL_ROWS
+        held[s * each : (s + 1) * each, :] = packet[:each]
+        both = packet[start : start + SMALL_ROWS] + packet[start + SMALL_ROWS :]
+        lines[s * per : (s + 1) * per, :] = both[:per]
+    at = 0
+    for layer in range(2):
+        for target in (qkv, proj, fc1):
+            rows = target.shape[1]
+            for i in range(0, target.shape[2], 128):
+                target[layer, :, i : i + 128] = held[at : at + rows, :]
+                at += rows
+        far = fc2.shape[1]
+        fc2[layer] = held[at : at + far, :]
+        at += far
+    at = 0
+    for target in (gains, shifts, qv, outs):
+        for layer in range(2):
+            target[layer] = lines[at : at + 2, :]
+            at += 2
+    for layer in range(2):
+        for i in range(0, fc1_bias.shape[1], 128):
+            fc1_bias[layer : layer + 1, i : i + 128] = lines[at : at + 1, :]
+            at += 1
+    for i in range(0, table.shape[1], 128):
+        table[:, i : i + 128] = lines[at : at + table.shape[0], :]
+        at += table.shape[0]
+
+
+def whole_kernel(body, inputs, outputs, scratch=()):
+    full = pl.BlockSpec(memory_space=pltpu.VMEM)
+    return pl.pallas_call(
+        body,
+        in_specs=[full] * len(inputs),
+        out_specs=[full] * len(outputs),
+        out_shape=[jax.ShapeDtypeStruct(*out) for out in outputs],
+        scratch_shapes=[pltpu.VMEM(shape, F32) for shape in scratch],
+        compiler_params=pltpu.CompilerParams(vmem_limit_bytes=VMEM_LIMIT),
+    )(*inputs)
+
+
+def sum_everywhere(grads, smalls, depth, wide):
+    seqs, parts = axis_sizes()
+    rows = depth // parts
+    held = 2 * (4 * depth + 2 * wide) // parts
+    each = held // seqs
+    size = -(-each // 16) * 16 + 2 * SMALL_ROWS
+    count = 16 + 2 * (wide // 128) + 2 * HEADS * (smalls[-1].shape[1] // 128)
+    per = -(-count // seqs)
+    tail = (seqs * per + SMALL_ROWS, 128)
+
+    def pack(*refs):
+        kernel_pack(seqs, parts, each, *refs)
+
+    def unpack(*refs):
+        kernel_unpack(each, per, *refs)
+
+    (packets,) = whole_kernel(
+        pack,
+        [*grads, *smalls],
+        [((seqs * parts, size, 128), BF)],
+        [(held + 16, 128), tail],
+    )
+    packets = lax.all_to_all(packets, ("seq", "wt"), 0, 0, tiled=True)
+    (mine,) = whole_kernel(kernel_reduce, [packets], [((size, 128), BF)])
+    mine = lax.all_gather(mine, "seq", axis=0)
+    return whole_kernel(
+        unpack,
+        [mine],
+        [
+            ((2, 2, depth), F32), ((2, 2, depth), F32), ((2, rows, 3 * depth), F32),
+            ((2, 2, depth), F32), (smalls[-1].shape, F32), ((2, rows, depth), F32),
+            ((2, 2, depth), F32), ((2, rows, wide), F32), ((2, wide), F32),
+            ((2, wide // parts, depth), F32),
+        ],
+        [(held, 128), tail],
+    )
 
 
 def per_device(
@@ -405,21 +718,13 @@
 ):
     images, height, width, depth = tokens.shape
     wide = w_fc1.shape[-1]
-    parts = lax.axis_size("wt")
     rows, cols = height // WIN, width // WIN
     count = POS * images
     table_size = pos_table.shape[1]
 
-    weights = []
-    for layer in range(2):
-        packed = jnp.concatenate(
-            [w_qkv[layer], w_proj[layer], w_fc1[layer], pack_second(w_fc2[layer])], 1
-        )
-        whole = lax.all_gather(packed, "wt", axis=0, tiled=True)
-        cuts = [3 * depth, 4 * depth, 4 * depth + wide]
-        qkv, proj, fc1, fc2 = jnp.split(whole, cuts, 1)
-        weights.append((qkv, proj, fc1, unpack_second(fc2, parts)))
-
+    place = lax.axis_index("wt").astype(jnp.int32)[None]
+    slices = [pack_slices(w_qkv[l], w_proj[l], w_fc1[l], w_fc2[l]) for l in range(2)]
+    first_weights = whole_weights(place, slices[0], depth, wide)
     x = tokens.transpose(1, 2, 0, 3)
     cot = cotangent.transpose(1, 2, 0, 3)
     selector = (
@@ -442,6 +747,9 @@
     apart = jnp.pad(apart, [(0, 0)] * 3 + [(0, SLOT - POS)] * 2)
     masks = jnp.concatenate([apart, apart], -1)
 
+    first_weights, later, masks = lax.optimization_barrier((first_weights, slices[1], masks))
+    weights = [first_weights, whole_weights(place, later, depth, wide)]
+
     zeros = jnp.zeros((depth,), F32)
     qkv_biases = [
         jnp.concatenate([qv_bias[l, 0], zeros, qv_bias[l, 1]])[None] for l in range(2)
@@ -458,48 +766,108 @@
 
     vecs = [vectors(0), vectors(1)]
 
-    field = pl.BlockSpec((WIN, WIN, images, depth), lambda r, c: (r, c, 0, 0))
-    probs_spec = pl.BlockSpec((1, 1, images, SLOT, HEADS * SLOT), lambda r, c: (r, c, 0, 0, 0))
-    mask_spec = pl.BlockSpec((1, 1, images, SLOT, 2 * SLOT), lambda r, c: (r, c, 0, 0, 0))
+    field_shape = (height, width, images, depth)
+    field = ((WIN, WIN, images, depth), lambda r, c: (r, c, 0, 0))
+    probs_spec = ((1, 1, images, SLOT, HEADS * SLOT), lambda r, c: (r, c, 0, 0, 0))
+    mask_spec = ((1, 1, images, SLOT, 2 * SLOT), lambda r, c: (r, c, 0, 0, 0))
 
     def flat(columns):
-        return pl.BlockSpec((1, 1, count, columns), lambda r, c: (r, c, 0, 0))
-
-    def whole_of(shape):
-        return pl.BlockSpec(tuple(shape), lambda r, c: (0,) * len(shape))
-
-    field_shape = (height, width, images, depth)
+        return (1, 1, count, columns), lambda r, c: (r, c, 0, 0)
 
     def flat_type(columns, dtype):
         return jax.ShapeDtypeStruct((rows, cols, count, columns), dtype)
 
     probs_type = jax.ShapeDtypeStruct((rows, cols, images, SLOT, HEADS * SLOT), BF)
-
-    def run(kernel, inputs, outputs, slots):
+    rim_types = [
+        jax.ShapeDtypeStruct((SHIFT, width, images, depth), BF),
+        jax.ShapeDtypeStruct((height, SHIFT, images, depth), BF),
+        jax.ShapeDtypeStruct((SHIFT, SHIFT, images, depth), BF),
+    ]
+
+    def run(kernel, part, inputs, outputs, slots, earlier=None, held=False):
+        steps, order = window_order(part, rows, cols)
+
+        def spec_of(spec, shape):
+            if spec is None:
+                return pl.BlockSpec(tuple(shape), lambda i: (0,) * len(shape))
+            block, index = spec
+            return pl.BlockSpec(block, lambda i: index(*order(i)))
+
+        with_rims = part != "all" and part[1]
+        n_in, n_out = len(inputs), len(outputs)
+        ins = [a for a, _ in inputs]
+        in_specs = [spec_of(spec, a.shape) for a, spec in inputs]
+        aliases = {}
+        if earlier is not None:
+            for n, (array, (_, spec)) in enumerate(zip(earlier, outputs)):
+                if spec is not None:
+                    aliases[len(ins)] = n
+                ins.append(array)
+                in_specs.append(
+                    spec_of(None, array.shape)
+                    if spec is None
+                    else pl.BlockSpec(memory_space=pl.ANY)
+                )
+        n_all = len(ins)
+        types = [t for t, _ in outputs] + (rim_types if with_rims else [])
+        out_specs = [spec_of(spec, t.shape) for t, spec in outputs]
+        out_specs += [spec_of(None, t.shape) for t in rim_types] if with_rims else []
+
         def body(*refs):
-            kernel(images, *refs)
-
-        return pl.pallas_call(
+            place = (*order(pl.program_id(0)), rows, cols)
+            outs = refs[n_all : n_all + n_out]
+            rims = refs[n_all + n_out : n_all + n_out + 3] if with_rims else None
+            rest = refs[n_all + len(types) :]
+
+            @pl.when(first_of_grid())
+            def _():
+                for n, (_, spec) in enumerate(outputs):
+                    if spec is None:
+                        if earlier is None:
+                            outs[n][...] = jnp.zeros_like(outs[n])
+                        else:
+                            outs[n][...] = refs[n_in + n][...]
+
+            kernel(images, place, rims, *refs[:n_in], *outs, *rest)
+
+        scratch = [pltpu.VMEM((WIN, WIN, images, depth), BF)] if held else []
+        scratch += [pltpu.VMEM((SLOT * images, depth), F32)] * slots
+        results = pl.pallas_call(
             body,
-            grid=(rows, cols),
-            in_specs=[spec if spec is not None else whole_of(a.shape) for a, spec in inputs],
-            out_specs=[spec if spec is not None else whole_of(t.shape) for t, spec in outputs],
-            out_shape=[t for t, _ in outputs],
-            scratch_shapes=[pltpu.VMEM((SLOT * images, depth), F32)] * slots,
+            grid=(steps,),
+            in_specs=in_specs,
+            out_specs=out_specs,
+            out_shape=types,
+            scratch_shapes=scratch,
+            input_output_aliases=aliases,
             compiler_params=pltpu.CompilerParams(vmem_limit_bytes=VMEM_LIMIT),
-        )(*[a for a, _ in inputs])
+            cost_estimate=pl.CostEstimate(
+                flops=steps * 10**9, bytes_accessed=10**7, transcendentals=0
+            ),
+        )(*ins)
+        return results[:n_out], results[n_out:]
+
+    def run_both(kernel, edge, inputs, halos, outputs, slots, by, held=False):
+        lead = len(halos)
+        rim_inputs = [(a, None) for halo in halos for a in halo]
+        inputs_a = inputs[:lead] + rim_inputs + inputs[lead:]
+        first, rims = run(kernel, (edge, True), inputs_a, outputs, slots, held=held)
+        rims = send_rims(rims, by)
+        return run(kernel, (edge, False), inputs, outputs, slots, first, held=held)[0], rims
 
     def total(*shape):
         return (jax.ShapeDtypeStruct(shape, F32), None)
 
     qkv0, proj0, fc10, fc20 = weights[0]
     qkv1, proj1, fc11, fc21 = weights[1]
-    stream1, hidden1, middle0, att0, probs0, act0, slope0 = run(
+    (stream1, hidden1, middle0, att0, probs0, act0, slope0), halo = run_both(
         kernel_first_layer,
+        "first",
         [
             (x, field), (qkv0, None), (proj0, None), (fc10, None), (fc20, None), (vecs[0], None),
             (qkv_biases[0], None), (fc1_bias[0:1], None), (biases[0], None),
         ],
+        [],
         [
             (flat_type(depth, F32), flat(depth)),
             (jax.ShapeDtypeStruct(field_shape, BF), field),
@@ -510,23 +878,29 @@
             (flat_type(wide, BF), flat(wide)),
         ],
         4,
-    )
-    hidden1 = roll_ahead(hidden1)
-    att1, probs1 = run(
+        -1,
+    )
+    (att1, probs1), out_halo = run_both(
         kernel_shifted_forward,
-        [
-            (hidden1, field), (qkv1, None), (qkv_biases[1], None), (biases[1], None),
+        "last",
+        [
+            (hidden1, None), (qkv1, None), (qkv_biases[1], None), (biases[1], None),
             (masks, mask_spec),
         ],
+        [halo],
         [(jax.ShapeDtypeStruct(field_shape, BF), field), (probs_type, probs_spec)],
         4,
-    )
-    mixed, grad1, low1, g_proj1, g_fc11, g_fc21, sums1, fc1_sums1 = run(
+        1,
+        held=True,
+    )
+    (mixed, grad1, low1, g_proj1, g_fc11, g_fc21, sums1, fc1_sums1), low_halo = run_both(
         kernel_middle,
-        [
-            (stream1, flat(depth)), (roll_behind(att1), field), (cot, field), (proj1, None),
+        "first",
+        [
+            (att1, None), (stream1, flat(depth)), (cot, field), (proj1, None),
             (fc11, None), (fc21, None), (vecs[1], None), (fc1_bias[1:2], None),
         ],
+        [out_halo],
         [
             (jax.ShapeDtypeStruct(field_shape, BF), field),
             (flat_type(depth, F32), flat(depth)),
@@ -535,23 +909,31 @@
             total(8, wide),
         ],
         0,
-    )
-    hidden_grad1, g_qkv1, qv_sums1, bias_sums1 = run(
+        -1,
+        held=True,
+    )
+    (hidden_grad1, g_qkv1, qv_sums1, bias_sums1), grad_halo = run_both(
         kernel_shifted_backward,
-        [
-            (hidden1, field), (att1, field), (roll_ahead(low1), field), (probs1, probs_spec),
+        "last",
+        [
+            (hidden1, None), (low1, None), (att1, field), (probs1, probs_spec),
             (qkv1, None), (qkv_biases[1], None),
         ],
+        [halo, low_halo],
         [
             (jax.ShapeDtypeStruct(field_shape, BF), field),
             total(depth, 3 * depth), total(2, 8, depth), total(SLOT, HEADS * SLOT),
         ],
         8,
-    )
-    grad0, low0, g_proj0, g_fc10, g_fc20, sums0, fc1_sums0 = run(
+        1,
+        held=True,
+    )
+    (grad0, low0, g_proj0, g_fc10, g_fc20, sums0, fc1_sums0), _ = run(
         kernel_first_feed_backward,
-        [
-            (roll_behind(hidden_grad1), field), (stream1, flat(depth)), (grad1, flat(depth)),
+        "all",
+        [
+            (hidden_grad1, None), *[(a, None) for a in grad_halo],
+            (stream1, flat(depth)), (grad1, flat(depth)),
             (middle0, flat(depth)), (act0, flat(wide)), (slope0, flat(wide)), (att0, flat(depth)),
             (proj0, None), (fc10, None), (fc20, None), (vecs[0], None),
         ],
@@ -561,9 +943,11 @@
             total(8, wide),
         ],
         0,
-    )
-    tokens_grad, g_qkv0, qv_sums0, bias_sums0, sums00 = run(
+        held=True,
+    )
+    (tokens_grad, g_qkv0, qv_sums0, bias_sums0, sums00), _ = run(
         kernel_first_attention_backward,
+        "all",
         [
             (x, field), (grad0, flat(depth)), (low0, flat(depth)), (att0, flat(depth)),
             (probs0, probs_spec), (qkv0, None), (vecs[0], None), (qkv_biases[0], None),
@@ -576,54 +960,20 @@
         8,
     )
 
-    owned = []
-    for g_qkv, g_proj, g_fc1, g_fc2 in (
-        (g_qkv0, g_proj0, g_fc10, g_fc20), (g_qkv1, g_proj1, g_fc11, g_fc21)
-    ):
-        packed = jnp.concatenate(
-            [g_qkv, g_proj, g_fc1, g_fc2.reshape(depth, parts, -1).transpose(1, 2, 0).reshape(parts, wide // parts, depth).reshape(parts, 4, -1, depth).transpose(0, 2, 1, 3).reshape(depth, wide)], 1
-        ).astype(BF)
-        mine = lax.psum_scatter(packed, "wt", scatter_dimension=0, tiled=True)
-        mine = lax.psum(mine, "seq").astype(F32)
-        a, b, c, d = jnp.split(mine, [3 * depth, 4 * depth, 4 * depth + wide], 1)
-        owned.append((a, b, c, unpack_second(d, 1)))
-
-    def one(sums):
-        return jnp.sum(sums, -2)
-
-    sums0, sums1, sums00 = one(sums0), one(sums1), one(sums00)
     bias_sums = jnp.stack([bias_sums0, bias_sums1]).reshape(2, SLOT, HEADS, SLOT)
-    bias_sums = bias_sums[:, :POS, :, :POS].transpose(1, 3, 0, 2).reshape(POS * POS, 2 * HEADS)
-    table_grads = jnp.dot(selector.T, bias_sums, precision=lax.Precision.HIGHEST)
-    table_grads = table_grads.reshape(table_size, 2, HEADS).transpose(1, 0, 2)
-    small = lax.psum(
-        (
-            jnp.stack([jnp.stack([sums00[0], sums0[1]]), jnp.stack([sums0[4], sums1[1]])]),
-            jnp.stack([jnp.stack([sums00[1], sums0[2]]), jnp.stack([sums0[5], sums1[2]])]),
-            jnp.stack([one(qv_sums0), one(qv_sums1)]),
-            table_grads,
-            jnp.stack([jnp.stack([sums0[3], sums0[0]]), jnp.stack([sums1[3], sums1[0]])]),
-            jnp.stack([one(fc1_sums0), one(fc1_sums1)]),
-        ),
-        ("seq", "wt"),
-    )
-
-    def both(index):
-        return jnp.stack([owned[0][index], owned[1][index]])
-
+    bias_sums = bias_sums[:, :POS, :, :POS].transpose(0, 2, 1, 3).reshape(2 * HEADS, POS * POS)
+    table = jnp.dot(bias_sums, selector, precision=lax.Precision.HIGHEST)
+    table = jnp.pad(table, ((0, 0), (0, -table_size % 128)))
+    gains, shifts, d_qkv, d_qv, d_table, d_proj, d_out, d_fc1, d_fc1_bias, d_fc2 = sum_everywhere(
+        [g_qkv0, g_proj0, g_fc10, g_fc20, g_qkv1, g_proj1, g_fc11, g_fc21],
+        [sums00, sums0, sums1, qv_sums0, qv_sums1, fc1_sums0, fc1_sums1, table],
+        depth,
+        wide,
+    )
+    d_table = d_table[:, :table_size].reshape(2, HEADS, table_size).transpose(0, 2, 1)
     return (
-        mixed.transpose(2, 0, 1, 3),
-        tokens_grad.transpose(2, 0, 1, 3),
-        small[0],
-        small[1],
-        both(0),
-        small[2],
-        small[3],
-        both(1),
-        small[4],
-        both(2),
-        small[5],
-        both(3),
+        mixed.transpose(2, 0, 1, 3), tokens_grad.transpose(2, 0, 1, 3), gains, shifts, d_qkv,
+        d_qv, d_table, d_proj, d_out, d_fc1, d_fc1_bias, d_fc2,
     )
 
 

time: 362 us -> 286 us (0.79)
  waiting for transfers between devices: 42.4 us -> 0.05 us
  blocking collectives: 70.4 us -> 39.2 us
  Pallas kernels: 167 us -> 193 us
  local copies, waits for them, and re-layouts: 33.6 us -> 18.8 us
  starting transfers between devices: 11.3 us -> 25.9 us
  other arithmetic: 18.2 us -> 3.95 us
  between operations: 14.7 us -> 1.21 us
    psum x1 -> x0, blocking collectives: 39 us -> none  [per_device(): lax.psum((jnp.stack([jnp.stack([sums00[0], sums0[1]]), jnp.stack([sums0[4...]
    all_to_all x0 -> x1, blocking collectives: none -> 28.1 us  [sum_everywhere(): packets = lax.all_to_all(packets, ('seq', 'wt'), 0, 0, tiled=True)]
    pallas_call x6 -> x15, Pallas kernels: 167 us -> 193 us  [the longest x10 183 us: run(): pl.pallas_call(body, grid=(steps,), in_specs=in_specs, out_specs=out_spec...]
    all_gather x2 -> x1, blocking collectives: 31.3 us -> 11.1 us  [sum_everywhere(): mine = lax.all_gather(mine, 'seq', axis=0)]
    ppermute x8 -> x14, starting transfers between devices: 5.73 us -> 23.9 us  [shift_by(): lax.ppermute(array, axis, [(i, (i + by) % count) for i in range(count)])]
    reduce_scatter x2 -> x0, waiting for transfers between devices: 17.1 us -> none  [per_device(): mine = lax.psum_scatter(packed, 'wt', scatter_dimension=0, tiled=True)]
    slice x28 -> x0, local copies, waits for them, and re-layouts: 16.3 us -> none  [the longest x2 2.1 us: roll_behind(): rim_rows = shift_by(field[-SHIFT:], 'seq', 1)]
    psum x1 -> x0, waiting for transfers between devices: 15.8 us -> none  [per_device(): mine = lax.psum(mine, 'seq').astype(F32)]
  transfers between devices with their start and end apart: 15 -> 18, of which waited for: 9 -> 0; matrix products, arithmetic and copies ran while one was open for 7% -> 5% of each run, Pallas kernels for 15% -> 32%
where the time goes in v2:
time: 286 us; the launch traced here: 285 us
  Pallas kernels  193 us (67%)
  blocking collectives  39.2 us (14%)
  starting transfers between devices  25.9 us (9%)
  local copies, waits for them, and re-layouts  18.8 us (7%)
  other arithmetic  3.95 us (1%)
    pallas_call x10, Pallas kernels, run(): pl.pallas_call(body, grid=(steps,), in_specs=in_specs, out_specs=out_spec...  183 us
    all_to_all x1, blocking collectives, sum_everywhere(): packets = lax.all_to_all(packets, ('seq', 'wt'), 0, 0, tiled=True)  28.1 us
    ppermute x14, starting transfers between devices, shift_by(): lax.ppermute(array, axis, [(i, (i + by) % count) for i in range(count)])  23.9 us
    all_gather x1, blocking collectives, sum_everywhere(): mine = lax.all_gather(mine, 'seq', axis=0)  11.1 us
    pallas_call x3, Pallas kernels, whole_kernel(): pl.pallas_call(body, in_specs=[full] * len(inputs), out_specs=[full] * le...  6.17 us
  transfers between devices with their start and end apart: 18, of which 0 were waited for; matrix products, arithmetic and copies ran while one was open for 5% of the time, Pallas kernels for 32%

profile of v2, /device:TPU:0, one launch (start us, length us, event | category | flops | bytes accessed | tf_op | source)
XLA Modules:
  0.0 284.9 jit_solution(8191153091899379344)
XLA Ops:
  0.7 0.8 slice_bitcast_fusion.2
  1.5 0.8 slice_bitcast_fusion
  2.3 0.7 constant_dynamic-update-slice_fusion.14
  3.1 0.8 constant_dynamic-update-slice_fusion.9
  3.9 5.1 %collective-permute-start = (bf16[384,128]{1,0:T(8,128)(2,1)S(1)}, bf16[384,128]{1,0:T(8,128)(2,1)S(1)}, u32[]{:S(2)}, u32[]{:S(2)}) collective-permute-start(bf16[384,128]{1,0:T(8,128)(2,1)S(1)} %get-tuple-element.195.refs_1_), channel_id=1, source_target_pairs={{0,3},{1,0},{2,1},{3,2},{4,7},{5,4},{6,5},{7,6},{8,11},{9,8},{10,9... | collective-permute-start | bytes 294920 | tf_op jit(solution)/shard_map/ppermute | solution.py:474
  9.0 1.0 collective-permute-start.2
  10.1 1.1 reshape.72
  11.2 0.3 copy.40
  11.5 0.2 ne.15
  11.7 1.3 broadcast_compare_fusion
  13.0 0.6 broadcast_in_dim.15.refs_6_.refs_7_
  13.6 0.1 eq.41
  13.8 2.0 fusion.6
  15.9 0.8 squeeze.52.refs_8_
  16.6 0.6 fusion.13
  17.2 0.6 broadcast_in_dim.16.refs_5_.refs_2_.refs_11_
  17.8 0.8 squeeze.55.refs_6_.refs_3_
  18.5 0.6 pad.17
  19.2 0.6 stack.16.refs_9_.refs_6_
  19.8 0.6 stack.15.refs_5_.refs_13_.refs_6_
  20.4 2.6 add_convert_fusion.refs_7_.refs_4_
  23.0 0.6 copy-done.2
  23.7 1.8 shard_map.229
  25.5 2.8 collective-permute-start.3
  28.3 1.1 collective-permute-start.4
  29.5 19.2 %shard_map.230 = (f32[4,4,392,128]{3,2,1,0:T(8,128)}, bf16[28,28,8,128]{3,2,1,0:T(8,128)(2,1)}, f32[4,4,392,128]{3,2,1,0:T(8,128)}, bf16[4,4,392,128]{3,2,1,0:T(...) custom-call(bf16[28,28,8,128]{3,2,1,0:T(8,128)(2,1)} %bitcast.89, ...), custom_call_target="tpu_custom_call" | custom-call | flops 7000000000 | bytes 10000000 | tf_op jit(solution)/shard_map/pallas_call | solution.py:835
  48.7 0.5 collective-permute-start.6
  49.2 3.5 %collective-permute-start.7 = (bf16[28,3,8,128]{3,2,1,0:T(8,128)(2,1)}, bf16[28,3,8,128]{3,2,1,0:T(8,128)(2,1)S(1)}, u32[]{:S(2)}, u32[]{:S(2)}) collective-permute-start(bf16[28,3,8,128]{3,2,1,0:T(8,128)(2,1)} %get-tuple-element.122), channel_id=1, source_target_pairs={{0,3},{1,0},{2,1},{3,2},{4,7},{5,4},{6,5},{7,6},{8,11},{9,8},{10,9... | collective-permute-start | bytes 516104 | tf_op jit(solution)/shard_map/ppermute | solution.py:474
  52.8 1.9 collective-permute-start.8
  54.6 23.7 %shard_map.231 = (f32[4,4,392,128]{3,2,1,0:T(8,128)}, bf16[28,28,8,128]{3,2,1,0:T(8,128)(2,1)}, f32[4,4,392,128]{3,2,1,0:T(8,128)}, bf16[4,4,392,128]{3,2,1,0:T(...) custom-call(bf16[28,28,8,128]{3,2,1,0:T(8,128)(2,1)} %bitcast.90, ...), custom_call_target="tpu_custom_call", output_to_operand_aliasing={{0}: (9, {}), {1}: (10, {}), {2}: (11, {}), {3}: (12, {}), ... | custom-call | flops 8999999488 | bytes 10000000 | tf_op jit(solution)/shard_map/pallas_call | solution.py:835
  78.3 0.6 copy-done.6
  79.0 0.6 copy-done.7
  79.6 1.9 shard_map.232
  81.5 0.6 copy-done.23
  82.2 10.6 %shard_map.233 = (bf16[28,28,8,128]{3,2,1,0:T(8,128)(2,1)}, bf16[4,4,8,64,256]{4,3,2,1,0:T(8,128)(2,1)}, bf16[3,28,8,128]{3,2,1,0:T(8,128)(2,1)}, bf16[28,3,8,128]{3,2,1,0:T(8,128)(2,1)}, bf16[3,3,8,128]{3,2,1,0:T(8,128)(2,1)}) custom-call(bf16[28,28,8,128]{3,2,1,0:T(8,128)(2,1)} %get-tuple-element.117.refs_0_, bf16[3,28,8,128]{3,2,1,0:T(8,128)(2,1)} %copy-done.15, ...), custom_call_target="tpu_custom_call" | custom-call | flops 7000000000 | bytes 10000000 | tf_op jit(solution)/shard_map/pallas_call | solution.py:835
  92.9 1.7 collective-permute-start.10
  94.6 12.4 %shard_map.234 = (bf16[28,28,8,128]{3,2,1,0:T(8,128)(2,1)}, bf16[4,4,8,64,256]{4,3,2,1,0:T(8,128)(2,1)}) custom-call(bf16[28,28,8,128]{3,2,1,0:T(8,128)(2,1)} %get-tuple-element.117.refs_0_, bf16[128,384]{1,0:T(8,128)(2,1)} %get-tuple-element.119.refs_4_.refs_1_.refs_10_, ...), custom_call_target="tpu_custom_call", output_to_operand_aliasing={{0}: (5, {}), {1}: (6, {})} | custom-call | flops 8999999488 | bytes 10000000 | tf_op jit(solution)/shard_map/pallas_call | solution.py:835
  107.1 0.6 copy-done.26
  107.8 14.7 %shard_map.235 = (bf16[28,28,8,128]{3,2,1,0:T(8,128)(2,1)}, f32[4,4,392,128]{3,2,1,0:T(8,128)}, bf16[28,28,8,128]{3,2,1,0:T(8,128)(2,1)}, f32[128,128]{1,0:T(8,1...) custom-call(bf16[28,28,8,128]{3,2,1,0:T(8,128)(2,1)} %get-tuple-elem, ...), custom_call_target="tpu_custom_call" | custom-call | flops 7000000000 | bytes 10000000 | tf_op jit(solution)/shard_map/pallas_call | solution.py:835
  122.5 2.7 collective-permute-start.12
  125.2 3.2 %collective-permute-start.13 = (bf16[28,3,8,128]{3,2,1,0:T(8,128)(2,1)}, bf16[28,3,8,128]{3,2,1,0:T(8,128)(2,1)S(1)}, u32[]{:S(2)}, u32[]{:S(2)}) collective-permute-start(bf16[28,3,8,128]{3,2,1,0:T(8,128)(2,1)} %get-tuple-element.146), channel_id=1, source_target_pairs={{0,3},{1,0},{2,1},{3,2},{4,7},{5,4},{6,5},{7,6},{8,11},{9,8},{10,9... | collective-permute-start | bytes 516104 | tf_op jit(solution)/shard_map/ppermute | solution.py:474
  128.5 0.1 collective-permute-start.14
  128.6 17.1 %shard_map.236 = (bf16[28,28,8,128]{3,2,1,0:T(8,128)(2,1)}, f32[4,4,392,128]{3,2,1,0:T(8,128)}, bf16[28,28,8,128]{3,2,1,0:T(8,128)(2,1)}, f32[128,128]{1,0:T(8,1...) custom-call(bf16[28,28,8,128]{3,2,1,0:T(8,128)(2,1)} %get-tuple-elem, ...), custom_call_target="tpu_custom_call", output_to_operand_aliasing={{0}: (8, {}), {1}: (9, {}), {2}: (10, {})} | custom-call | flops 8999999488 | bytes 10000000 | tf_op jit(solution)/shard_map/pallas_call | solution.py:835
  145.7 0.5 copy-done.25
  146.3 0.1 copy-done.18
  146.4 14.2 %shard_map.237 = (bf16[28,28,8,128]{3,2,1,0:T(8,128)(2,1)}, f32[128,384]{1,0:T(8,128)}, f32[2,8,128]{2,1,0:T(8,128)}, f32[64,256]{1,0:T(8,128)}, bf16[3,28,8,128...) custom-call(bf16[28,28,8,128]{3,2,1,0:T(8,128)(2,1)} %get-tuple-element.117.refs_0_, ...), custom_call_target="tpu_custom_call" | custom-call | flops 7000000000 | bytes 10000000 | tf_op jit(solution)/shard_map/pallas_call | solution.py:835
  160.7 0.3 collective-permute-start.15
  161.0 1.7 collective-permute-start.16
  162.7 16.6 %shard_map.238 = (bf16[28,28,8,128]{3,2,1,0:T(8,128)(2,1)}, f32[128,384]{1,0:T(8,128)}, f32[2,8,128]{2,1,0:T(8,128)}, f32[64,256]{1,0:T(8,128)}) custom-call(bf16[28,28,8,128]{3,2,1,0:T(8,128)(2,1)} %get-tuple-element.117.refs_0_, bf16[28,28,8,128]{3,2,1,0:T(8,128)(2,1)} %get-tuple-element.143.refs_1_, ...), custom_call_target="tpu_custom_call", output_to_operand_aliasing={{0}: (6, {})} | custom-call | flops 8999999488 | bytes 10000000 | tf_op jit(solution)/shard_map/pallas_call | solution.py:835
  179.3 0.9 stack.18
  180.3 0.5 copy-done.24
  180.9 0.1 copy-done.17
  181.0 22.7 %shard_map.239 = (f32[4,4,392,128]{3,2,1,0:T(8,128)}, bf16[4,4,392,128]{3,2,1,0:T(8,128)(2,1)}, f32[128,128]{1,0:T(8,128)}, f32[128,512]{1,0:T(8,128)}, f32[128,...) custom-call(bf16[28,28,8,128]{3,2,1,0:T(8,128)(2,1)} %get-tuple-element.152.refs_0_, ...), custom_call_target="tpu_custom_call" | custom-call | flops 16000000000 | bytes 10000000 | tf_op jit(solution)/shard_map/pallas_call | solution.py:835
  203.8 31.9 %shard_map.240 = (f32[28,28,8,128]{3,2,1,0:T(8,128)}, f32[128,384]{1,0:T(8,128)}, f32[2,8,128]{2,1,0:T(8,128)}, f32[64,256]{1,0:T(8,128)}, f32[2,8,128]{2,1,0:T(8,128)}) custom-call(bf16[28,28,8,128]{3,2,1,0:T(8,128)(2,1)} %bitcast.91, f32[4,4,392,128]{3,2,1,0:T(8,128)} %get-tuple-element.161.refs_1_, bf16[4,4,392,128]{3,2,1,0:T(8,128)(2,1)} %get-tuple-element.162.refs_2_, ...), custom_call_target="tpu_custom_call" | custom-call | flops 16000000000 | bytes 10000000 | tf_op jit(solution)/shard_map/pallas_call | solution.py:835
  235.6 1.0 stack.17
  236.6 0.1 reshape.73
  236.7 0.9 fusion.3
  237.6 0.6 pad.20.refs_15_
  238.2 2.6 shard_map.241
  240.8 28.1 %all_to_all.5.packet_ref = bf16[32,112,128]{2,1,0:T(8,128)(2,1)} all-to-all(bf16[32,112,128]{2,1,0:T(8,128)(2,1)} %shard_map.241), channel_id=1, replica_groups=mesh['seq'=8,'wt'=4] {'seq','wt'}, dimensions={0} | all-to-all | bytes 1835008 | tf_op jit(solution)/shard_map/all_to_all | solution.py:699
  268.9 1.9 shard_map.242
  270.8 11.1 %all-gather = bf16[896,128]{1,0:T(8,128)(2,1)} all-gather(bf16[112,128]{1,0:T(8,128)(2,1)} %shard_map.242), channel_id=2, replica_groups=mesh['seq'=8,'wt'=4] {'seq'}, dimensions={0}, use_global_device_ids=true | all-gather | bytes 258048 | tf_op jit(solution)/shard_map/all_gather | solution.py:701
  281.9 1.7 shard_map.243
  283.6 1.3 reshape.74
  (94 shorter events, 1.0 us)
Async XLA Ops:
  0.6 12.3 %copy-start.11 = (f32[2,2,128]{2,1,0:T(2,128)S(1)}, f32[2,2,128]{2,1,0:T(2,128)}, u32[]{:S(2)}) copy-start(f32[2,2,128]{2,1,0:T(2,128)} %param.17) | copy-start | bytes 6148
  0.7 12.3 %copy-start.12 = (f32[2,2,128]{2,1,0:T(2,128)S(1)}, f32[2,2,128]{2,1,0:T(2,128)}, u32[]{:S(2)}) copy-start(f32[2,2,128]{2,1,0:T(2,128)} %param.20) | copy-start | bytes 6148
  0.7 12.9 %copy-start.9 = (f32[2,169,4]{1,2,0:T(4,128)S(1)}, f32[2,169,4]{1,2,0:T(4,128)}, u32[]{:S(2)}) copy-start(f32[2,169,4]{1,2,0:T(4,128)} %param.21) | copy-start | bytes 16228
  0.7 13.0 %copy-start.8 = (s32[49,49]{1,0:T(8,128)S(1)}, s32[49,49]{1,0:T(8,128)}, u32[]{:S(2)}) copy-start(s32[49,49]{1,0:T(8,128)} %param.16) | copy-start | bytes 28816
  3.0 13.6 %copy-start.10 = (f32[2,512]{1,0:T(2,128)S(1)}, f32[2,512]{1,0:T(2,128)}, u32[]{:S(2)}) copy-start(f32[2,512]{1,0:T(2,128)} %param.25) | copy-start | bytes 12292
  3.9 15.2 %copy-start.1 = (bf16[384,128]{1,0:T(8,128)(2,1)}, bf16[384,128]{1,0:T(8,128)(2,1)S(1)}, u32[]{:S(2)}) copy-start(bf16[384,128]{1,0:T(8,128)(2,1)S(1)} %get-tuple-element.195.refs_1_) | copy-start | bytes 294916
  3.9 25.5 %copy-start = (bf16[384,128]{1,0:T(8,128)(2,1)}, bf16[384,128]{1,0:T(8,128)(2,1)S(1)}, u32[]{:S(2)}) copy-start(bf16[384,128]{1,0:T(8,128)(2,1)S(1)} %get-tuple-element.118.refs_1_) | copy-start | bytes 294916
  3.9 19.0 %collective-permute-start = (bf16[384,128]{1,0:T(8,128)(2,1)S(1)}, bf16[384,128]{1,0:T(8,128)(2,1)S(1)}, u32[]{:S(2)}, u32[]{:S(2)}) collective-permute-start(bf16[384,128]{1,0:T(8,128)(2,1)S(1)} %get-tuple-element.195.refs_1_), channel_id=1, source_target_pairs={{0,3},{1,0},{2,1},{3,2},{4,7},{5,4},{6,5},{7,6},{8,11},{9,8},{10,9... | collective-permute-start | bytes 294920 | tf_op jit(solution)/shard_map/ppermute | solution.py:474
  9.0 13.9 %collective-permute-start.1 = (bf16[384,128]{1,0:T(8,128)(2,1)S(1)}, bf16[384,128]{1,0:T(8,128)(2,1)S(1)}, u32[]{:S(2)}, u32[]{:S(2)}) collective-permute-start(bf16[384,128]{1,0:T(8,128)(2,1)S(1)} %get-tuple-element.195.refs_1_), channel_id=1, source_target_pairs={{0,2},{1,3},{2,0},{3,1},{4,6},{5,7},{6,4},{7,5},{8,10},{9,11},{10,... | collective-permute-start | bytes 294920 | tf_op jit(solution)/shard_map/ppermute | solution.py:474
  9.0 14.0 %collective-permute-start.2 = (bf16[384,128]{1,0:T(8,128)(2,1)S(1)}, bf16[384,128]{1,0:T(8,128)(2,1)S(1)}, u32[]{:S(2)}, u32[]{:S(2)}) collective-permute-start(bf16[384,128]{1,0:T(8,128)(2,1)S(1)} %get-tuple-element.195.refs_1_), channel_id=1, source_target_pairs={{0,1},{1,2},{2,3},{3,0},{4,5},{5,6},{6,7},{7,4},{8,9},{9,10},{10,1... | collective-permute-start | bytes 294920 | tf_op jit(solution)/shard_map/ppermute | solution.py:474
  11.7 7.5 %copy-start.13 = (f32[2,2,128]{2,1,0:T(2,128)S(1)}, f32[2,2,128]{2,1,0:T(2,128)}, u32[]{:S(2)}) copy-start(f32[2,2,128]{2,1,0:T(2,128)} %param.23) | copy-start | bytes 6148
  11.7 7.5 %copy-start.14 = (f32[2,2,128]{2,1,0:T(2,128)S(1)}, f32[2,2,128]{2,1,0:T(2,128)}, u32[]{:S(2)}) copy-start(f32[2,2,128]{2,1,0:T(2,128)} %param.18) | copy-start | bytes 6148
  23.0 0.6 copy-start.2
  23.0 0.7 copy-start.3
  23.0 0.7 copy-start.4
  25.5 27.2 %collective-permute-start.3 = (bf16[384,128]{1,0:T(8,128)(2,1)S(1)}, bf16[384,128]{1,0:T(8,128)(2,1)S(1)}, u32[]{:S(2)}, u32[]{:S(2)}) collective-permute-start(bf16[384,128]{1,0:T(8,128)(2,1)S(1)} %get-tuple-element.118.refs_1_), channel_id=1, source_target_pairs={{0,3},{1,0},{2,1},{3,2},{4,7},{5,4},{6,5},{7,6},{8,11},{9,8},{10,9... | collective-permute-start | bytes 294920 | tf_op jit(solution)/shard_map/ppermute | solution.py:474
  28.3 50.0 %collective-permute-start.4 = (bf16[384,128]{1,0:T(8,128)(2,1)S(1)}, bf16[384,128]{1,0:T(8,128)(2,1)S(1)}, u32[]{:S(2)}, u32[]{:S(2)}) collective-permute-start(bf16[384,128]{1,0:T(8,128)(2,1)S(1)} %get-tuple-element.118.refs_1_), channel_id=1, source_target_pairs={{0,2},{1,3},{2,0},{3,1},{4,6},{5,7},{6,4},{7,5},{8,10},{9,11},{10,... | collective-permute-start | bytes 294920 | tf_op jit(solution)/shard_map/ppermute | solution.py:474
  29.5 48.9 %collective-permute-start.5 = (bf16[384,128]{1,0:T(8,128)(2,1)S(1)}, bf16[384,128]{1,0:T(8,128)(2,1)S(1)}, u32[]{:S(2)}, u32[]{:S(2)}) collective-permute-start(bf16[384,128]{1,0:T(8,128)(2,1)S(1)} %get-tuple-element.118.refs_1_), channel_id=1, source_target_pairs={{0,1},{1,2},{2,3},{3,0},{4,5},{5,6},{6,7},{7,4},{8,9},{9,10},{10,1... | collective-permute-start | bytes 294920 | tf_op jit(solution)/shard_map/ppermute | solution.py:474
  48.7 32.8 %collective-permute-start.6 = (bf16[3,28,8,128]{3,2,1,0:T(8,128)(2,1)}, bf16[3,28,8,128]{3,2,1,0:T(8,128)(2,1)S(1)}, u32[]{:S(2)}, u32[]{:S(2)}) collective-permute-start(bf16[3,28,8,128]{3,2,1,0:T(8,128)(2,1)} %get-tuple-element.121), channel_id=1, source_target_pairs={{0,28},{4,0},{8,4},{12,8},{16,12},{20,16},{24,20},{28,24},{1,29},{... | collective-permute-start | bytes 516104 | tf_op jit(solution)/shard_map/ppermute | solution.py:474
  49.2 32.3 %collective-permute-start.7 = (bf16[28,3,8,128]{3,2,1,0:T(8,128)(2,1)}, bf16[28,3,8,128]{3,2,1,0:T(8,128)(2,1)S(1)}, u32[]{:S(2)}, u32[]{:S(2)}) collective-permute-start(bf16[28,3,8,128]{3,2,1,0:T(8,128)(2,1)} %get-tuple-element.122), channel_id=1, source_target_pairs={{0,3},{1,0},{2,1},{3,2},{4,7},{5,4},{6,5},{7,6},{8,11},{9,8},{10,9... | collective-permute-start | bytes 516104 | tf_op jit(solution)/shard_map/ppermute | solution.py:474
  52.8 25.5 %copy-start.5 = (bf16[384,128]{1,0:T(8,128)(2,1)}, bf16[384,128]{1,0:T(8,128)(2,1)S(1)}, u32[]{:S(2)}) copy-start(bf16[384,128]{1,0:T(8,128)(2,1)S(1)} %collective-permute-done.3.refs_2_) | copy-start | bytes 294916
  52.8 28.7 %collective-permute-start.8 = (bf16[3,3,8,128]{3,2,1,0:T(8,128)(2,1)}, bf16[3,3,8,128]{3,2,1,0:T(8,128)(2,1)S(1)}, u32[]{:S(2)}, u32[]{:S(2)}) collective-permute-start(bf16[3,3,8,128]{3,2,1,0:T(8,128)(2,1)} %get-tuple-element.123), channel_id=1, source_target_pairs={{0,31},{1,28},{2,29},{3,30},{4,3},{5,0},{6,1},{7,2},{8,7},{9,4},{1... | collective-permute-start | bytes 55304 | tf_op jit(solution)/shard_map/ppermute | solution.py:484
  78.3 0.6 copy-start.6
  79.0 0.6 copy-start.7
  81.5 0.6 copy-start.23
  81.5 0.7 copy-start.15
  81.5 0.7 copy-start.16
  92.9 14.2 %collective-permute-start.10 = (bf16[28,3,8,128]{3,2,1,0:T(8,128)(2,1)}, bf16[28,3,8,128]{3,2,1,0:T(8,128)(2,1)S(1)}, u32[]{:S(2)}, u32[]{:S(2)}) collective-permute-start(bf16[28,3,8,128]{3,2,1,0:T(8,128)(2,1)} %get-tuple-element.132), channel_id=1, source_target_pairs={{0,1},{1,2},{2,3},{3,0},{4,5},{5,6},{6,7},{7,4},{8,9},{9,10},{10,1... | collective-permute-start | bytes 516104 | tf_op jit(solution)/shard_map/ppermute | solution.py:474
  94.6 12.5 %collective-permute-start.9 = (bf16[3,28,8,128]{3,2,1,0:T(8,128)(2,1)}, bf16[3,28,8,128]{3,2,1,0:T(8,128)(2,1)S(1)}, u32[]{:S(2)}, u32[]{:S(2)}) collective-permute-start(bf16[3,28,8,128]{3,2,1,0:T(8,128)(2,1)} %get-tuple-element.131), channel_id=1, source_target_pairs={{0,4},{4,8},{8,12},{12,16},{16,20},{20,24},{24,28},{28,0},{1,5},{5... | collective-permute-start | bytes 516104 | tf_op jit(solution)/shard_map/ppermute | solution.py:474
  94.6 12.5 %collective-permute-start.11 = (bf16[3,3,8,128]{3,2,1,0:T(8,128)(2,1)}, bf16[3,3,8,128]{3,2,1,0:T(8,128)(2,1)S(1)}, u32[]{:S(2)}, u32[]{:S(2)}) collective-permute-start(bf16[3,3,8,128]{3,2,1,0:T(8,128)(2,1)} %get-tuple-element.133), channel_id=1, source_target_pairs={{0,5},{1,6},{2,7},{3,4},{4,9},{5,10},{6,11},{7,8},{8,13},{9,14},{1... | collective-permute-start | bytes 55304 | tf_op jit(solution)/shard_map/ppermute | solution.py:484
  107.1 0.6 copy-start.26
  107.1 0.7 copy-start.21
  107.1 0.7 copy-start.22
  122.5 23.2 %collective-permute-start.12 = (bf16[3,28,8,128]{3,2,1,0:T(8,128)(2,1)}, bf16[3,28,8,128]{3,2,1,0:T(8,128)(2,1)S(1)}, u32[]{:S(2)}, u32[]{:S(2)}) collective-permute-start(bf16[3,28,8,128]{3,2,1,0:T(8,128)(2,1)} %get-tuple-element.145), channel_id=1, source_target_pairs={{0,28},{4,0},{8,4},{12,8},{16,12},{20,16},{24,20},{28,24},{1,29},{... | collective-permute-start | bytes 516104 | tf_op jit(solution)/shard_map/ppermute | solution.py:474
  125.2 20.5 %collective-permute-start.13 = (bf16[28,3,8,128]{3,2,1,0:T(8,128)(2,1)}, bf16[28,3,8,128]{3,2,1,0:T(8,128)(2,1)S(1)}, u32[]{:S(2)}, u32[]{:S(2)}) collective-permute-start(bf16[28,3,8,128]{3,2,1,0:T(8,128)(2,1)} %get-tuple-element.146), channel_id=1, source_target_pairs={{0,3},{1,0},{2,1},{3,2},{4,7},{5,4},{6,5},{7,6},{8,11},{9,8},{10,9... | collective-permute-start | bytes 516104 | tf_op jit(solution)/shard_map/ppermute | solution.py:474
  128.5 17.2 %collective-permute-start.14 = (bf16[3,3,8,128]{3,2,1,0:T(8,128)(2,1)}, bf16[3,3,8,128]{3,2,1,0:T(8,128)(2,1)S(1)}, u32[]{:S(2)}, u32[]{:S(2)}) collective-permute-start(bf16[3,3,8,128]{3,2,1,0:T(8,128)(2,1)} %get-tuple-element.147), channel_id=1, source_target_pairs={{0,31},{1,28},{2,29},{3,30},{4,3},{5,0},{6,1},{7,2},{8,7},{9,4},{1... | collective-permute-start | bytes 55304 | tf_op jit(solution)/shard_map/ppermute | solution.py:484
  145.7 0.6 copy-start.25
  145.7 0.7 copy-start.18
  145.7 0.7 copy-start.20
  160.7 19.6 %collective-permute-start.15 = (bf16[3,28,8,128]{3,2,1,0:T(8,128)(2,1)}, bf16[3,28,8,128]{3,2,1,0:T(8,128)(2,1)S(1)}, u32[]{:S(2)}, u32[]{:S(2)}) collective-permute-start(bf16[3,28,8,128]{3,2,1,0:T(8,128)(2,1)} %get-tuple-element.153), channel_id=1, source_target_pairs={{0,4},{4,8},{8,12},{12,16},{16,20},{20,24},{24,28},{28,0},{1,5},{5... | collective-permute-start | bytes 516104 | tf_op jit(solution)/shard_map/ppermute | solution.py:474
  161.0 19.3 %collective-permute-start.16 = (bf16[28,3,8,128]{3,2,1,0:T(8,128)(2,1)}, bf16[28,3,8,128]{3,2,1,0:T(8,128)(2,1)S(1)}, u32[]{:S(2)}, u32[]{:S(2)}) collective-permute-start(bf16[28,3,8,128]{3,2,1,0:T(8,128)(2,1)} %get-tuple-element.154), channel_id=1, source_target_pairs={{0,1},{1,2},{2,3},{3,0},{4,5},{5,6},{6,7},{7,4},{8,9},{9,10},{10,1... | collective-permute-start | bytes 516104 | tf_op jit(solution)/shard_map/ppermute | solution.py:474
  162.7 17.6 %collective-permute-start.17 = (bf16[3,3,8,128]{3,2,1,0:T(8,128)(2,1)}, bf16[3,3,8,128]{3,2,1,0:T(8,128)(2,1)S(1)}, u32[]{:S(2)}, u32[]{:S(2)}) collective-permute-start(bf16[3,3,8,128]{3,2,1,0:T(8,128)(2,1)} %get-tuple-element.155), channel_id=1, source_target_pairs={{0,5},{1,6},{2,7},{3,4},{4,9},{5,10},{6,11},{7,8},{8,13},{9,14},{1... | collective-permute-start | bytes 55304 | tf_op jit(solution)/shard_map/ppermute | solution.py:484
  180.3 0.6 copy-start.24
  180.3 0.7 copy-start.17
  180.3 0.7 copy-start.19

commit v3 on v2

--- a/solution.py
+++ b/solution.py
@@ -19,7 +19,9 @@
 OFF = -1e30
 BF = jnp.bfloat16
 F32 = jnp.float32
-VMEM_LIMIT = 56 * 1024 * 1024
+MIB = 1024 * 1024
+VMEM_LIMIT = 56 * MIB
+LIMITS = ((56, 56), (16, 16), (16, 16), (16, 16), 56)
 
 
 def mm(left, right):
@@ -83,27 +85,19 @@
     return total
 
 
-def lane_segments():
-    row = lax.broadcasted_iota(jnp.int32, (HEADS * SLOT, HEADS * SLOT), 0) >> 6
-    col = lax.broadcasted_iota(jnp.int32, (HEADS * SLOT, HEADS * SLOT), 1) >> 6
-    return jnp.where(row == col, 1.0, 0.0).astype(BF)
-
-
 def head_lanes():
     row = lax.broadcasted_iota(jnp.int32, (HEADS * SLOT, HEADS * HEAD_DIM), 0) >> 6
     col = lax.broadcasted_iota(jnp.int32, (HEADS * SLOT, HEADS * HEAD_DIM), 1) >> 5
     return jnp.where(row == col, 1.0, 0.0).astype(BF)
 
 
-def segment_max(scores):
+def segment_max(every):
     low = lax.broadcasted_iota(jnp.int32, (SLOT, 2 * SLOT), 1) < SLOT
-    parts = []
-    for start in (0, 2 * SLOT):
-        pair = scores[:, start : start + 2 * SLOT]
-        first = jnp.max(jnp.where(low, pair, OFF), 1, keepdims=True)
-        second = jnp.max(jnp.where(low, OFF, pair), 1, keepdims=True)
-        parts.append(jnp.where(low, first, second))
-    return jnp.concatenate(parts, 1)
+    pairs = [s[:, start : start + 2 * SLOT] for s in every for start in (0, 2 * SLOT)]
+    first = [jnp.max(jnp.where(low, pair, OFF), 1, keepdims=True) for pair in pairs]
+    second = [jnp.max(jnp.where(low, OFF, pair), 1, keepdims=True) for pair in pairs]
+    highest = [jnp.where(low, a, b) for a, b in zip(first, second)]
+    return [jnp.concatenate(highest[n : n + 2], 1) for n in range(0, len(highest), 2)]
 
 
 def zero_tails(first_step, count, *refs):
@@ -121,9 +115,9 @@
     return ref[pl.ds(image, SLOT, stride=images), :]
 
 
-def attention_forward(images, parts, bias, masks, probs_ref, out_ref):
+def attention_forward(images, parts, bias, masks, powers_ref, out_ref, share_ref):
     sc_q, sc_k, sc_v = parts
-    segments = lane_segments()
+    lanes = head_lanes()
     everything = range(images)
     scores = [
         mm_nt(window(sc_q, i, images).astype(BF), head_blocks(window(sc_k, i, images)))
@@ -134,48 +128,78 @@
     if masks is not None:
         apart = [masks[0, 0, i].astype(F32) * (-100.0 * LOG2E) for i in everything]
         scores = [scores[i] + jnp.concatenate([apart[i], apart[i]], 1) for i in everything]
-    powers = [jnp.exp2(s - segment_max(s)) for s in scores]
-    sums = [mm(p.astype(BF), segments) for p in powers]
-    probs = [(p / s).astype(BF) for p, s in zip(powers, sums)]
+    powers = [jnp.exp2(s - top) for s, top in zip(scores, segment_max(scores))]
+    powers = [p.astype(BF) for p in powers]
+    both = [
+        mm(powers[i], jnp.concatenate([head_blocks(window(sc_v, i, images)), lanes], 1))
+        for i in everything
+    ]
+    depth = lanes.shape[1]
+    shares = [1.0 / one[:, depth:] for one in both]
     for i in everything:
-        probs_ref[0, 0, i] = probs[i]
-        out_ref[pl.ds(i, SLOT, stride=images), :] = mm(
-            probs[i], head_blocks(window(sc_v, i, images))
-        )
-
-
-def attention_backward(images, parts, sc_grad, sc_out, probs_ref, grads, bias_acc):
+        place = pl.ds(i, SLOT, stride=images)
+        powers_ref[0, 0, i] = powers[i]
+        out_ref[place, :] = both[i][:, :depth] * shares[i]
+        share_ref[place, :] = shares[i]
+
+
+def attention_backward(images, parts, sc_grad, sc_out, powers_ref, grads, bias_acc):
     sc_q, sc_k, sc_v = parts
     sc_dq, sc_dk, sc_dv = grads
     lanes = head_lanes()
+    depth = lanes.shape[1]
     everything = range(images)
-    upstream = [window(sc_grad, i, images) for i in everything]
+    upstream = [window(sc_grad, i, images).astype(BF) for i in everything]
     centred = [
         mm_nt(
-            jnp.concatenate(
-                [
-                    upstream[i].astype(BF),
-                    (-(upstream[i] * window(sc_out, i, images))).astype(BF),
-                ],
-                1,
-            ),
+            jnp.concatenate([upstream[i], window(sc_out, i, images).astype(BF)], 1),
             jnp.concatenate([head_blocks(window(sc_v, i, images)), lanes], 1),
         )
         for i in everything
     ]
-    probs = [probs_ref[0, 0, i] for i in everything]
-    score_grads = [(probs[i].astype(F32) * centred[i]).astype(BF) for i in everything]
+    powers = [powers_ref[0, 0, i] for i in everything]
+    score_grads = [(powers[i].astype(F32) * centred[i]).astype(BF) for i in everything]
     total = score_grads[0].astype(F32)
     for i in everything[1:]:
         total = total + score_grads[i].astype(F32)
     bias_acc[...] += total
+    d_queries = [mm(score_grads[i], head_blocks(window(sc_k, i, images))) for i in everything]
+    empty = jnp.zeros((SLOT, depth), BF)
+    d_both = [
+        mm_tn(
+            jnp.concatenate([score_grads[i], powers[i]], 0),
+            jnp.concatenate(
+                [
+                    jnp.concatenate([window(sc_q, i, images).astype(BF), empty], 1),
+                    jnp.concatenate([empty, upstream[i]], 1),
+                ],
+                0,
+            ),
+        )
+        for i in everything
+    ]
     for i in everything:
         place = pl.ds(i, SLOT, stride=images)
-        sc_dq[place, :] = mm(score_grads[i], head_blocks(window(sc_k, i, images))) * SCALE
-        sc_dk[place, :] = (
-            gather_heads(mm_tn(score_grads[i], window(sc_q, i, images).astype(BF))) * SCALE
-        )
-        sc_dv[place, :] = gather_heads(mm_tn(probs[i], upstream[i].astype(BF)))
+        sc_dq[place, :] = d_queries[i] * SCALE
+        sc_dk[place, :] = gather_heads(d_both[i][:, :depth]) * SCALE
+        sc_dv[place, :] = gather_heads(d_both[i][:, depth:])
+
+
+def put_upstream(count, sc_grad, sc_out, gradient, out, share):
+    shared = gradient * share
+    sc_grad[:count, :] = shared
+    sc_out[:count, :] = -(shared * out)
+
+
+def put_norm(refs, normed, inverse):
+    normed_ref, inverse_ref = refs
+    normed_ref[0, 0] = normed.astype(BF)
+    inverse_ref[0, 0] = jnp.broadcast_to(inverse, normed.shape).astype(BF)
+
+
+def get_norm(refs):
+    normed_ref, inverse_ref = refs
+    return normed_ref[0, 0].astype(F32), inverse_ref[0, 0].astype(F32)
 
 
 def split_projection(hidden, w_qkv, qkv_bias, parts, count):
@@ -194,21 +218,24 @@
 
 def kernel_first_layer(
     images, place, rims, x_ref, w_qkv, w_proj, w_fc1, w_fc2, vecs, qkv_bias, fc1_bias, bias,
-    stream_out, hidden_out, middle_out, out_out, probs_out, act_out, slope_out,
-    sc_q, sc_k, sc_v, sc_out,
+    stream_out, hidden_out, out_out, share_out, powers_out, act_out, slope_out,
+    n_one, r_one, n_two, r_two, n_next, r_next,
+    sc_q, sc_k, sc_v, sc_out, sc_share,
 ):
     count = POS * images
     zero_tails(first_of_grid(), count, sc_q, sc_k, sc_v)
     stream = tokens_of(x_ref)
-    normed, _ = norm_parts(stream)
+    normed, inverse = norm_parts(stream)
+    put_norm((n_one, r_one), normed, inverse)
     hidden = (normed * vecs[0:1] + vecs[1:2]).astype(BF)
     split_projection(hidden, w_qkv[...], qkv_bias[...], (sc_q, sc_k, sc_v), count)
-    attention_forward(images, (sc_q, sc_k, sc_v), bias[...], None, probs_out, sc_out)
+    attention_forward(images, (sc_q, sc_k, sc_v), bias[...], None, powers_out, sc_out, sc_share)
     attended = sc_out[:count, :].astype(BF)
     out_out[0, 0] = attended
+    share_out[0, 0] = sc_share[:count, :]
     middle = stream + (mm(attended, w_proj[...]) + vecs[4:5])
-    middle_out[0, 0] = middle
-    normed, _ = norm_parts(middle)
+    normed, inverse = norm_parts(middle)
+    put_norm((n_two, r_two), normed, inverse)
     inner = (normed * vecs[2:3] + vecs[3:4]).astype(BF)
     activated, slope = gelu_parts(mm(inner, w_fc1[...]) + fc1_bias[...])
     activated = activated.astype(BF)
@@ -216,7 +243,8 @@
     slope_out[0, 0] = slope.astype(BF)
     stream = middle + mm(activated, w_fc2[...]) + vecs[5:6]
     stream_out[0, 0] = stream
-    normed, _ = norm_parts(stream)
+    normed, inverse = norm_parts(stream)
+    put_norm((n_next, r_next), normed, inverse)
     block = put_tokens(hidden_out, normed * vecs[6:7] + vecs[7:8])
     if rims is not None:
         put_rims(block, rims, place, "first")
@@ -226,12 +254,16 @@
     images, place, rims, hidden_ref, *refs
 ):
     halo, refs = (None, refs) if rims is None else (refs[:3], refs[3:])
-    w_qkv, qkv_bias, bias, masks, out_out, probs_out, held, sc_q, sc_k, sc_v, sc_out = refs
+    (
+        w_qkv, qkv_bias, bias, masks, out_out, share_out, powers_out,
+        held, sc_q, sc_k, sc_v, sc_out, sc_share,
+    ) = refs
     count = POS * images
     zero_tails(first_of_grid(), count, sc_q, sc_k, sc_v)
     hidden = ahead_window(hidden_ref, halo, held, place).astype(BF)
     split_projection(hidden, w_qkv[...], qkv_bias[...], (sc_q, sc_k, sc_v), count)
-    attention_forward(images, (sc_q, sc_k, sc_v), bias[...], masks, probs_out, sc_out)
+    attention_forward(images, (sc_q, sc_k, sc_v), bias[...], masks, powers_out, sc_out, sc_share)
+    share_out[0, 0] = sc_share[:count, :]
     block = put_tokens(out_out, sc_out[:count, :])
     if rims is not None:
         put_rims(block, rims, place, "last")
@@ -398,17 +430,17 @@
         (None, None, refs) if rims is None else (refs[:3], refs[3:6], refs[6:])
     )
     (
-        out_ref, probs_ref, w_qkv, qkv_bias, hidden_grad_out, g_qkv, qv_sums, bias_acc,
+        out_ref, share_ref, powers_ref, w_qkv, qkv_bias, hidden_grad_out, g_qkv, qv_sums, bias_acc,
         held, sc_q, sc_k, sc_v, sc_out, sc_grad, sc_dq, sc_dk, sc_dv,
     ) = refs
     count = POS * images
     zero_tails(first_of_grid(), count, sc_q, sc_k, sc_v, sc_out, sc_grad)
     hidden = ahead_window(hidden_ref, halo, held, place).astype(BF)
     split_projection(hidden, w_qkv[...], qkv_bias[...], (sc_q, sc_k, sc_v), count)
-    sc_out[:count, :] = tokens_of(out_ref)
-    sc_grad[:count, :] = ahead_window(low_ref, low_halo, held, place)
+    gradient = ahead_window(low_ref, low_halo, held, place)
+    put_upstream(count, sc_grad, sc_out, gradient, tokens_of(out_ref), share_ref[0, 0])
     grads = (sc_dq, sc_dk, sc_dv)
-    attention_backward(images, (sc_q, sc_k, sc_v), sc_grad, sc_out, probs_ref, grads, bias_acc)
+    attention_backward(images, (sc_q, sc_k, sc_v), sc_grad, sc_out, powers_ref, grads, bias_acc)
     joined = joined_gradients(count, grads, qv_sums)
     g_qkv[...] += mm_tn(hidden, joined)
     block = put_tokens(hidden_grad_out, mm_nt(joined, w_qkv[...]))
@@ -416,57 +448,52 @@
         put_rims(block, rims, place, "last")
 
 
-def kernel_first_feed_backward(
-    images, place, rims, hidden_grad_ref, rim_rows, rim_cols, corner, stream_ref, grad_ref, middle_ref, act_ref, slope_ref, att_ref,
-    w_proj, w_fc1, w_fc2, vecs,
-    grad_out, low_out, g_proj, g_fc1, g_fc2, sums, fc1_sums, held,
+def kernel_first_backward(
+    images, place, rims, hidden_grad_ref, rim_rows, rim_cols, corner, grad_ref,
+    n_one, r_one, n_two, r_two, n_next, r_next, act_ref, slope_ref, att_ref, share_ref, powers_ref,
+    w_qkv, w_proj, w_fc1, w_fc2, vecs, qkv_bias,
+    tokens_grad_out, g_qkv, g_proj, g_fc1, g_fc2, sums, fc1_sums, qv_sums, bias_acc,
+    held, sc_q, sc_k, sc_v, sc_out, sc_grad, sc_dq, sc_dk, sc_dv,
 ):
+    count = POS * images
+    zero_tails(first_of_grid(), count, sc_q, sc_k, sc_v, sc_out, sc_grad)
     upstream = behind_window(hidden_grad_ref, (rim_rows, rim_cols, corner), held, place)
-    normed, inverse = norm_parts(stream_ref[0, 0])
+    normed_one, inverse_one = get_norm((n_one, r_one))
+    hidden = (normed_one * vecs[0:1] + vecs[1:2]).astype(BF)
+    split_projection(hidden, w_qkv[...], qkv_bias[...], (sc_q, sc_k, sc_v), count)
+    normed, inverse = get_norm((n_next, r_next))
     gradient = grad_ref[0, 0] + norm_backward(upstream, normed, inverse, vecs[6:7])
     sums[4] += fold_rows(upstream * normed)
     sums[5] += fold_rows(upstream)
     out_low = gradient.astype(BF)
-    normed, inverse = norm_parts(middle_ref[0, 0])
+    normed, inverse = get_norm((n_two, r_two))
     inner = (normed * vecs[2:3] + vecs[3:4]).astype(BF)
     activated = act_ref[0, 0]
     expanded_low, inner_grad = feed_forward_backward(
         out_low, inner, activated, slope_ref[0, 0].astype(F32), w_fc1[...], w_fc2[...]
     )
+    updated = gradient + norm_backward(inner_grad, normed, inverse, vecs[2:3])
+    branch_low = updated.astype(BF)
+    low = mm_nt(branch_low, w_proj[...]).astype(BF).astype(F32)
+    attended = att_ref[0, 0]
+    put_upstream(count, sc_grad, sc_out, low, attended.astype(F32), share_ref[0, 0])
+    grads = (sc_dq, sc_dk, sc_dv)
+    attention_backward(images, (sc_q, sc_k, sc_v), sc_grad, sc_out, powers_ref, grads, bias_acc)
     g_fc2[...] += mm_tn(out_low, activated)
     g_fc1[...] += mm_tn(inner, expanded_low)
+    g_proj[...] += mm_tn(attended, branch_low)
     fc1_sums[...] += fold_rows(expanded_low.astype(F32))
-    updated = gradient + norm_backward(inner_grad, normed, inverse, vecs[2:3])
-    grad_out[0, 0] = updated
-    branch_low = updated.astype(BF)
-    g_proj[...] += mm_tn(att_ref[0, 0], branch_low)
-    low_out[0, 0] = mm_nt(branch_low, w_proj[...]).astype(BF)
     sums[0] += fold_rows(out_low.astype(F32))
     sums[1] += fold_rows(inner_grad * normed)
     sums[2] += fold_rows(inner_grad)
     sums[3] += fold_rows(branch_low.astype(F32))
-
-
-def kernel_first_attention_backward(
-    images, place, rims, x_ref, grad_ref, low_ref, att_ref, probs_ref, w_qkv, vecs, qkv_bias,
-    tokens_grad_out, g_qkv, qv_sums, bias_acc, sums,
-    sc_q, sc_k, sc_v, sc_out, sc_grad, sc_dq, sc_dk, sc_dv,
-):
-    count = POS * images
-    zero_tails(first_of_grid(), count, sc_q, sc_k, sc_v, sc_out, sc_grad)
-    normed, inverse = norm_parts(tokens_of(x_ref))
-    hidden = (normed * vecs[0:1] + vecs[1:2]).astype(BF)
-    split_projection(hidden, w_qkv[...], qkv_bias[...], (sc_q, sc_k, sc_v), count)
-    sc_out[:count, :] = att_ref[0, 0].astype(F32)
-    sc_grad[:count, :] = low_ref[0, 0].astype(F32)
-    grads = (sc_dq, sc_dk, sc_dv)
-    attention_backward(images, (sc_q, sc_k, sc_v), sc_grad, sc_out, probs_ref, grads, bias_acc)
     joined = joined_gradients(count, grads, qv_sums)
     g_qkv[...] += mm_tn(hidden, joined)
     upstream = mm_nt(joined, w_qkv[...])
-    put_tokens(tokens_grad_out, grad_ref[0, 0] + norm_backward(upstream, normed, inverse, vecs[0:1]))
-    sums[0] += fold_rows(upstream * normed)
-    sums[1] += fold_rows(upstream)
+    term = norm_backward(upstream, normed_one, inverse_one, vecs[0:1])
+    put_tokens(tokens_grad_out, updated + term)
+    sums[6] += fold_rows(upstream * normed_one)
+    sums[7] += fold_rows(upstream)
 
 
 def shift_by(array, axis, by):
@@ -571,14 +598,14 @@
 
 
 def small_rows(refs):
-    (sums00, sums0, sums1, qv0, qv1, fc1_0, fc1_1, table) = refs
+    (sums0, sums1, qv0, qv1, fc1_0, fc1_1, table) = refs
 
     def one(ref, k):
         return jnp.sum(ref[k], 0, keepdims=True)
 
     rows = [
-        one(sums00, 0), one(sums0, 1), one(sums0, 4), one(sums1, 1),
-        one(sums00, 1), one(sums0, 2), one(sums0, 5), one(sums1, 2),
+        one(sums0, 6), one(sums0, 1), one(sums0, 4), one(sums1, 1),
+        one(sums0, 7), one(sums0, 2), one(sums0, 5), one(sums1, 2),
         one(qv0, 0), one(qv0, 1), one(qv1, 0), one(qv1, 1),
         one(sums0, 3), one(sums0, 0), one(sums1, 3), one(sums1, 0),
     ]
@@ -589,7 +616,7 @@
 
 
 def kernel_pack(seqs, parts, each, *refs):
-    grads, smalls, out, held, lines = refs[:8], refs[8:16], refs[16], refs[17], refs[18]
+    grads, smalls, out, held, lines = refs[:8], refs[8:15], refs[15], refs[16], refs[17]
     depth = grads[0].shape[0]
     rows = depth // parts
     lines[...] = jnp.zeros_like(lines)
@@ -784,7 +811,7 @@
         jax.ShapeDtypeStruct((SHIFT, SHIFT, images, depth), BF),
     ]
 
-    def run(kernel, part, inputs, outputs, slots, earlier=None, held=False):
+    def run(kernel, part, inputs, outputs, slots, limit, earlier=None, held=False):
         steps, order = window_order(part, rows, cols)
 
         def spec_of(spec, shape):
@@ -840,27 +867,32 @@
             out_shape=types,
             scratch_shapes=scratch,
             input_output_aliases=aliases,
-            compiler_params=pltpu.CompilerParams(vmem_limit_bytes=VMEM_LIMIT),
+            compiler_params=pltpu.CompilerParams(vmem_limit_bytes=limit * MIB),
             cost_estimate=pl.CostEstimate(
                 flops=steps * 10**9, bytes_accessed=10**7, transcendentals=0
             ),
         )(*ins)
         return results[:n_out], results[n_out:]
 
-    def run_both(kernel, edge, inputs, halos, outputs, slots, by, held=False):
+    def run_both(kernel, edge, inputs, halos, outputs, slots, by, limits, held=False):
         lead = len(halos)
         rim_inputs = [(a, None) for halo in halos for a in halo]
         inputs_a = inputs[:lead] + rim_inputs + inputs[lead:]
-        first, rims = run(kernel, (edge, True), inputs_a, outputs, slots, held=held)
+        first, rims = run(
+            kernel, (edge, True), inputs_a, outputs, slots, limits[0], held=held
+        )
         rims = send_rims(rims, by)
-        return run(kernel, (edge, False), inputs, outputs, slots, first, held=held)[0], rims
+        second, _ = run(
+            kernel, (edge, False), inputs, outputs, slots, limits[1], first, held=held
+        )
+        return second, rims
 
     def total(*shape):
         return (jax.ShapeDtypeStruct(shape, F32), None)
 
     qkv0, proj0, fc10, fc20 = weights[0]
     qkv1, proj1, fc11, fc21 = weights[1]
-    (stream1, hidden1, middle0, att0, probs0, act0, slope0), halo = run_both(
+    (stream1, hidden1, att0, share0, powers0, act0, slope0, *norms0), halo = run_both(
         kernel_first_layer,
         "first",
         [
@@ -871,16 +903,18 @@
         [
             (flat_type(depth, F32), flat(depth)),
             (jax.ShapeDtypeStruct(field_shape, BF), field),
+            (flat_type(depth, BF), flat(depth)),
             (flat_type(depth, F32), flat(depth)),
-            (flat_type(depth, BF), flat(depth)),
             (probs_type, probs_spec),
             (flat_type(wide, BF), flat(wide)),
             (flat_type(wide, BF), flat(wide)),
+            *[(flat_type(depth, BF), flat(depth))] * 6,
         ],
-        4,
+        5,
         -1,
-    )
-    (att1, probs1), out_halo = run_both(
+        LIMITS[0],
+    )
+    (att1, share1, powers1), out_halo = run_both(
         kernel_shifted_forward,
         "last",
         [
@@ -888,9 +922,14 @@
             (masks, mask_spec),
         ],
         [halo],
-        [(jax.ShapeDtypeStruct(field_shape, BF), field), (probs_type, probs_spec)],
-        4,
+        [
+            (jax.ShapeDtypeStruct(field_shape, BF), field),
+            (flat_type(depth, F32), flat(depth)),
+            (probs_type, probs_spec),
+        ],
+        5,
         1,
+        LIMITS[1],
         held=True,
     )
     (mixed, grad1, low1, g_proj1, g_fc11, g_fc21, sums1, fc1_sums1), low_halo = run_both(
@@ -910,13 +949,15 @@
         ],
         0,
         -1,
+        LIMITS[2],
         held=True,
     )
     (hidden_grad1, g_qkv1, qv_sums1, bias_sums1), grad_halo = run_both(
         kernel_shifted_backward,
         "last",
         [
-            (hidden1, None), (low1, None), (att1, field), (probs1, probs_spec),
+            (hidden1, None), (low1, None), (att1, field), (share1, flat(depth)),
+            (powers1, probs_spec),
             (qkv1, None), (qkv_biases[1], None),
         ],
         [halo, low_halo],
@@ -926,38 +967,29 @@
         ],
         8,
         1,
+        LIMITS[3],
         held=True,
     )
-    (grad0, low0, g_proj0, g_fc10, g_fc20, sums0, fc1_sums0), _ = run(
-        kernel_first_feed_backward,
+    (
+        tokens_grad, g_qkv0, g_proj0, g_fc10, g_fc20, sums0, fc1_sums0, qv_sums0, bias_sums0
+    ), _ = run(
+        kernel_first_backward,
         "all",
         [
-            (hidden_grad1, None), *[(a, None) for a in grad_halo],
-            (stream1, flat(depth)), (grad1, flat(depth)),
-            (middle0, flat(depth)), (act0, flat(wide)), (slope0, flat(wide)), (att0, flat(depth)),
-            (proj0, None), (fc10, None), (fc20, None), (vecs[0], None),
-        ],
-        [
-            (flat_type(depth, F32), flat(depth)), (flat_type(depth, BF), flat(depth)),
-            total(depth, depth), total(depth, wide), total(depth, wide), total(6, 8, depth),
-            total(8, wide),
-        ],
-        0,
-        held=True,
-    )
-    (tokens_grad, g_qkv0, qv_sums0, bias_sums0, sums00), _ = run(
-        kernel_first_attention_backward,
-        "all",
-        [
-            (x, field), (grad0, flat(depth)), (low0, flat(depth)), (att0, flat(depth)),
-            (probs0, probs_spec), (qkv0, None), (vecs[0], None), (qkv_biases[0], None),
+            (hidden_grad1, None), *[(a, None) for a in grad_halo], (grad1, flat(depth)),
+            *[(a, flat(depth)) for a in norms0], (act0, flat(wide)), (slope0, flat(wide)),
+            (att0, flat(depth)), (share0, flat(depth)), (powers0, probs_spec),
+            (qkv0, None), (proj0, None), (fc10, None), (fc20, None), (vecs[0], None),
+            (qkv_biases[0], None),
         ],
         [
             (jax.ShapeDtypeStruct(field_shape, F32), field),
-            total(depth, 3 * depth), total(2, 8, depth), total(SLOT, HEADS * SLOT),
-            total(2, 8, depth),
+            total(depth, 3 * depth), total(depth, depth), total(depth, wide), total(depth, wide),
+            total(8, 8, depth), total(8, wide), total(2, 8, depth), total(SLOT, HEADS * SLOT),
         ],
         8,
+        LIMITS[4],
+        held=True,
     )
 
     bias_sums = jnp.stack([bias_sums0, bias_sums1]).reshape(2, SLOT, HEADS, SLOT)
@@ -966,7 +998,7 @@
     table = jnp.pad(table, ((0, 0), (0, -table_size % 128)))
     gains, shifts, d_qkv, d_qv, d_table, d_proj, d_out, d_fc1, d_fc1_bias, d_fc2 = sum_everywhere(
         [g_qkv0, g_proj0, g_fc10, g_fc20, g_qkv1, g_proj1, g_fc11, g_fc21],
-        [sums00, sums0, sums1, qv_sums0, qv_sums1, fc1_sums0, fc1_sums1, table],
+        [sums0, sums1, qv_sums0, qv_sums1, fc1_sums0, fc1_sums1, table],
         depth,
         wide,
     )

time: 286 us -> 256 us (0.90)
  Pallas kernels: 193 us -> 161 us
  local copies, waits for them, and re-layouts: 18.8 us -> 22 us
    pallas_call x10 -> x9, Pallas kernels: 183 us -> 151 us  [run(): pl.pallas_call(body, grid=(steps,), in_specs=in_specs, out_specs=out_spec...]
    unnamed x68 -> x80, local copies, waits for them, and re-layouts: 5.69 us -> 11.4 us
  transfers between devices with their start and end apart: 18 -> 18, of which waited for: 0 -> 0; matrix products, arithmetic and copies ran while one was open for 5% -> 4% of each run, Pallas kernels for 32% -> 32%
where the time goes in v3:
time: 256 us; the launch traced here: 255 us
  Pallas kernels  161 us (63%)
  blocking collectives  39.3 us (15%)
  starting transfers between devices  25.8 us (10%)
  local copies, waits for them, and re-layouts  22 us (9%)
  matrix products  2.85 us (1%)
  other arithmetic  2.57 us (1%)
    pallas_call x9, Pallas kernels, run(): pl.pallas_call(body, grid=(steps,), in_specs=in_specs, out_specs=out_spec...  151 us
    all_to_all x1, blocking collectives, sum_everywhere(): packets = lax.all_to_all(packets, ('seq', 'wt'), 0, 0, tiled=True)  28.2 us
    ppermute x14, starting transfers between devices, shift_by(): lax.ppermute(array, axis, [(i, (i + by) % count) for i in range(count)])  23.9 us
    unnamed x80, local copies, waits for them, and re-layouts  11.4 us
    all_gather x1, blocking collectives, sum_everywhere(): mine = lax.all_gather(mine, 'seq', axis=0)  11.1 us
    pallas_call x3, Pallas kernels, whole_kernel(): pl.pallas_call(body, in_specs=[full] * len(inputs), out_specs=[full] * le...  6.19 us
  transfers between devices with their start and end apart: 18, of which 0 were waited for; matrix products, arithmetic and copies ran while one was open for 4% of the time, Pallas kernels for 32%

profile of v3, /device:TPU:0, one launch (start us, length us, event | category | flops | bytes accessed | tf_op | source)
XLA Modules:
  0.0 254.9 jit_solution(6445762022787520199)
XLA Ops:
  0.6 0.8 slice_bitcast_fusion.2
  1.4 0.8 slice_bitcast_fusion
  2.2 0.7 constant_dynamic-update-slice_fusion.14
  3.0 0.8 constant_dynamic-update-slice_fusion.9
  3.9 5.1 %collective-permute-start = (bf16[384,128]{1,0:T(8,128)(2,1)S(1)}, bf16[384,128]{1,0:T(8,128)(2,1)S(1)}, u32[]{:S(2)}, u32[]{:S(2)}) collective-permute-start(bf16[384,128]{1,0:T(8,128)(2,1)S(1)} %get-tuple-element.217.refs_1_), channel_id=1, source_target_pairs={{0,3},{1,0},{2,1},{3,2},{4,7},{5,4},{6,5},{7,6},{8,11},{9,8},{10,9... | collective-permute-start | bytes 294920 | tf_op jit(solution)/shard_map/ppermute | solution.py:501
  9.0 1.0 collective-permute-start.2
  10.0 1.2 reshape.72
  11.2 0.3 copy.47
  11.4 0.2 ne.15
  11.6 1.3 broadcast_compare_fusion
  13.0 0.6 broadcast_in_dim.15.refs_6_.refs_21_
  13.7 2.0 fusion.6
  15.8 0.8 squeeze.52.refs_8_
  16.6 0.6 fusion.13
  17.2 0.1 squeeze.55.refs_6_.refs_3_
  17.3 0.6 pad.17
  18.0 0.6 stack.15.refs_5_.refs_20_
  18.6 1.2 add_convert_fusion.refs_7_.refs_4_
  19.8 0.6 copy-done.19
  20.4 1.8 shard_map.229
  22.3 2.8 %collective-permute-start.3 = (bf16[384,128]{1,0:T(8,128)(2,1)S(1)}, bf16[384,128]{1,0:T(8,128)(2,1)S(1)}, u32[]{:S(2)}, u32[]{:S(2)}) collective-permute-start(bf16[384,128]{1,0:T(8,128)(2,1)S(1)} %get-tuple-element.135.refs_1_), channel_id=1, source_target_pairs={{0,3},{1,0},{2,1},{3,2},{4,7},{5,4},{6,5},{7,6},{8,11},{9,8},{10,9... | collective-permute-start | bytes 294920 | tf_op jit(solution)/shard_map/ppermute | solution.py:501
  25.1 1.1 collective-permute-start.4
  26.2 18.7 %shard_map.230 = (f32[4,4,392,128]{3,2,1,0:T(8,128)}, bf16[28,28,8,128]{3,2,1,0:T(8,128)(2,1)}, bf16[4,4,392,128]{3,2,1,0:T(8,128)(2,1)}, f32[4,4,392,128]{3,2,1...) custom-call(bf16[28,28,8,128]{3,2,1,0:T(8,128)(2,1)} %bitcast.85, ...), custom_call_target="tpu_custom_call" | custom-call | flops 7000000000 | bytes 10000000 | tf_op jit(solution)/shard_map/pallas_call | solution.py:862
  44.9 0.5 collective-permute-start.6
  45.5 3.5 %collective-permute-start.7 = (bf16[28,3,8,128]{3,2,1,0:T(8,128)(2,1)}, bf16[28,3,8,128]{3,2,1,0:T(8,128)(2,1)S(1)}, u32[]{:S(2)}, u32[]{:S(2)}) collective-permute-start(bf16[28,3,8,128]{3,2,1,0:T(8,128)(2,1)} %get-tuple-element.139), channel_id=1, source_target_pairs={{0,3},{1,0},{2,1},{3,2},{4,7},{5,4},{6,5},{7,6},{8,11},{9,8},{10,9... | collective-permute-start | bytes 516104 | tf_op jit(solution)/shard_map/ppermute | solution.py:501
  49.0 1.9 collective-permute-start.8
  50.9 22.9 %shard_map.231 = (f32[4,4,392,128]{3,2,1,0:T(8,128)}, bf16[28,28,8,128]{3,2,1,0:T(8,128)(2,1)}, bf16[4,4,392,128]{3,2,1,0:T(8,128)(2,1)}, f32[4,4,392,128]{3,2,1...) custom-call(bf16[28,28,8,128]{3,2,1,0:T(8,128)(2,1)} %bitcast.86, ...), custom_call_target="tpu_custom_call", output_to_operand_aliasing={{0}: (9, {}), {1}: (10, {}), {2}: (11, {}), {3}: (12, {}), ... | custom-call | flops 8999999488 | bytes 10000000 | tf_op jit(solution)/shard_map/pallas_call | solution.py:862
  73.9 0.6 copy-done.21
  74.5 0.6 copy-done.22
  75.1 1.9 shard_map.232
  77.0 1.4 copy-done.1
  78.4 0.9 copy-done.12
  79.3 7.2 %shard_map.233 = (bf16[28,28,8,128]{3,2,1,0:T(8,128)(2,1)S(1)}, f32[4,4,392,128]{3,2,1,0:T(8,128)S(1)}, bf16[4,4,8,64,256]{4,3,2,1,0:T(8,128)(2,1)S(1)}, bf16[3,...) custom-call(bf16[28,28,8,128]{3,2,1,0:T(8,128)(2,1)S(1)} %copy-done.1, ...), custom_call_target="tpu_custom_call" | custom-call | flops 7000000000 | bytes 10000000 | tf_op jit(solution)/shard_map/pallas_call | solution.py:862
  86.5 1.8 collective-permute-start.10
  88.4 9.0 %shard_map.234 = (bf16[28,28,8,128]{3,2,1,0:T(8,128)(2,1)S(1)}, f32[4,4,392,128]{3,2,1,0:T(8,128)S(1)}, bf16[4,4,8,64,256]{4,3,2,1,0:T(8,128)(2,1)S(1)}) custom-call(bf16[28,28,8,128]{3,2,1,0:T(8,128)(2,1)S(1)} %copy-done.1, bf16[128,384]{1,0:T(8,128)(2,1)S(1)} %copy-done.13, ...), custom_call_target="tpu_custom_call", output_to_operand_aliasing={{0}: (5, {}), {1}: (6, {}), {2}: (7, {})} | custom-call | flops 8999999488 | bytes 10000000 | tf_op jit(solution)/shard_map/pallas_call | solution.py:862
  97.5 12.5 %shard_map.235 = (bf16[28,28,8,128]{3,2,1,0:T(8,128)(2,1)}, f32[4,4,392,128]{3,2,1,0:T(8,128)S(1)}, bf16[28,28,8,128]{3,2,1,0:T(8,128)(2,1)S(1)}, f32[128,128]{1...) custom-call(bf16[28,28,8,128]{3,2,1,0:T(8,128)(2,1)S(1)} %get-tuple-, ...), custom_call_target="tpu_custom_call" | custom-call | flops 7000000000 | bytes 10000000 | tf_op jit(solution)/shard_map/pallas_call | solution.py:862
  109.9 2.6 %collective-permute-start.12 = (bf16[3,28,8,128]{3,2,1,0:T(8,128)(2,1)S(1)}, bf16[3,28,8,128]{3,2,1,0:T(8,128)(2,1)S(1)}, u32[]{:S(2)}, u32[]{:S(2)}) collective-permute-start(bf16[3,28,8,128]{3,2,1,0:T(8,128)(2,1)S(1)} %get-tuple-element.164), channel_id=1, source_target_pairs={{0,28},{4,0},{8,4},{12,8},{16,12},{20,16},{24,20},{28,24},{1,29},{... | collective-permute-start | bytes 516104 | tf_op jit(solution)/shard_map/ppermute | solution.py:501
  112.5 3.2 %collective-permute-start.13 = (bf16[28,3,8,128]{3,2,1,0:T(8,128)(2,1)S(1)}, bf16[28,3,8,128]{3,2,1,0:T(8,128)(2,1)S(1)}, u32[]{:S(2)}, u32[]{:S(2)}) collective-permute-start(bf16[28,3,8,128]{3,2,1,0:T(8,128)(2,1)S(1)} %get-tuple-element.165), channel_id=1, source_target_pairs={{0,3},{1,0},{2,1},{3,2},{4,7},{5,4},{6,5},{7,6},{8,11},{9,8},{10,9... | collective-permute-start | bytes 516104 | tf_op jit(solution)/shard_map/ppermute | solution.py:501
  115.8 0.1 collective-permute-start.14
  115.9 14.8 %shard_map.236 = (bf16[28,28,8,128]{3,2,1,0:T(8,128)(2,1)}, f32[4,4,392,128]{3,2,1,0:T(8,128)S(1)}, bf16[28,28,8,128]{3,2,1,0:T(8,128)(2,1)S(1)}, f32[128,128]{1...) custom-call(bf16[28,28,8,128]{3,2,1,0:T(8,128)(2,1)S(1)} %get-tuple-, ...), custom_call_target="tpu_custom_call", output_to_operand_aliasing={{0}: (8, {}), {1}: (9, {}), {2}: (10, {})} | custom-call | flops 8999999488 | bytes 10000000 | tf_op jit(solution)/shard_map/pallas_call | solution.py:862
  130.7 0.7 copy-done.2
  131.4 0.7 copy-done.3
  132.1 0.6 copy-done.5
  132.7 0.6 copy-done.6
  133.3 0.6 copy-done.7
  134.0 11.1 %shard_map.237 = (bf16[28,28,8,128]{3,2,1,0:T(8,128)(2,1)S(1)}, f32[128,384]{1,0:T(8,128)S(1)}, f32[2,8,128]{2,1,0:T(8,128)S(1)}, f32[64,256]{1,0:T(8,128)S(1)},...) custom-call(bf16[28,28,8,128]{3,2,1,0:T(8,128)(2,1)S(1)} %copy-done.1, ...), custom_call_target="tpu_custom_call" | custom-call | flops 7000000000 | bytes 10000000 | tf_op jit(solution)/shard_map/pallas_call | solution.py:862
  145.1 0.3 collective-permute-start.15
  145.4 1.7 collective-permute-start.16
  147.2 13.9 %shard_map.238 = (bf16[28,28,8,128]{3,2,1,0:T(8,128)(2,1)S(1)}, f32[128,384]{1,0:T(8,128)S(1)}, f32[2,8,128]{2,1,0:T(8,128)S(1)}, f32[64,256]{1,0:T(8,128)S(1)}) custom-call(bf16[28,28,8,128]{3,2,1,0:T(8,128)(2,1)S(1)} %copy-done.1, bf16[28,28,8,128]{3,2,1,0:T(8,128)(2,1)S(1)} %get-tuple-element.161.refs_1_, ...), custom_call_target="tpu_custom_call", output_to_operand_aliasing={{0}: (7, {})} | custom-call | flops 8999999488 | bytes 10000000 | tf_op jit(solution)/shard_map/pallas_call | solution.py:862
  161.1 0.7 copy-done.4
  161.8 0.6 copy-done.8
  162.4 1.2 copy-done.15
  163.7 0.5 copy-done.32
  164.4 41.1 %shard_map.239 = (f32[28,28,8,128]{3,2,1,0:T(8,128)}, f32[128,384]{1,0:T(8,128)}, f32[128,128]{1,0:T(8,128)}, f32[128,512]{1,0:T(8,128)}, f32[128,512]{1,0:T(8,1...) custom-call(bf16[28,28,8,128]{3,2,1,0:T(8,128)(2,1)} %copy-done.15, ...), custom_call_target="tpu_custom_call" | custom-call | flops 16000000000 | bytes 10000000 | tf_op jit(solution)/shard_map/pallas_call | solution.py:862
  205.6 0.9 stack.17
  206.6 0.1 reshape.73
  206.7 0.9 fusion.3
  207.6 0.6 pad.20.refs_14_
  208.2 2.6 %shard_map.240 = bf16[32,112,128]{2,1,0:T(8,128)(2,1)} custom-call(f32[128,384]{1,0:T(8,128)} %get-tuple-element.188.refs_0_, f32[128,128]{1,0:T(8,128)} %get-tuple-element.189.refs_1_, f32[128,512]{1,0:T(8,128)} %get-tuple-element.190.refs_2_, f32[128,512]{1,0:T(8,128)} %get-tuple-element.191.refs_3_, f32[128,384]{1,0:T(8,128)} %copy-done.4, ...), custom_call_target="tpu_custom_call" | custom-call | tf_op jit(solution)/shard_map/pallas_call | solution.py:694
  210.7 28.2 %all_to_all.5.packet_ref = bf16[32,112,128]{2,1,0:T(8,128)(2,1)} all-to-all(bf16[32,112,128]{2,1,0:T(8,128)(2,1)} %shard_map.240), channel_id=1, replica_groups=mesh['seq'=8,'wt'=4] {'seq','wt'}, dimensions={0} | all-to-all | bytes 1835008 | tf_op jit(solution)/shard_map/all_to_all | solution.py:726
  238.9 1.9 shard_map.241
  240.9 11.1 %all-gather = bf16[896,128]{1,0:T(8,128)(2,1)} all-gather(bf16[112,128]{1,0:T(8,128)(2,1)} %shard_map.241), channel_id=2, replica_groups=mesh['seq'=8,'wt'=4] {'seq'}, dimensions={0}, use_global_device_ids=true | all-gather | bytes 258048 | tf_op jit(solution)/shard_map/all_gather | solution.py:728
  251.9 1.7 shard_map.242
  253.6 1.3 reshape.74
  (105 shorter events, 0.9 us)
Async XLA Ops:
  3.8 9.1 %copy-start.18 = (bf16[384,128]{1,0:T(8,128)(2,1)}, bf16[384,128]{1,0:T(8,128)(2,1)S(1)}, u32[]{:S(2)}) copy-start(bf16[384,128]{1,0:T(8,128)(2,1)S(1)} %get-tuple-element.217.refs_1_) | copy-start | bytes 294916
  3.9 22.4 %copy-start.17 = (bf16[384,128]{1,0:T(8,128)(2,1)}, bf16[384,128]{1,0:T(8,128)(2,1)S(1)}, u32[]{:S(2)}) copy-start(bf16[384,128]{1,0:T(8,128)(2,1)S(1)} %get-tuple-element.135.refs_1_) | copy-start | bytes 294916
  3.9 9.1 %copy-start.26 = (f32[2,2,128]{2,1,0:T(2,128)S(1)}, f32[2,2,128]{2,1,0:T(2,128)}, u32[]{:S(2)}) copy-start(f32[2,2,128]{2,1,0:T(2,128)} %param.17) | copy-start | bytes 6148
  3.9 9.1 %copy-start.27 = (f32[2,2,128]{2,1,0:T(2,128)S(1)}, f32[2,2,128]{2,1,0:T(2,128)}, u32[]{:S(2)}) copy-start(f32[2,2,128]{2,1,0:T(2,128)} %param.20) | copy-start | bytes 6148
  3.9 15.9 %collective-permute-start = (bf16[384,128]{1,0:T(8,128)(2,1)S(1)}, bf16[384,128]{1,0:T(8,128)(2,1)S(1)}, u32[]{:S(2)}, u32[]{:S(2)}) collective-permute-start(bf16[384,128]{1,0:T(8,128)(2,1)S(1)} %get-tuple-element.217.refs_1_), channel_id=1, source_target_pairs={{0,3},{1,0},{2,1},{3,2},{4,7},{5,4},{6,5},{7,6},{8,11},{9,8},{10,9... | collective-permute-start | bytes 294920 | tf_op jit(solution)/shard_map/ppermute | solution.py:501
  9.0 10.8 %collective-permute-start.1 = (bf16[384,128]{1,0:T(8,128)(2,1)S(1)}, bf16[384,128]{1,0:T(8,128)(2,1)}, u32[]{:S(2)}, u32[]{:S(2)}) collective-permute-start(bf16[384,128]{1,0:T(8,128)(2,1)S(1)} %get-tuple-element.217.refs_1_), channel_id=1, source_target_pairs={{0,2},{1,3},{2,0},{3,1},{4,6},{5,7},{6,4},{7,5},{8,10},{9,11},{10,... | collective-permute-start | bytes 294920 | tf_op jit(solution)/shard_map/ppermute | solution.py:501
  9.0 10.8 %collective-permute-start.2 = (bf16[384,128]{1,0:T(8,128)(2,1)S(1)}, bf16[384,128]{1,0:T(8,128)(2,1)}, u32[]{:S(2)}, u32[]{:S(2)}) collective-permute-start(bf16[384,128]{1,0:T(8,128)(2,1)S(1)} %get-tuple-element.217.refs_1_), channel_id=1, source_target_pairs={{0,1},{1,2},{2,3},{3,0},{4,5},{5,6},{6,7},{7,4},{8,9},{9,10},{10,1... | collective-permute-start | bytes 294920 | tf_op jit(solution)/shard_map/ppermute | solution.py:501
  10.0 3.6 %copy-start.24 = (f32[2,169,4]{1,2,0:T(4,128)S(1)}, f32[2,169,4]{1,2,0:T(4,128)}, u32[]{:S(2)}) copy-start(f32[2,169,4]{1,2,0:T(4,128)} %param.21) | copy-start | bytes 16228
  10.0 3.6 %copy-start.23 = (s32[49,49]{1,0:T(8,128)S(1)}, s32[49,49]{1,0:T(8,128)}, u32[]{:S(2)}) copy-start(s32[49,49]{1,0:T(8,128)} %param.16) | copy-start | bytes 28816
  11.6 5.0 %copy-start.25 = (f32[2,512]{1,0:T(2,128)S(1)}, f32[2,512]{1,0:T(2,128)}, u32[]{:S(2)}) copy-start(f32[2,512]{1,0:T(2,128)} %param.25) | copy-start | bytes 12292
  15.7 2.2 copy-start.28
  15.7 2.2 copy-start.29
  19.8 0.6 copy-start.19
  22.3 26.7 %collective-permute-start.3 = (bf16[384,128]{1,0:T(8,128)(2,1)S(1)}, bf16[384,128]{1,0:T(8,128)(2,1)S(1)}, u32[]{:S(2)}, u32[]{:S(2)}) collective-permute-start(bf16[384,128]{1,0:T(8,128)(2,1)S(1)} %get-tuple-element.135.refs_1_), channel_id=1, source_target_pairs={{0,3},{1,0},{2,1},{3,2},{4,7},{5,4},{6,5},{7,6},{8,11},{9,8},{10,9... | collective-permute-start | bytes 294920 | tf_op jit(solution)/shard_map/ppermute | solution.py:501
  25.1 48.7 %collective-permute-start.4 = (bf16[384,128]{1,0:T(8,128)(2,1)S(1)}, bf16[384,128]{1,0:T(8,128)(2,1)S(1)}, u32[]{:S(2)}, u32[]{:S(2)}) collective-permute-start(bf16[384,128]{1,0:T(8,128)(2,1)S(1)} %get-tuple-element.135.refs_1_), channel_id=1, source_target_pairs={{0,2},{1,3},{2,0},{3,1},{4,6},{5,7},{6,4},{7,5},{8,10},{9,11},{10,... | collective-permute-start | bytes 294920 | tf_op jit(solution)/shard_map/ppermute | solution.py:501
  26.2 47.6 %collective-permute-start.5 = (bf16[384,128]{1,0:T(8,128)(2,1)S(1)}, bf16[384,128]{1,0:T(8,128)(2,1)S(1)}, u32[]{:S(2)}, u32[]{:S(2)}) collective-permute-start(bf16[384,128]{1,0:T(8,128)(2,1)S(1)} %get-tuple-element.135.refs_1_), channel_id=1, source_target_pairs={{0,1},{1,2},{2,3},{3,0},{4,5},{5,6},{6,7},{7,4},{8,9},{9,10},{10,1... | collective-permute-start | bytes 294920 | tf_op jit(solution)/shard_map/ppermute | solution.py:501
  44.9 32.0 %collective-permute-start.6 = (bf16[3,28,8,128]{3,2,1,0:T(8,128)(2,1)}, bf16[3,28,8,128]{3,2,1,0:T(8,128)(2,1)S(1)}, u32[]{:S(2)}, u32[]{:S(2)}) collective-permute-start(bf16[3,28,8,128]{3,2,1,0:T(8,128)(2,1)} %get-tuple-element.138), channel_id=1, source_target_pairs={{0,28},{4,0},{8,4},{12,8},{16,12},{20,16},{24,20},{28,24},{1,29},{... | collective-permute-start | bytes 516104 | tf_op jit(solution)/shard_map/ppermute | solution.py:501
  45.5 31.5 %collective-permute-start.7 = (bf16[28,3,8,128]{3,2,1,0:T(8,128)(2,1)}, bf16[28,3,8,128]{3,2,1,0:T(8,128)(2,1)S(1)}, u32[]{:S(2)}, u32[]{:S(2)}) collective-permute-start(bf16[28,3,8,128]{3,2,1,0:T(8,128)(2,1)} %get-tuple-element.139), channel_id=1, source_target_pairs={{0,3},{1,0},{2,1},{3,2},{4,7},{5,4},{6,5},{7,6},{8,11},{9,8},{10,9... | collective-permute-start | bytes 516104 | tf_op jit(solution)/shard_map/ppermute | solution.py:501
  49.0 24.8 %copy-start.20 = (bf16[384,128]{1,0:T(8,128)(2,1)}, bf16[384,128]{1,0:T(8,128)(2,1)S(1)}, u32[]{:S(2)}) copy-start(bf16[384,128]{1,0:T(8,128)(2,1)S(1)} %collective-permute-done.3.refs_2_) | copy-start | bytes 294916
  49.0 27.9 %collective-permute-start.8 = (bf16[3,3,8,128]{3,2,1,0:T(8,128)(2,1)}, bf16[3,3,8,128]{3,2,1,0:T(8,128)(2,1)S(1)}, u32[]{:S(2)}, u32[]{:S(2)}) collective-permute-start(bf16[3,3,8,128]{3,2,1,0:T(8,128)(2,1)} %get-tuple-element.140), channel_id=1, source_target_pairs={{0,31},{1,28},{2,29},{3,30},{4,3},{5,0},{6,1},{7,2},{8,7},{9,4},{1... | collective-permute-start | bytes 55304 | tf_op jit(solution)/shard_map/ppermute | solution.py:511
  73.8 0.6 copy-start.21
  74.5 0.6 copy-start.22
  77.0 1.4 copy-start.1
  78.4 0.9 copy-start.12
  79.3 9.0 %copy-start.13 = (bf16[128,384]{1,0:T(8,128)(2,1)S(1)}, bf16[128,384]{1,0:T(8,128)(2,1)}, u32[]{:S(2)}) copy-start(bf16[128,384]{1,0:T(8,128)(2,1)} %get-tuple-element.136.refs_4_.refs_1_.refs_11_.refs_5_) | copy-start | bytes 294916
  86.5 10.9 %collective-permute-start.10 = (bf16[28,3,8,128]{3,2,1,0:T(8,128)(2,1)S(1)}, bf16[28,3,8,128]{3,2,1,0:T(8,128)(2,1)S(1)}, u32[]{:S(2)}, u32[]{:S(2)}) collective-permute-start(bf16[28,3,8,128]{3,2,1,0:T(8,128)(2,1)S(1)} %get-tuple-element.150), channel_id=1, source_target_pairs={{0,1},{1,2},{2,3},{3,0},{4,5},{5,6},{6,7},{7,4},{8,9},{9,10},{10,1... | collective-permute-start | bytes 516104 | tf_op jit(solution)/shard_map/ppermute | solution.py:501
  88.3 9.1 %collective-permute-start.9 = (bf16[3,28,8,128]{3,2,1,0:T(8,128)(2,1)S(1)}, bf16[3,28,8,128]{3,2,1,0:T(8,128)(2,1)S(1)}, u32[]{:S(2)}, u32[]{:S(2)}) collective-permute-start(bf16[3,28,8,128]{3,2,1,0:T(8,128)(2,1)S(1)} %get-tuple-element.149), channel_id=1, source_target_pairs={{0,4},{4,8},{8,12},{12,16},{16,20},{20,24},{24,28},{28,0},{1,5},{5... | collective-permute-start | bytes 516104 | tf_op jit(solution)/shard_map/ppermute | solution.py:501
  88.3 9.1 %collective-permute-start.11 = (bf16[3,3,8,128]{3,2,1,0:T(8,128)(2,1)S(1)}, bf16[3,3,8,128]{3,2,1,0:T(8,128)(2,1)S(1)}, u32[]{:S(2)}, u32[]{:S(2)}) collective-permute-start(bf16[3,3,8,128]{3,2,1,0:T(8,128)(2,1)S(1)} %get-tuple-element.151), channel_id=1, source_target_pairs={{0,5},{1,6},{2,7},{3,4},{4,9},{5,10},{6,11},{7,8},{8,13},{9,14},{1... | collective-permute-start | bytes 55304 | tf_op jit(solution)/shard_map/ppermute | solution.py:511
  88.3 9.1 %copy-start = (f32[4,4,392,128]{3,2,1,0:T(8,128)S(1)}, f32[4,4,392,128]{3,2,1,0:T(8,128)}, u32[]{:S(2)}) copy-start(f32[4,4,392,128]{3,2,1,0:T(8,128)} %get-tuple-element.145.refs_4_.refs_1_) | copy-start | bytes 9633796
  88.3 9.1 %copy-start.9 = (bf16[8,28,28,128]{3,0,2,1:T(8,128)(2,1)S(1)}, bf16[8,28,28,128]{3,0,2,1:T(8,128)(2,1)}, u32[]{:S(2)}) copy-start(bf16[8,28,28,128]{3,0,2,1:T(8,128)(2,1)} %param.27) | copy-start | bytes 4816900
  88.3 9.1 %copy-start.10 = (bf16[128,512]{1,0:T(8,128)(2,1)S(1)}, bf16[128,512]{1,0:T(8,128)(2,1)}, u32[]{:S(2)}) copy-start(bf16[128,512]{1,0:T(8,128)(2,1)} %get-tuple-element.147.refs_7_.refs_4_) | copy-start | bytes 393220
  88.3 9.1 %copy-start.11 = (bf16[512,128]{1,0:T(8,128)(2,1)S(1)}, bf16[512,128]{1,0:T(8,128)(2,1)}, u32[]{:S(2)}) copy-start(bf16[512,128]{1,0:T(8,128)(2,1)} %get-tuple-element.148.refs_8_.refs_5_) | copy-start | bytes 393220
  88.4 9.1 %copy-start.14 = (bf16[128,128]{1,0:T(8,128)(2,1)S(1)}, bf16[128,128]{1,0:T(8,128)(2,1)}, u32[]{:S(2)}) copy-start(bf16[128,128]{1,0:T(8,128)(2,1)} %get-tuple-element.146.refs_6_.refs_3_) | copy-start | bytes 98308
  109.9 24.0 %collective-permute-start.12 = (bf16[3,28,8,128]{3,2,1,0:T(8,128)(2,1)S(1)}, bf16[3,28,8,128]{3,2,1,0:T(8,128)(2,1)S(1)}, u32[]{:S(2)}, u32[]{:S(2)}) collective-permute-start(bf16[3,28,8,128]{3,2,1,0:T(8,128)(2,1)S(1)} %get-tuple-element.164), channel_id=1, source_target_pairs={{0,28},{4,0},{8,4},{12,8},{16,12},{20,16},{24,20},{28,24},{1,29},{... | collective-permute-start | bytes 516104 | tf_op jit(solution)/shard_map/ppermute | solution.py:501
  112.5 21.4 %collective-permute-start.13 = (bf16[28,3,8,128]{3,2,1,0:T(8,128)(2,1)S(1)}, bf16[28,3,8,128]{3,2,1,0:T(8,128)(2,1)S(1)}, u32[]{:S(2)}, u32[]{:S(2)}) collective-permute-start(bf16[28,3,8,128]{3,2,1,0:T(8,128)(2,1)S(1)} %get-tuple-element.165), channel_id=1, source_target_pairs={{0,3},{1,0},{2,1},{3,2},{4,7},{5,4},{6,5},{7,6},{8,11},{9,8},{10,9... | collective-permute-start | bytes 516104 | tf_op jit(solution)/shard_map/ppermute | solution.py:501
  115.8 18.2 %collective-permute-start.14 = (bf16[3,3,8,128]{3,2,1,0:T(8,128)(2,1)S(1)}, bf16[3,3,8,128]{3,2,1,0:T(8,128)(2,1)S(1)}, u32[]{:S(2)}, u32[]{:S(2)}) collective-permute-start(bf16[3,3,8,128]{3,2,1,0:T(8,128)(2,1)S(1)} %get-tuple-element.166), channel_id=1, source_target_pairs={{0,31},{1,28},{2,29},{3,30},{4,3},{5,0},{6,1},{7,2},{8,7},{9,4},{1... | collective-permute-start | bytes 55304 | tf_op jit(solution)/shard_map/ppermute | solution.py:511
  130.7 0.7 copy-start.2
  131.4 0.7 copy-start.3
  132.1 0.6 copy-start.5
  132.7 0.6 copy-start.6
  133.3 0.6 copy-start.7
  133.9 11.2 %copy-start.16 = (f32[4,4,392,128]{3,2,1,0:T(8,128)}, f32[4,4,392,128]{3,2,1,0:T(8,128)S(1)}, u32[]{:S(2)}) copy-start(f32[4,4,392,128]{3,2,1,0:T(8,128)S(1)} %get-tuple-element.175.refs_4_) | copy-start | bytes 9633796
  145.1 18.6 %collective-permute-start.15 = (bf16[3,28,8,128]{3,2,1,0:T(8,128)(2,1)S(1)}, bf16[3,28,8,128]{3,2,1,0:T(8,128)(2,1)S(1)}, u32[]{:S(2)}, u32[]{:S(2)}) collective-permute-start(bf16[3,28,8,128]{3,2,1,0:T(8,128)(2,1)S(1)} %get-tuple-element.172), channel_id=1, source_target_pairs={{0,4},{4,8},{8,12},{12,16},{16,20},{20,24},{24,28},{28,0},{1,5},{5... | collective-permute-start | bytes 516104 | tf_op jit(solution)/shard_map/ppermute | solution.py:501
  145.4 18.3 %collective-permute-start.16 = (bf16[28,3,8,128]{3,2,1,0:T(8,128)(2,1)S(1)}, bf16[28,3,8,128]{3,2,1,0:T(8,128)(2,1)S(1)}, u32[]{:S(2)}, u32[]{:S(2)}) collective-permute-start(bf16[28,3,8,128]{3,2,1,0:T(8,128)(2,1)S(1)} %get-tuple-element.173), channel_id=1, source_target_pairs={{0,1},{1,2},{2,3},{3,0},{4,5},{5,6},{6,7},{7,4},{8,9},{9,10},{10,1... | collective-permute-start | bytes 516104 | tf_op jit(solution)/shard_map/ppermute | solution.py:501
  147.2 16.5 %collective-permute-start.17 = (bf16[3,3,8,128]{3,2,1,0:T(8,128)(2,1)S(1)}, bf16[3,3,8,128]{3,2,1,0:T(8,128)(2,1)S(1)}, u32[]{:S(2)}, u32[]{:S(2)}) collective-permute-start(bf16[3,3,8,128]{3,2,1,0:T(8,128)(2,1)S(1)} %get-tuple-element.174), channel_id=1, source_target_pairs={{0,5},{1,6},{2,7},{3,4},{4,9},{5,10},{6,11},{7,8},{8,13},{9,14},{1... | collective-permute-start | bytes 55304 | tf_op jit(solution)/shard_map/ppermute | solution.py:511
  161.1 0.7 copy-start.4
  161.8 0.6 copy-start.8
  162.4 1.2 copy-start.15
  163.7 0.6 copy-start.32
  163.7 0.7 copy-start.30
  163.7 0.7 copy-start.31

commit v4 on v3

--- a/solution.py
+++ b/solution.py
@@ -14,6 +14,7 @@
 EPSILON = 1e-05
 POS = WIN * WIN
 SLOT = 64
+ASKED = 56
 LOG2E = math.log2(math.e)
 SCALE = 1.0 / math.sqrt(HEAD_DIM)
 OFF = -1e30
@@ -21,6 +22,7 @@
 F32 = jnp.float32
 MIB = 1024 * 1024
 VMEM_LIMIT = 56 * MIB
+GROUP = 1
 LIMITS = ((56, 56), (16, 16), (16, 16), (16, 16), 56)
 
 
@@ -92,7 +94,7 @@
 
 
 def segment_max(every):
-    low = lax.broadcasted_iota(jnp.int32, (SLOT, 2 * SLOT), 1) < SLOT
+    low = lax.broadcasted_iota(jnp.int32, (ASKED, 2 * SLOT), 1) < SLOT
     pairs = [s[:, start : start + 2 * SLOT] for s in every for start in (0, 2 * SLOT)]
     first = [jnp.max(jnp.where(low, pair, OFF), 1, keepdims=True) for pair in pairs]
     second = [jnp.max(jnp.where(low, OFF, pair), 1, keepdims=True) for pair in pairs]
@@ -111,8 +113,8 @@
     return pl.program_id(0) == 0
 
 
-def window(ref, image, images):
-    return ref[pl.ds(image, SLOT, stride=images), :]
+def window(ref, image, images, rows=SLOT):
+    return ref[pl.ds(image, rows, stride=images), :]
 
 
 def attention_forward(images, parts, bias, masks, powers_ref, out_ref, share_ref):
@@ -120,7 +122,7 @@
     lanes = head_lanes()
     everything = range(images)
     scores = [
-        mm_nt(window(sc_q, i, images).astype(BF), head_blocks(window(sc_k, i, images)))
+        mm_nt(window(sc_q, i, images, ASKED).astype(BF), head_blocks(window(sc_k, i, images)))
         * (SCALE * LOG2E)
         + bias
         for i in everything
@@ -137,7 +139,7 @@
     depth = lanes.shape[1]
     shares = [1.0 / one[:, depth:] for one in both]
     for i in everything:
-        place = pl.ds(i, SLOT, stride=images)
+        place = pl.ds(i, ASKED, stride=images)
         powers_ref[0, 0, i] = powers[i]
         out_ref[place, :] = both[i][:, :depth] * shares[i]
         share_ref[place, :] = shares[i]
@@ -149,38 +151,39 @@
     lanes = head_lanes()
     depth = lanes.shape[1]
     everything = range(images)
-    upstream = [window(sc_grad, i, images).astype(BF) for i in everything]
+    upstream = [window(sc_grad, i, images, ASKED) for i in everything]
     centred = [
         mm_nt(
-            jnp.concatenate([upstream[i], window(sc_out, i, images).astype(BF)], 1),
+            jnp.concatenate([upstream[i], window(sc_out, i, images, ASKED)], 1).astype(BF),
             jnp.concatenate([head_blocks(window(sc_v, i, images)), lanes], 1),
         )
         for i in everything
     ]
-    powers = [powers_ref[0, 0, i] for i in everything]
-    score_grads = [(powers[i].astype(F32) * centred[i]).astype(BF) for i in everything]
-    total = score_grads[0].astype(F32)
+    powers = [powers_ref[0, 0, i].astype(F32) for i in everything]
+    score_grads = [powers[i] * centred[i] for i in everything]
+    low_grads = [one.astype(BF) for one in score_grads]
+    total = low_grads[0].astype(F32)
     for i in everything[1:]:
-        total = total + score_grads[i].astype(F32)
+        total = total + low_grads[i].astype(F32)
     bias_acc[...] += total
-    d_queries = [mm(score_grads[i], head_blocks(window(sc_k, i, images))) for i in everything]
-    empty = jnp.zeros((SLOT, depth), BF)
+    d_queries = [mm(low_grads[i], head_blocks(window(sc_k, i, images))) for i in everything]
+    empty = jnp.zeros((ASKED, depth), F32)
     d_both = [
         mm_tn(
-            jnp.concatenate([score_grads[i], powers[i]], 0),
+            jnp.concatenate([score_grads[i], powers[i]], 0).astype(BF),
             jnp.concatenate(
                 [
-                    jnp.concatenate([window(sc_q, i, images).astype(BF), empty], 1),
+                    jnp.concatenate([window(sc_q, i, images, ASKED), empty], 1),
                     jnp.concatenate([empty, upstream[i]], 1),
                 ],
                 0,
-            ),
+            ).astype(BF),
         )
         for i in everything
     ]
     for i in everything:
         place = pl.ds(i, SLOT, stride=images)
-        sc_dq[place, :] = d_queries[i] * SCALE
+        sc_dq[pl.ds(i, ASKED, stride=images), :] = d_queries[i] * SCALE
         sc_dk[place, :] = gather_heads(d_both[i][:, :depth]) * SCALE
         sc_dv[place, :] = gather_heads(d_both[i][:, depth:])
 
@@ -202,8 +205,11 @@
     return normed_ref[0, 0].astype(F32), inverse_ref[0, 0].astype(F32)
 
 
-def split_projection(hidden, w_qkv, qkv_bias, parts, count):
-    projected = mm(hidden, w_qkv) + qkv_bias
+def split_projection(hidden, w_qkv, qv_ref, layer, parts, count):
+    query_bias, value_bias = qv_ref[layer, 0:1], qv_ref[layer, 1:2]
+    projected = mm(hidden, w_qkv) + jnp.concatenate(
+        [query_bias, jnp.zeros_like(query_bias), value_bias], 1
+    )
     projected = projected.astype(BF).astype(F32)
     depth = hidden.shape[1]
     for n, ref in enumerate(parts):
@@ -217,8 +223,8 @@
 
 
 def kernel_first_layer(
-    images, place, rims, x_ref, w_qkv, w_proj, w_fc1, w_fc2, vecs, qkv_bias, fc1_bias, bias,
-    stream_out, hidden_out, out_out, share_out, powers_out, act_out, slope_out,
+    images, place, rims, x_ref, w_qkv, w_proj, w_fc1, w_fc2, gains, shifts, outs, qkv_bias, fc1_bias, bias,
+    stream_out, hidden_out, out_out, share_out, powers_out, expanded_out,
     n_one, r_one, n_two, r_two, n_next, r_next,
     sc_q, sc_k, sc_v, sc_out, sc_share,
 ):
@@ -227,25 +233,24 @@
     stream = tokens_of(x_ref)
     normed, inverse = norm_parts(stream)
     put_norm((n_one, r_one), normed, inverse)
-    hidden = (normed * vecs[0:1] + vecs[1:2]).astype(BF)
-    split_projection(hidden, w_qkv[...], qkv_bias[...], (sc_q, sc_k, sc_v), count)
+    hidden = (normed * gains[0, 0:1] + shifts[0, 0:1]).astype(BF)
+    split_projection(hidden, w_qkv[...], qkv_bias, 0, (sc_q, sc_k, sc_v), count)
     attention_forward(images, (sc_q, sc_k, sc_v), bias[...], None, powers_out, sc_out, sc_share)
     attended = sc_out[:count, :].astype(BF)
     out_out[0, 0] = attended
     share_out[0, 0] = sc_share[:count, :]
-    middle = stream + (mm(attended, w_proj[...]) + vecs[4:5])
+    middle = stream + (mm(attended, w_proj[...]) + outs[0, 0:1])
     normed, inverse = norm_parts(middle)
     put_norm((n_two, r_two), normed, inverse)
-    inner = (normed * vecs[2:3] + vecs[3:4]).astype(BF)
-    activated, slope = gelu_parts(mm(inner, w_fc1[...]) + fc1_bias[...])
-    activated = activated.astype(BF)
-    act_out[0, 0] = activated
-    slope_out[0, 0] = slope.astype(BF)
-    stream = middle + mm(activated, w_fc2[...]) + vecs[5:6]
+    inner = (normed * gains[0, 1:2] + shifts[0, 1:2]).astype(BF)
+    expanded = mm(inner, w_fc1[...]) + fc1_bias[0:1]
+    expanded_out[0, 0] = expanded.astype(BF)
+    activated = gelu_parts(expanded)[0].astype(BF)
+    stream = middle + mm(activated, w_fc2[...]) + outs[0, 1:2]
     stream_out[0, 0] = stream
     normed, inverse = norm_parts(stream)
     put_norm((n_next, r_next), normed, inverse)
-    block = put_tokens(hidden_out, normed * vecs[6:7] + vecs[7:8])
+    block = put_tokens(hidden_out, normed * gains[1, 0:1] + shifts[1, 0:1])
     if rims is not None:
         put_rims(block, rims, place, "first")
 
@@ -261,7 +266,7 @@
     count = POS * images
     zero_tails(first_of_grid(), count, sc_q, sc_k, sc_v)
     hidden = ahead_window(hidden_ref, halo, held, place).astype(BF)
-    split_projection(hidden, w_qkv[...], qkv_bias[...], (sc_q, sc_k, sc_v), count)
+    split_projection(hidden, w_qkv[...], qkv_bias, 1, (sc_q, sc_k, sc_v), count)
     attention_forward(images, (sc_q, sc_k, sc_v), bias[...], masks, powers_out, sc_out, sc_share)
     share_out[0, 0] = sc_share[:count, :]
     block = put_tokens(out_out, sc_out[:count, :])
@@ -385,17 +390,17 @@
 def kernel_middle(images, place, rims, out_ref, *refs):
     halo, refs = (None, refs) if rims is None else (refs[:3], refs[3:])
     (
-        stream_ref, cot_ref, w_proj, w_fc1, w_fc2, vecs, fc1_bias,
+        stream_ref, cot_ref, w_proj, w_fc1, w_fc2, gains, shifts, outs, fc1_bias,
         mixed_out, grad_out, low_out, g_proj, g_fc1, g_fc2, sums, fc1_sums, held,
     ) = refs
     stream = stream_ref[0, 0]
     attended = behind_window(out_ref, halo, held, place).astype(BF)
-    middle = stream + (mm(attended, w_proj[...]) + vecs[4:5])
+    middle = stream + (mm(attended, w_proj[...]) + outs[1, 0:1])
     normed, inverse = norm_parts(middle)
-    inner = (normed * vecs[2:3] + vecs[3:4]).astype(BF)
-    activated, slope = gelu_parts(mm(inner, w_fc1[...]) + fc1_bias[...])
+    inner = (normed * gains[1, 1:2] + shifts[1, 1:2]).astype(BF)
+    activated, slope = gelu_parts(mm(inner, w_fc1[...]) + fc1_bias[1:2])
     activated = activated.astype(BF)
-    put_tokens(mixed_out, middle + mm(activated, w_fc2[...]) + vecs[5:6])
+    put_tokens(mixed_out, middle + mm(activated, w_fc2[...]) + outs[1, 1:2])
     gradient = tokens_of(cot_ref)
     out_low = gradient.astype(BF)
     expanded_low, inner_grad = feed_forward_backward(
@@ -404,7 +409,7 @@
     g_fc2[...] += mm_tn(out_low, activated)
     g_fc1[...] += mm_tn(inner, expanded_low)
     fc1_sums[...] += fold_rows(expanded_low.astype(F32))
-    norm_term = norm_backward(inner_grad, normed, inverse, vecs[2:3])
+    norm_term = norm_backward(inner_grad, normed, inverse, gains[1, 1:2])
     updated = gradient + norm_term
     grad_out[0, 0] = updated
     branch_low = updated.astype(BF)
@@ -436,7 +441,7 @@
     count = POS * images
     zero_tails(first_of_grid(), count, sc_q, sc_k, sc_v, sc_out, sc_grad)
     hidden = ahead_window(hidden_ref, halo, held, place).astype(BF)
-    split_projection(hidden, w_qkv[...], qkv_bias[...], (sc_q, sc_k, sc_v), count)
+    split_projection(hidden, w_qkv[...], qkv_bias, 1, (sc_q, sc_k, sc_v), count)
     gradient = ahead_window(low_ref, low_halo, held, place)
     put_upstream(count, sc_grad, sc_out, gradient, tokens_of(out_ref), share_ref[0, 0])
     grads = (sc_dq, sc_dk, sc_dv)
@@ -450,8 +455,8 @@
 
 def kernel_first_backward(
     images, place, rims, hidden_grad_ref, rim_rows, rim_cols, corner, grad_ref,
-    n_one, r_one, n_two, r_two, n_next, r_next, act_ref, slope_ref, att_ref, share_ref, powers_ref,
-    w_qkv, w_proj, w_fc1, w_fc2, vecs, qkv_bias,
+    n_one, r_one, n_two, r_two, n_next, r_next, expanded_ref, att_ref, share_ref, powers_ref,
+    w_qkv, w_proj, w_fc1, w_fc2, gains, shifts, qkv_bias,
     tokens_grad_out, g_qkv, g_proj, g_fc1, g_fc2, sums, fc1_sums, qv_sums, bias_acc,
     held, sc_q, sc_k, sc_v, sc_out, sc_grad, sc_dq, sc_dk, sc_dv,
 ):
@@ -459,20 +464,21 @@
     zero_tails(first_of_grid(), count, sc_q, sc_k, sc_v, sc_out, sc_grad)
     upstream = behind_window(hidden_grad_ref, (rim_rows, rim_cols, corner), held, place)
     normed_one, inverse_one = get_norm((n_one, r_one))
-    hidden = (normed_one * vecs[0:1] + vecs[1:2]).astype(BF)
-    split_projection(hidden, w_qkv[...], qkv_bias[...], (sc_q, sc_k, sc_v), count)
+    hidden = (normed_one * gains[0, 0:1] + shifts[0, 0:1]).astype(BF)
+    split_projection(hidden, w_qkv[...], qkv_bias, 0, (sc_q, sc_k, sc_v), count)
     normed, inverse = get_norm((n_next, r_next))
-    gradient = grad_ref[0, 0] + norm_backward(upstream, normed, inverse, vecs[6:7])
+    gradient = grad_ref[0, 0] + norm_backward(upstream, normed, inverse, gains[1, 0:1])
     sums[4] += fold_rows(upstream * normed)
     sums[5] += fold_rows(upstream)
     out_low = gradient.astype(BF)
     normed, inverse = get_norm((n_two, r_two))
-    inner = (normed * vecs[2:3] + vecs[3:4]).astype(BF)
-    activated = act_ref[0, 0]
+    inner = (normed * gains[0, 1:2] + shifts[0, 1:2]).astype(BF)
+    activated, slope = gelu_parts(expanded_ref[0, 0].astype(F32))
+    activated = activated.astype(BF)
     expanded_low, inner_grad = feed_forward_backward(
-        out_low, inner, activated, slope_ref[0, 0].astype(F32), w_fc1[...], w_fc2[...]
-    )
-    updated = gradient + norm_backward(inner_grad, normed, inverse, vecs[2:3])
+        out_low, inner, activated, slope, w_fc1[...], w_fc2[...]
+    )
+    updated = gradient + norm_backward(inner_grad, normed, inverse, gains[0, 1:2])
     branch_low = updated.astype(BF)
     low = mm_nt(branch_low, w_proj[...]).astype(BF).astype(F32)
     attended = att_ref[0, 0]
@@ -490,7 +496,7 @@
     joined = joined_gradients(count, grads, qv_sums)
     g_qkv[...] += mm_tn(hidden, joined)
     upstream = mm_nt(joined, w_qkv[...])
-    term = norm_backward(upstream, normed_one, inverse_one, vecs[0:1])
+    term = norm_backward(upstream, normed_one, inverse_one, gains[0, 0:1])
     put_tokens(tokens_grad_out, updated + term)
     sums[6] += fold_rows(upstream * normed_one)
     sums[7] += fold_rows(upstream)
@@ -763,40 +769,24 @@
         precision=lax.Precision.HIGHEST,
     ).reshape(POS, POS, 2, HEADS)
     padded = jnp.pad(
-        jnp.pad(tables.transpose(2, 0, 3, 1), ((0, 0), (0, SLOT - POS), (0, 0), (0, 0))),
+        jnp.pad(tables.transpose(2, 0, 3, 1), ((0, 0), (0, ASKED - POS), (0, 0), (0, 0))),
         ((0, 0), (0, 0), (0, 0), (0, SLOT - POS)),
         constant_values=OFF,
     )
-    biases = padded.reshape(2, SLOT, HEADS * SLOT)
+    biases = padded.reshape(2, ASKED, HEADS * SLOT)
     ids = region.reshape(images, rows, WIN, cols, WIN).transpose(1, 3, 0, 2, 4)
     ids = ids.reshape(rows, cols, images, POS)
     apart = (ids[..., :, None] != ids[..., None, :]).astype(BF)
-    apart = jnp.pad(apart, [(0, 0)] * 3 + [(0, SLOT - POS)] * 2)
+    apart = jnp.pad(apart, [(0, 0)] * 3 + [(0, ASKED - POS), (0, SLOT - POS)])
     masks = jnp.concatenate([apart, apart], -1)
 
     first_weights, later, masks = lax.optimization_barrier((first_weights, slices[1], masks))
     weights = [first_weights, whole_weights(place, later, depth, wide)]
 
-    zeros = jnp.zeros((depth,), F32)
-    qkv_biases = [
-        jnp.concatenate([qv_bias[l, 0], zeros, qv_bias[l, 1]])[None] for l in range(2)
-    ]
-
-    def vectors(layer):
-        after = norm_gain[1, 0], norm_bias[1, 0]
-        return jnp.stack(
-            [
-                norm_gain[layer, 0], norm_bias[layer, 0], norm_gain[layer, 1], norm_bias[layer, 1],
-                out_bias[layer, 0], out_bias[layer, 1], *after,
-            ]
-        )
-
-    vecs = [vectors(0), vectors(1)]
-
     field_shape = (height, width, images, depth)
     field = ((WIN, WIN, images, depth), lambda r, c: (r, c, 0, 0))
-    probs_spec = ((1, 1, images, SLOT, HEADS * SLOT), lambda r, c: (r, c, 0, 0, 0))
-    mask_spec = ((1, 1, images, SLOT, 2 * SLOT), lambda r, c: (r, c, 0, 0, 0))
+    probs_spec = ((1, 1, images, ASKED, HEADS * SLOT), lambda r, c: (r, c, 0, 0, 0))
+    mask_spec = ((1, 1, images, ASKED, 2 * SLOT), lambda r, c: (r, c, 0, 0, 0))
 
     def flat(columns):
         return (1, 1, count, columns), lambda r, c: (r, c, 0, 0)
@@ -804,20 +794,21 @@
     def flat_type(columns, dtype):
         return jax.ShapeDtypeStruct((rows, cols, count, columns), dtype)
 
-    probs_type = jax.ShapeDtypeStruct((rows, cols, images, SLOT, HEADS * SLOT), BF)
+    probs_type = jax.ShapeDtypeStruct((rows, cols, images, ASKED, HEADS * SLOT), BF)
     rim_types = [
         jax.ShapeDtypeStruct((SHIFT, width, images, depth), BF),
         jax.ShapeDtypeStruct((height, SHIFT, images, depth), BF),
         jax.ShapeDtypeStruct((SHIFT, SHIFT, images, depth), BF),
     ]
 
-    def run(kernel, part, inputs, outputs, slots, limit, earlier=None, held=False):
-        steps, order = window_order(part, rows, cols)
+    def run(kernel, part, inputs, outputs, slots, limit, earlier=None, held=False, group=1):
+        steps, order = window_order(part, rows, cols // group)
 
         def spec_of(spec, shape):
             if spec is None:
                 return pl.BlockSpec(tuple(shape), lambda i: (0,) * len(shape))
             block, index = spec
+            block = (block[0], block[1] * group, *block[2:])
             return pl.BlockSpec(block, lambda i: index(*order(i)))
 
         with_rims = part != "all" and part[1]
@@ -841,7 +832,7 @@
         out_specs += [spec_of(None, t.shape) for t in rim_types] if with_rims else []
 
         def body(*refs):
-            place = (*order(pl.program_id(0)), rows, cols)
+            row, col = order(pl.program_id(0))
             outs = refs[n_all : n_all + n_out]
             rims = refs[n_all + n_out : n_all + n_out + 3] if with_rims else None
             rest = refs[n_all + len(types) :]
@@ -855,7 +846,22 @@
                         else:
                             outs[n][...] = refs[n_in + n][...]
 
-            kernel(images, place, rims, *refs[:n_in], *outs, *rest)
+            def view(ref, spec, k):
+                if spec is None or group == 1:
+                    return ref
+                size = spec[0][1]
+                return ref.at[:, pl.ds(k * size, size)]
+
+            each = len(rest) // group
+            for k in range(group):
+                kernel(
+                    images,
+                    (row, col * group + k, rows, cols),
+                    rims,
+                    *[view(ref, spec, k) for ref, (_, spec) in zip(refs[:n_in], inputs)],
+                    *[view(ref, spec, k) for ref, (_, spec) in zip(outs, outputs)],
+                    *rest[k * each : (k + 1) * each],
+                )
 
         scratch = [pltpu.VMEM((WIN, WIN, images, depth), BF)] if held else []
         scratch += [pltpu.VMEM((SLOT * images, depth), F32)] * slots
@@ -865,7 +871,7 @@
             in_specs=in_specs,
             out_specs=out_specs,
             out_shape=types,
-            scratch_shapes=scratch,
+            scratch_shapes=scratch * group,
             input_output_aliases=aliases,
             compiler_params=pltpu.CompilerParams(vmem_limit_bytes=limit * MIB),
             cost_estimate=pl.CostEstimate(
@@ -892,12 +898,13 @@
 
     qkv0, proj0, fc10, fc20 = weights[0]
     qkv1, proj1, fc11, fc21 = weights[1]
-    (stream1, hidden1, att0, share0, powers0, act0, slope0, *norms0), halo = run_both(
+    (stream1, hidden1, att0, share0, powers0, expanded0, *norms0), halo = run_both(
         kernel_first_layer,
         "first",
         [
-            (x, field), (qkv0, None), (proj0, None), (fc10, None), (fc20, None), (vecs[0], None),
-            (qkv_biases[0], None), (fc1_bias[0:1], None), (biases[0], None),
+            (x, field), (qkv0, None), (proj0, None), (fc10, None), (fc20, None), (norm_gain, None),
+            (norm_bias, None), (out_bias, None), (qv_bias, None), (fc1_bias, None),
+            (biases[0], None),
         ],
         [],
         [
@@ -907,7 +914,6 @@
             (flat_type(depth, F32), flat(depth)),
             (probs_type, probs_spec),
             (flat_type(wide, BF), flat(wide)),
-            (flat_type(wide, BF), flat(wide)),
             *[(flat_type(depth, BF), flat(depth))] * 6,
         ],
         5,
@@ -918,7 +924,7 @@
         kernel_shifted_forward,
         "last",
         [
-            (hidden1, None), (qkv1, None), (qkv_biases[1], None), (biases[1], None),
+            (hidden1, None), (qkv1, None), (qv_bias, None), (biases[1], None),
             (masks, mask_spec),
         ],
         [halo],
@@ -937,7 +943,8 @@
         "first",
         [
             (att1, None), (stream1, flat(depth)), (cot, field), (proj1, None),
-            (fc11, None), (fc21, None), (vecs[1], None), (fc1_bias[1:2], None),
+            (fc11, None), (fc21, None), (norm_gain, None), (norm_bias, None),
+            (out_bias, None), (fc1_bias, None),
         ],
         [out_halo],
         [
@@ -958,12 +965,12 @@
         [
             (hidden1, None), (low1, None), (att1, field), (share1, flat(depth)),
             (powers1, probs_spec),
-            (qkv1, None), (qkv_biases[1], None),
+            (qkv1, None), (qv_bias, None),
         ],
         [halo, low_halo],
         [
             (jax.ShapeDtypeStruct(field_shape, BF), field),
-            total(depth, 3 * depth), total(2, 8, depth), total(SLOT, HEADS * SLOT),
+            total(depth, 3 * depth), total(2, 8, depth), total(ASKED, HEADS * SLOT),
         ],
         8,
         1,
@@ -977,22 +984,23 @@
         "all",
         [
             (hidden_grad1, None), *[(a, None) for a in grad_halo], (grad1, flat(depth)),
-            *[(a, flat(depth)) for a in norms0], (act0, flat(wide)), (slope0, flat(wide)),
+            *[(a, flat(depth)) for a in norms0], (expanded0, flat(wide)),
             (att0, flat(depth)), (share0, flat(depth)), (powers0, probs_spec),
-            (qkv0, None), (proj0, None), (fc10, None), (fc20, None), (vecs[0], None),
-            (qkv_biases[0], None),
+            (qkv0, None), (proj0, None), (fc10, None), (fc20, None), (norm_gain, None),
+            (norm_bias, None), (qv_bias, None),
         ],
         [
             (jax.ShapeDtypeStruct(field_shape, F32), field),
             total(depth, 3 * depth), total(depth, depth), total(depth, wide), total(depth, wide),
-            total(8, 8, depth), total(8, wide), total(2, 8, depth), total(SLOT, HEADS * SLOT),
+            total(8, 8, depth), total(8, wide), total(2, 8, depth), total(ASKED, HEADS * SLOT),
         ],
         8,
         LIMITS[4],
         held=True,
-    )
-
-    bias_sums = jnp.stack([bias_sums0, bias_sums1]).reshape(2, SLOT, HEADS, SLOT)
+        group=GROUP,
+    )
+
+    bias_sums = jnp.stack([bias_sums0, bias_sums1]).reshape(2, ASKED, HEADS, SLOT)
     bias_sums = bias_sums[:, :POS, :, :POS].transpose(0, 2, 1, 3).reshape(2 * HEADS, POS * POS)
     table = jnp.dot(bias_sums, selector, precision=lax.Precision.HIGHEST)
     table = jnp.pad(table, ((0, 0), (0, -table_size % 128)))

time: 256 us -> 252 us (0.984)
    unnamed x80 -> x84, local copies, waits for them, and re-layouts: 11.4 us -> 11.6 us
  transfers between devices with their start and end apart: 18 -> 18, of which waited for: 0 -> 1; matrix products, arithmetic and copies ran while one was open for 4% -> 3% of each run, Pallas kernels for 32% -> 31%
where the time goes in v4:
time: 252 us
  Pallas kernels  160 us (63%)
  blocking collectives  39.3 us (16%)
  starting transfers between devices  25.7 us (10%)
  local copies, waits for them, and re-layouts  20.1 us (8%)
  matrix products  2.85 us (1%)
    pallas_call x9, Pallas kernels, run(): pl.pallas_call(body, grid=(steps,), in_specs=in_specs, out_specs=out_spec...  150 us
    all_to_all x1, blocking collectives, sum_everywhere(): packets = lax.all_to_all(packets, ('seq', 'wt'), 0, 0, tiled=True)  28.2 us
    ppermute x14, starting transfers between devices, shift_by(): lax.ppermute(array, axis, [(i, (i + by) % count) for i in range(count)])  23.7 us
    unnamed x84, local copies, waits for them, and re-layouts  11.6 us
    all_gather x1, blocking collectives, sum_everywhere(): mine = lax.all_gather(mine, 'seq', axis=0)  11.1 us
    pallas_call x3, Pallas kernels, whole_kernel(): pl.pallas_call(body, in_specs=[full] * len(inputs), out_specs=[full] * le...  6.2 us
  transfers between devices with their start and end apart: 18, of which 1 were waited for; matrix products, arithmetic and copies ran while one was open for 3% of the time, Pallas kernels for 31%

profile of v4, /device:TPU:0, one launch (start us, length us, event | category | flops | bytes accessed | tf_op | source)
XLA Modules:
  0.0 251.6 jit_solution(10353594540330995361)
XLA Ops:
  0.6 0.8 slice_bitcast_fusion.2
  1.4 0.8 slice_bitcast_fusion
  2.2 0.7 constant_dynamic-update-slice_fusion.14
  3.0 0.8 constant_dynamic-update-slice_fusion.9
  3.9 5.1 %collective-permute-start = (bf16[384,128]{1,0:T(8,128)(2,1)S(1)}, bf16[384,128]{1,0:T(8,128)(2,1)S(1)}, u32[]{:S(2)}, u32[]{:S(2)}) collective-permute-start(bf16[384,128]{1,0:T(8,128)(2,1)S(1)} %get-tuple-element.213.refs_1_), channel_id=1, source_target_pairs={{0,3},{1,0},{2,1},{3,2},{4,7},{5,4},{6,5},{7,6},{8,11},{9,8},{10,9... | collective-permute-start | bytes 294920 | tf_op jit(solution)/shard_map/ppermute | solution.py:507
  9.0 1.0 collective-permute-start.2
  10.0 1.1 reshape.72
  11.1 0.3 copy.46
  11.4 0.2 ne.15
  11.6 1.3 broadcast_compare_fusion
  13.1 2.0 fusion.6
  15.2 0.7 squeeze.38.refs_10_
  15.9 0.1 squeeze.39.refs_6_.refs_3_
  16.0 0.5 pad.17
  16.5 1.0 add_convert_fusion.refs_7_.refs_4_
  17.6 0.1 collective-permute-done.1.refs_3_
  17.7 0.5 copy-done.27
  18.2 0.1 copy-done.28
  18.4 1.8 shard_map.229
  20.2 2.7 %collective-permute-start.3 = (bf16[384,128]{1,0:T(8,128)(2,1)S(1)}, bf16[384,128]{1,0:T(8,128)(2,1)S(1)}, u32[]{:S(2)}, u32[]{:S(2)}) collective-permute-start(bf16[384,128]{1,0:T(8,128)(2,1)S(1)} %get-tuple-element.132.refs_1_), channel_id=1, source_target_pairs={{0,3},{1,0},{2,1},{3,2},{4,7},{5,4},{6,5},{7,6},{8,11},{9,8},{10,9... | collective-permute-start | bytes 294920 | tf_op jit(solution)/shard_map/ppermute | solution.py:507
  22.9 1.1 collective-permute-start.4
  24.1 0.4 collective-permute-start.5
  24.5 17.2 %shard_map.230 = (f32[4,4,392,128]{3,2,1,0:T(8,128)}, bf16[28,28,8,128]{3,2,1,0:T(8,128)(2,1)}, bf16[4,4,392,128]{3,2,1,0:T(8,128)(2,1)}, f32[4,4,392,128]{3,2,1...) custom-call(bf16[28,28,8,128]{3,2,1,0:T(8,128)(2,1)} %bitcast.57, ...), custom_call_target="tpu_custom_call" | custom-call | flops 7000000000 | bytes 10000000 | tf_op jit(solution)/shard_map/pallas_call | solution.py:868
  41.7 0.5 collective-permute-start.6
  42.2 3.1 %collective-permute-start.7 = (bf16[28,3,8,128]{3,2,1,0:T(8,128)(2,1)}, bf16[28,3,8,128]{3,2,1,0:T(8,128)(2,1)S(1)}, u32[]{:S(2)}, u32[]{:S(2)}) collective-permute-start(bf16[28,3,8,128]{3,2,1,0:T(8,128)(2,1)} %get-tuple-element.136), channel_id=1, source_target_pairs={{0,3},{1,0},{2,1},{3,2},{4,7},{5,4},{6,5},{7,6},{8,11},{9,8},{10,9... | collective-permute-start | bytes 516104 | tf_op jit(solution)/shard_map/ppermute | solution.py:507
  45.3 1.9 collective-permute-start.8
  47.2 21.0 %shard_map.231 = (f32[4,4,392,128]{3,2,1,0:T(8,128)}, bf16[28,28,8,128]{3,2,1,0:T(8,128)(2,1)}, bf16[4,4,392,128]{3,2,1,0:T(8,128)(2,1)}, f32[4,4,392,128]{3,2,1...) custom-call(bf16[28,28,8,128]{3,2,1,0:T(8,128)(2,1)} %bitcast.58, ...), custom_call_target="tpu_custom_call", output_to_operand_aliasing={{0}: (11, {}), {1}: (12, {}), {2}: (13, {}), {3}: (14, {}),... | custom-call | flops 8999999488 | bytes 10000000 | tf_op jit(solution)/shard_map/pallas_call | solution.py:868
  68.2 0.6 copy-done.25
  68.8 0.6 copy-done.26
  69.5 1.8 shard_map.232
  71.4 0.9 copy-done.10
  72.2 1.4 copy-done.19
  73.7 7.0 %shard_map.233 = (bf16[28,28,8,128]{3,2,1,0:T(8,128)(2,1)S(1)}, f32[4,4,392,128]{3,2,1,0:T(8,128)S(1)}, bf16[4,4,8,56,256]{4,3,2,1,0:T(8,128)(2,1)S(1)}, bf16[3,...) custom-call(bf16[28,28,8,128]{3,2,1,0:T(8,128)(2,1)S(1)} %copy-done.19, ...), custom_call_target="tpu_custom_call" | custom-call | flops 7000000000 | bytes 10000000 | tf_op jit(solution)/shard_map/pallas_call | solution.py:868
  80.7 1.8 collective-permute-start.10
  82.6 8.8 %shard_map.234 = (bf16[28,28,8,128]{3,2,1,0:T(8,128)(2,1)S(1)}, f32[4,4,392,128]{3,2,1,0:T(8,128)S(1)}, bf16[4,4,8,56,256]{4,3,2,1,0:T(8,128)(2,1)S(1)}) custom-call(bf16[28,28,8,128]{3,2,1,0:T(8,128)(2,1)S(1)} %copy-done.19, bf16[128,384]{1,0:T(8,128)(2,1)S(1)} %copy-done.10, ...), custom_call_target="tpu_custom_call", output_to_operand_aliasing={{0}: (5, {}), {1}: (6, {}), {2}: (7, {})} | custom-call | flops 8999999488 | bytes 10000000 | tf_op jit(solution)/shard_map/pallas_call | solution.py:868
  91.4 12.4 %shard_map.235 = (bf16[28,28,8,128]{3,2,1,0:T(8,128)(2,1)}, f32[4,4,392,128]{3,2,1,0:T(8,128)S(1)}, bf16[28,28,8,128]{3,2,1,0:T(8,128)(2,1)S(1)}, f32[128,128]{1...) custom-call(bf16[28,28,8,128]{3,2,1,0:T(8,128)(2,1)S(1)} %get-tuple-, ...), custom_call_target="tpu_custom_call" | custom-call | flops 7000000000 | bytes 10000000 | tf_op jit(solution)/shard_map/pallas_call | solution.py:868
  103.9 2.6 %collective-permute-start.12 = (bf16[3,28,8,128]{3,2,1,0:T(8,128)(2,1)S(1)}, bf16[3,28,8,128]{3,2,1,0:T(8,128)(2,1)S(1)}, u32[]{:S(2)}, u32[]{:S(2)}) collective-permute-start(bf16[3,28,8,128]{3,2,1,0:T(8,128)(2,1)S(1)} %get-tuple-element.161), channel_id=1, source_target_pairs={{0,28},{4,0},{8,4},{12,8},{16,12},{20,16},{24,20},{28,24},{1,29},{... | collective-permute-start | bytes 516104 | tf_op jit(solution)/shard_map/ppermute | solution.py:507
  106.5 3.2 %collective-permute-start.13 = (bf16[28,3,8,128]{3,2,1,0:T(8,128)(2,1)S(1)}, bf16[28,3,8,128]{3,2,1,0:T(8,128)(2,1)S(1)}, u32[]{:S(2)}, u32[]{:S(2)}) collective-permute-start(bf16[28,3,8,128]{3,2,1,0:T(8,128)(2,1)S(1)} %get-tuple-element.162), channel_id=1, source_target_pairs={{0,3},{1,0},{2,1},{3,2},{4,7},{5,4},{6,5},{7,6},{8,11},{9,8},{10,9... | collective-permute-start | bytes 516104 | tf_op jit(solution)/shard_map/ppermute | solution.py:507
  109.8 0.1 collective-permute-start.14
  109.9 14.7 %shard_map.236 = (bf16[28,28,8,128]{3,2,1,0:T(8,128)(2,1)}, f32[4,4,392,128]{3,2,1,0:T(8,128)S(1)}, bf16[28,28,8,128]{3,2,1,0:T(8,128)(2,1)S(1)}, f32[128,128]{1...) custom-call(bf16[28,28,8,128]{3,2,1,0:T(8,128)(2,1)S(1)} %get-tuple-, ...), custom_call_target="tpu_custom_call", output_to_operand_aliasing={{0}: (10, {}), {1}: (11, {}), {2}: (12, {})} | custom-call | flops 8999999488 | bytes 10000000 | tf_op jit(solution)/shard_map/pallas_call | solution.py:868
  124.6 0.7 copy-done
  125.4 0.7 copy-done.1
  126.1 0.6 copy-done.3
  126.7 0.6 copy-done.4
  127.3 0.6 copy-done.5
  128.0 11.1 %shard_map.237 = (bf16[28,28,8,128]{3,2,1,0:T(8,128)(2,1)S(1)}, f32[128,384]{1,0:T(8,128)S(1)}, f32[2,8,128]{2,1,0:T(8,128)S(1)}, f32[56,256]{1,0:T(8,128)S(1)},...) custom-call(bf16[28,28,8,128]{3,2,1,0:T(8,128)(2,1)S(1)} %copy-done.19,, ...), custom_call_target="tpu_custom_call" | custom-call | flops 7000000000 | bytes 10000000 | tf_op jit(solution)/shard_map/pallas_call | solution.py:868
  139.0 0.3 collective-permute-start.15
  139.4 1.7 collective-permute-start.16
  141.1 13.9 %shard_map.238 = (bf16[28,28,8,128]{3,2,1,0:T(8,128)(2,1)S(1)}, f32[128,384]{1,0:T(8,128)S(1)}, f32[2,8,128]{2,1,0:T(8,128)S(1)}, f32[56,256]{1,0:T(8,128)S(1)}) custom-call(bf16[28,28,8,128]{3,2,1,0:T(8,128)(2,1)S(1)} %copy-done.19, bf16[28,28,8,128]{3,2,1,0:T(8,128)(2,1)S(1)} %get-tuple-element.158.refs_1_, ...), custom_call_target="tpu_custom_call", output_to_operand_aliasing={{0}: (7, {})} | custom-call | flops 8999999488 | bytes 10000000 | tf_op jit(solution)/shard_map/pallas_call | solution.py:868
  155.1 0.7 copy-done.2
  155.7 0.6 copy-done.6
  156.3 1.1 copy-done.21
  157.6 0.5 copy-done.34
  158.4 43.8 %shard_map.239 = (f32[28,28,8,128]{3,2,1,0:T(8,128)}, f32[128,384]{1,0:T(8,128)}, f32[128,128]{1,0:T(8,128)}, f32[128,512]{1,0:T(8,128)}, f32[128,512]{1,0:T(8,1...) custom-call(bf16[28,28,8,128]{3,2,1,0:T(8,128)(2,1)} %copy-done.21, ...), custom_call_target="tpu_custom_call" | custom-call | flops 16000000000 | bytes 10000000 | tf_op jit(solution)/shard_map/pallas_call | solution.py:868
  202.2 0.9 stack.9
  203.2 0.1 reshape.73
  203.3 0.9 fusion.3
  204.2 0.6 pad.20.refs_14_
  204.8 2.6 %shard_map.240 = bf16[32,112,128]{2,1,0:T(8,128)(2,1)} custom-call(f32[128,384]{1,0:T(8,128)} %get-tuple-element.184.refs_0_, f32[128,128]{1,0:T(8,128)} %get-tuple-element.185.refs_1_, f32[128,512]{1,0:T(8,128)} %get-tuple-element.186.refs_2_, f32[128,512]{1,0:T(8,128)} %get-tuple-element.187.refs_3_, f32[128,384]{1,0:T(8,128)} %copy-done.2, ...), custom_call_target="tpu_custom_call" | custom-call | tf_op jit(solution)/shard_map/pallas_call | solution.py:700
  207.4 28.2 %all_to_all.5.packet_ref = bf16[32,112,128]{2,1,0:T(8,128)(2,1)} all-to-all(bf16[32,112,128]{2,1,0:T(8,128)(2,1)} %shard_map.240), channel_id=1, replica_groups=mesh['seq'=8,'wt'=4] {'seq','wt'}, dimensions={0} | all-to-all | bytes 1835008 | tf_op jit(solution)/shard_map/all_to_all | solution.py:732
  235.6 1.9 shard_map.241
  237.5 11.1 %all-gather = bf16[896,128]{1,0:T(8,128)(2,1)} all-gather(bf16[112,128]{1,0:T(8,128)(2,1)} %shard_map.241), channel_id=2, replica_groups=mesh['seq'=8,'wt'=4] {'seq'}, dimensions={0}, use_global_device_ids=true | all-gather | bytes 258048 | tf_op jit(solution)/shard_map/all_gather | solution.py:734
  248.6 1.7 shard_map.242
  250.3 1.3 reshape.74
  (99 shorter events, 0.9 us)
Async XLA Ops:
  3.8 9.1 %copy-start.23 = (bf16[384,128]{1,0:T(8,128)(2,1)}, bf16[384,128]{1,0:T(8,128)(2,1)S(1)}, u32[]{:S(2)}) copy-start(bf16[384,128]{1,0:T(8,128)(2,1)S(1)} %get-tuple-element.213.refs_1_) | copy-start | bytes 294916
  3.9 20.2 %copy-start.22 = (bf16[384,128]{1,0:T(8,128)(2,1)}, bf16[384,128]{1,0:T(8,128)(2,1)S(1)}, u32[]{:S(2)}) copy-start(bf16[384,128]{1,0:T(8,128)(2,1)S(1)} %get-tuple-element.132.refs_1_) | copy-start | bytes 294916
  3.9 9.0 %copy-start.31 = (f32[2,169,4]{1,2,0:T(4,128)S(1)}, f32[2,169,4]{1,2,0:T(4,128)}, u32[]{:S(2)}) copy-start(f32[2,169,4]{1,2,0:T(4,128)} %param.21) | copy-start | bytes 16228
  3.9 13.7 %collective-permute-start = (bf16[384,128]{1,0:T(8,128)(2,1)S(1)}, bf16[384,128]{1,0:T(8,128)(2,1)S(1)}, u32[]{:S(2)}, u32[]{:S(2)}) collective-permute-start(bf16[384,128]{1,0:T(8,128)(2,1)S(1)} %get-tuple-element.213.refs_1_), channel_id=1, source_target_pairs={{0,3},{1,0},{2,1},{3,2},{4,7},{5,4},{6,5},{7,6},{8,11},{9,8},{10,9... | collective-permute-start | bytes 294920 | tf_op jit(solution)/shard_map/ppermute | solution.py:507
  9.0 8.7 %collective-permute-start.1 = (bf16[384,128]{1,0:T(8,128)(2,1)S(1)}, bf16[384,128]{1,0:T(8,128)(2,1)S(1)}, u32[]{:S(2)}, u32[]{:S(2)}) collective-permute-start(bf16[384,128]{1,0:T(8,128)(2,1)S(1)} %get-tuple-element.213.refs_1_), channel_id=1, source_target_pairs={{0,2},{1,3},{2,0},{3,1},{4,6},{5,7},{6,4},{7,5},{8,10},{9,11},{10,... | collective-permute-start | bytes 294920 | tf_op jit(solution)/shard_map/ppermute | solution.py:507
  9.0 8.7 %collective-permute-start.2 = (bf16[384,128]{1,0:T(8,128)(2,1)S(1)}, bf16[384,128]{1,0:T(8,128)(2,1)S(1)}, u32[]{:S(2)}, u32[]{:S(2)}) collective-permute-start(bf16[384,128]{1,0:T(8,128)(2,1)S(1)} %get-tuple-element.213.refs_1_), channel_id=1, source_target_pairs={{0,1},{1,2},{2,3},{3,0},{4,5},{5,6},{6,7},{7,4},{8,9},{9,10},{10,1... | collective-permute-start | bytes 294920 | tf_op jit(solution)/shard_map/ppermute | solution.py:507
  10.0 3.0 %copy-start.30 = (s32[49,49]{1,0:T(8,128)S(1)}, s32[49,49]{1,0:T(8,128)}, u32[]{:S(2)}) copy-start(s32[49,49]{1,0:T(8,128)} %param.16) | copy-start | bytes 28816
  17.6 0.6 copy-start.27
  17.7 0.6 copy-start.28
  17.7 0.7 copy-start.29
  20.2 25.1 %collective-permute-start.3 = (bf16[384,128]{1,0:T(8,128)(2,1)S(1)}, bf16[384,128]{1,0:T(8,128)(2,1)S(1)}, u32[]{:S(2)}, u32[]{:S(2)}) collective-permute-start(bf16[384,128]{1,0:T(8,128)(2,1)S(1)} %get-tuple-element.132.refs_1_), channel_id=1, source_target_pairs={{0,3},{1,0},{2,1},{3,2},{4,7},{5,4},{6,5},{7,6},{8,11},{9,8},{10,9... | collective-permute-start | bytes 294920 | tf_op jit(solution)/shard_map/ppermute | solution.py:507
  22.9 45.2 %collective-permute-start.4 = (bf16[384,128]{1,0:T(8,128)(2,1)S(1)}, bf16[384,128]{1,0:T(8,128)(2,1)S(1)}, u32[]{:S(2)}, u32[]{:S(2)}) collective-permute-start(bf16[384,128]{1,0:T(8,128)(2,1)S(1)} %get-tuple-element.132.refs_1_), channel_id=1, source_target_pairs={{0,2},{1,3},{2,0},{3,1},{4,6},{5,7},{6,4},{7,5},{8,10},{9,11},{10,... | collective-permute-start | bytes 294920 | tf_op jit(solution)/shard_map/ppermute | solution.py:507
  24.1 44.1 %collective-permute-start.5 = (bf16[384,128]{1,0:T(8,128)(2,1)S(1)}, bf16[384,128]{1,0:T(8,128)(2,1)S(1)}, u32[]{:S(2)}, u32[]{:S(2)}) collective-permute-start(bf16[384,128]{1,0:T(8,128)(2,1)S(1)} %get-tuple-element.132.refs_1_), channel_id=1, source_target_pairs={{0,1},{1,2},{2,3},{3,0},{4,5},{5,6},{6,7},{7,4},{8,9},{9,10},{10,1... | collective-permute-start | bytes 294920 | tf_op jit(solution)/shard_map/ppermute | solution.py:507
  41.7 29.6 %collective-permute-start.6 = (bf16[3,28,8,128]{3,2,1,0:T(8,128)(2,1)}, bf16[3,28,8,128]{3,2,1,0:T(8,128)(2,1)S(1)}, u32[]{:S(2)}, u32[]{:S(2)}) collective-permute-start(bf16[3,28,8,128]{3,2,1,0:T(8,128)(2,1)} %get-tuple-element.135), channel_id=1, source_target_pairs={{0,28},{4,0},{8,4},{12,8},{16,12},{20,16},{24,20},{28,24},{1,29},{... | collective-permute-start | bytes 516104 | tf_op jit(solution)/shard_map/ppermute | solution.py:507
  42.2 29.1 %collective-permute-start.7 = (bf16[28,3,8,128]{3,2,1,0:T(8,128)(2,1)}, bf16[28,3,8,128]{3,2,1,0:T(8,128)(2,1)S(1)}, u32[]{:S(2)}, u32[]{:S(2)}) collective-permute-start(bf16[28,3,8,128]{3,2,1,0:T(8,128)(2,1)} %get-tuple-element.136), channel_id=1, source_target_pairs={{0,3},{1,0},{2,1},{3,2},{4,7},{5,4},{6,5},{7,6},{8,11},{9,8},{10,9... | collective-permute-start | bytes 516104 | tf_op jit(solution)/shard_map/ppermute | solution.py:507
  45.3 22.8 %copy-start.24 = (bf16[384,128]{1,0:T(8,128)(2,1)}, bf16[384,128]{1,0:T(8,128)(2,1)S(1)}, u32[]{:S(2)}) copy-start(bf16[384,128]{1,0:T(8,128)(2,1)S(1)} %collective-permute-done.3.refs_2_) | copy-start | bytes 294916
  45.3 26.0 %collective-permute-start.8 = (bf16[3,3,8,128]{3,2,1,0:T(8,128)(2,1)}, bf16[3,3,8,128]{3,2,1,0:T(8,128)(2,1)S(1)}, u32[]{:S(2)}, u32[]{:S(2)}) collective-permute-start(bf16[3,3,8,128]{3,2,1,0:T(8,128)(2,1)} %get-tuple-element.137), channel_id=1, source_target_pairs={{0,31},{1,28},{2,29},{3,30},{4,3},{5,0},{6,1},{7,2},{8,7},{9,4},{1... | collective-permute-start | bytes 55304 | tf_op jit(solution)/shard_map/ppermute | solution.py:517
  47.2 24.2 %copy-start.17 = (f32[2,2,128]{2,1,0:T(2,128)S(1)}, f32[2,2,128]{2,1,0:T(2,128)}, u32[]{:S(2)}) copy-start(f32[2,2,128]{2,1,0:T(2,128)} %refs_21_.1) | copy-start | bytes 6148
  68.2 0.6 copy-start.25
  68.8 0.6 copy-start.26
  71.3 0.9 copy-start.10
  72.2 1.4 copy-start.19
  80.7 10.6 %collective-permute-start.10 = (bf16[28,3,8,128]{3,2,1,0:T(8,128)(2,1)S(1)}, bf16[28,3,8,128]{3,2,1,0:T(8,128)(2,1)S(1)}, u32[]{:S(2)}, u32[]{:S(2)}) collective-permute-start(bf16[28,3,8,128]{3,2,1,0:T(8,128)(2,1)S(1)} %get-tuple-element.147), channel_id=1, source_target_pairs={{0,1},{1,2},{2,3},{3,0},{4,5},{5,6},{6,7},{7,4},{8,9},{9,10},{10,1... | collective-permute-start | bytes 516104 | tf_op jit(solution)/shard_map/ppermute | solution.py:507
  82.5 8.9 %collective-permute-start.9 = (bf16[3,28,8,128]{3,2,1,0:T(8,128)(2,1)S(1)}, bf16[3,28,8,128]{3,2,1,0:T(8,128)(2,1)S(1)}, u32[]{:S(2)}, u32[]{:S(2)}) collective-permute-start(bf16[3,28,8,128]{3,2,1,0:T(8,128)(2,1)S(1)} %get-tuple-element.146), channel_id=1, source_target_pairs={{0,4},{4,8},{8,12},{12,16},{16,20},{20,24},{24,28},{28,0},{1,5},{5... | collective-permute-start | bytes 516104 | tf_op jit(solution)/shard_map/ppermute | solution.py:507
  82.5 8.9 %collective-permute-start.11 = (bf16[3,3,8,128]{3,2,1,0:T(8,128)(2,1)S(1)}, bf16[3,3,8,128]{3,2,1,0:T(8,128)(2,1)S(1)}, u32[]{:S(2)}, u32[]{:S(2)}) collective-permute-start(bf16[3,3,8,128]{3,2,1,0:T(8,128)(2,1)S(1)} %get-tuple-element.148), channel_id=1, source_target_pairs={{0,5},{1,6},{2,7},{3,4},{4,9},{5,10},{6,11},{7,8},{8,13},{9,14},{1... | collective-permute-start | bytes 55304 | tf_op jit(solution)/shard_map/ppermute | solution.py:517
  82.5 8.9 %copy-start.7 = (bf16[8,28,28,128]{3,0,2,1:T(8,128)(2,1)S(1)}, bf16[8,28,28,128]{3,0,2,1:T(8,128)(2,1)}, u32[]{:S(2)}) copy-start(bf16[8,28,28,128]{3,0,2,1:T(8,128)(2,1)} %param.27) | copy-start | bytes 4816900
  82.5 8.9 %copy-start.8 = (bf16[128,512]{1,0:T(8,128)(2,1)S(1)}, bf16[128,512]{1,0:T(8,128)(2,1)}, u32[]{:S(2)}) copy-start(bf16[128,512]{1,0:T(8,128)(2,1)} %get-tuple-element.144.refs_7_.refs_4_) | copy-start | bytes 393220
  82.5 8.9 %copy-start.9 = (bf16[512,128]{1,0:T(8,128)(2,1)S(1)}, bf16[512,128]{1,0:T(8,128)(2,1)}, u32[]{:S(2)}) copy-start(bf16[512,128]{1,0:T(8,128)(2,1)} %get-tuple-element.145.refs_8_.refs_5_) | copy-start | bytes 393220
  82.5 8.9 %copy-start.12 = (bf16[128,128]{1,0:T(8,128)(2,1)S(1)}, bf16[128,128]{1,0:T(8,128)(2,1)}, u32[]{:S(2)}) copy-start(bf16[128,128]{1,0:T(8,128)(2,1)} %get-tuple-element.143.refs_6_.refs_3_) | copy-start | bytes 98308
  82.5 8.9 %copy-start.13 = (f32[2,512]{1,0:T(2,128)S(1)}, f32[2,512]{1,0:T(2,128)}, u32[]{:S(2)}) copy-start(f32[2,512]{1,0:T(2,128)} %refs_9_.7) | copy-start | bytes 12292
  82.5 8.9 %copy-start.14 = (f32[2,2,128]{2,1,0:T(2,128)S(1)}, f32[2,2,128]{2,1,0:T(2,128)}, u32[]{:S(2)}) copy-start(f32[2,2,128]{2,1,0:T(2,128)} %refs_8_.5) | copy-start | bytes 6148
  82.5 8.9 %copy-start.15 = (f32[2,2,128]{2,1,0:T(2,128)S(1)}, f32[2,2,128]{2,1,0:T(2,128)}, u32[]{:S(2)}) copy-start(f32[2,2,128]{2,1,0:T(2,128)} %refs_19_.1) | copy-start | bytes 6148
  82.5 8.9 %copy-start.16 = (f32[2,2,128]{2,1,0:T(2,128)S(1)}, f32[2,2,128]{2,1,0:T(2,128)}, u32[]{:S(2)}) copy-start(f32[2,2,128]{2,1,0:T(2,128)} %refs_20_.1) | copy-start | bytes 6148
  82.6 8.9 %copy-start.18 = (f32[4,4,392,128]{3,2,1,0:T(8,128)S(1)}, f32[4,4,392,128]{3,2,1,0:T(8,128)}, u32[]{:S(2)}) copy-start(f32[4,4,392,128]{3,2,1,0:T(8,128)} %get-tuple-element.142.refs_4_.refs_1_) | copy-start | bytes 9633796
  103.9 24.0 %collective-permute-start.12 = (bf16[3,28,8,128]{3,2,1,0:T(8,128)(2,1)S(1)}, bf16[3,28,8,128]{3,2,1,0:T(8,128)(2,1)S(1)}, u32[]{:S(2)}, u32[]{:S(2)}) collective-permute-start(bf16[3,28,8,128]{3,2,1,0:T(8,128)(2,1)S(1)} %get-tuple-element.161), channel_id=1, source_target_pairs={{0,28},{4,0},{8,4},{12,8},{16,12},{20,16},{24,20},{28,24},{1,29},{... | collective-permute-start | bytes 516104 | tf_op jit(solution)/shard_map/ppermute | solution.py:507
  106.5 21.4 %collective-permute-start.13 = (bf16[28,3,8,128]{3,2,1,0:T(8,128)(2,1)S(1)}, bf16[28,3,8,128]{3,2,1,0:T(8,128)(2,1)S(1)}, u32[]{:S(2)}, u32[]{:S(2)}) collective-permute-start(bf16[28,3,8,128]{3,2,1,0:T(8,128)(2,1)S(1)} %get-tuple-element.162), channel_id=1, source_target_pairs={{0,3},{1,0},{2,1},{3,2},{4,7},{5,4},{6,5},{7,6},{8,11},{9,8},{10,9... | collective-permute-start | bytes 516104 | tf_op jit(solution)/shard_map/ppermute | solution.py:507
  109.8 18.2 %collective-permute-start.14 = (bf16[3,3,8,128]{3,2,1,0:T(8,128)(2,1)S(1)}, bf16[3,3,8,128]{3,2,1,0:T(8,128)(2,1)S(1)}, u32[]{:S(2)}, u32[]{:S(2)}) collective-permute-start(bf16[3,3,8,128]{3,2,1,0:T(8,128)(2,1)S(1)} %get-tuple-element.163), channel_id=1, source_target_pairs={{0,31},{1,28},{2,29},{3,30},{4,3},{5,0},{6,1},{7,2},{8,7},{9,4},{1... | collective-permute-start | bytes 55304 | tf_op jit(solution)/shard_map/ppermute | solution.py:517
  109.9 18.0 %copy-start.11 = (bf16[128,384]{1,0:T(8,128)(2,1)S(1)}, bf16[128,384]{1,0:T(8,128)(2,1)}, u32[]{:S(2)}) copy-start(bf16[128,384]{1,0:T(8,128)(2,1)} %get-tuple-element.133.refs_4_.refs_1_.refs_11_.refs_5_) | copy-start | bytes 294916
  124.6 0.7 copy-start
  125.4 0.7 copy-start.1
  126.1 0.6 copy-start.3
  126.7 0.6 copy-start.4
  127.3 0.6 copy-start.5
  127.9 11.1 %copy-start.20 = (f32[4,4,392,128]{3,2,1,0:T(8,128)}, f32[4,4,392,128]{3,2,1,0:T(8,128)S(1)}, u32[]{:S(2)}) copy-start(f32[4,4,392,128]{3,2,1,0:T(8,128)S(1)} %get-tuple-element.172.refs_4_) | copy-start | bytes 9633796
  139.0 18.6 %collective-permute-start.15 = (bf16[3,28,8,128]{3,2,1,0:T(8,128)(2,1)S(1)}, bf16[3,28,8,128]{3,2,1,0:T(8,128)(2,1)S(1)}, u32[]{:S(2)}, u32[]{:S(2)}) collective-permute-start(bf16[3,28,8,128]{3,2,1,0:T(8,128)(2,1)S(1)} %get-tuple-element.169), channel_id=1, source_target_pairs={{0,4},{4,8},{8,12},{12,16},{16,20},{20,24},{24,28},{28,0},{1,5},{5... | collective-permute-start | bytes 516104 | tf_op jit(solution)/shard_map/ppermute | solution.py:507
  139.4 18.2 %collective-permute-start.16 = (bf16[28,3,8,128]{3,2,1,0:T(8,128)(2,1)S(1)}, bf16[28,3,8,128]{3,2,1,0:T(8,128)(2,1)S(1)}, u32[]{:S(2)}, u32[]{:S(2)}) collective-permute-start(bf16[28,3,8,128]{3,2,1,0:T(8,128)(2,1)S(1)} %get-tuple-element.170), channel_id=1, source_target_pairs={{0,1},{1,2},{2,3},{3,0},{4,5},{5,6},{6,7},{7,4},{8,9},{9,10},{10,1... | collective-permute-start | bytes 516104 | tf_op jit(solution)/shard_map/ppermute | solution.py:507
  141.1 16.5 %collective-permute-start.17 = (bf16[3,3,8,128]{3,2,1,0:T(8,128)(2,1)S(1)}, bf16[3,3,8,128]{3,2,1,0:T(8,128)(2,1)S(1)}, u32[]{:S(2)}, u32[]{:S(2)}) collective-permute-start(bf16[3,3,8,128]{3,2,1,0:T(8,128)(2,1)S(1)} %get-tuple-element.171), channel_id=1, source_target_pairs={{0,5},{1,6},{2,7},{3,4},{4,9},{5,10},{6,11},{7,8},{8,13},{9,14},{1... | collective-permute-start | bytes 55304 | tf_op jit(solution)/shard_map/ppermute | solution.py:517
  155.0 0.7 copy-start.2
  155.7 0.6 copy-start.6
  156.3 1.1 copy-start.21
  157.6 0.6 copy-start.34
  157.6 0.7 copy-start.32
  157.6 0.7 copy-start.33

commit v5 on v4

--- a/solution.py
+++ b/solution.py
@@ -22,8 +22,7 @@
 F32 = jnp.float32
 MIB = 1024 * 1024
 VMEM_LIMIT = 56 * MIB
-GROUP = 1
-LIMITS = ((56, 56), (16, 16), (16, 16), (16, 16), 56)
+LIMITS = ((60, 60), (16, 16), (16, 16), (16, 16), 60)
 
 
 def mm(left, right):
@@ -465,7 +464,6 @@
     upstream = behind_window(hidden_grad_ref, (rim_rows, rim_cols, corner), held, place)
     normed_one, inverse_one = get_norm((n_one, r_one))
     hidden = (normed_one * gains[0, 0:1] + shifts[0, 0:1]).astype(BF)
-    split_projection(hidden, w_qkv[...], qkv_bias, 0, (sc_q, sc_k, sc_v), count)
     normed, inverse = get_norm((n_next, r_next))
     gradient = grad_ref[0, 0] + norm_backward(upstream, normed, inverse, gains[1, 0:1])
     sums[4] += fold_rows(upstream * normed)
@@ -482,6 +480,7 @@
     branch_low = updated.astype(BF)
     low = mm_nt(branch_low, w_proj[...]).astype(BF).astype(F32)
     attended = att_ref[0, 0]
+    split_projection(hidden, w_qkv[...], qkv_bias, 0, (sc_q, sc_k, sc_v), count)
     put_upstream(count, sc_grad, sc_out, low, attended.astype(F32), share_ref[0, 0])
     grads = (sc_dq, sc_dk, sc_dv)
     attention_backward(images, (sc_q, sc_k, sc_v), sc_grad, sc_out, powers_ref, grads, bias_acc)
@@ -618,7 +617,14 @@
     for ref in (fc1_0, fc1_1):
         line = jnp.sum(ref[...], 0, keepdims=True)
         rows += [line[:, i : i + 128] for i in range(0, line.shape[1], 128)]
-    return rows + [table[:, i : i + 128] for i in range(0, table.shape[1], 128)]
+    size = table.shape[1]
+    for i in range(0, size, 128):
+        piece = table[:, i : min(i + 128, size)]
+        gap = 128 - piece.shape[1]
+        if gap:
+            piece = jnp.concatenate([piece, jnp.zeros((piece.shape[0], gap), F32)], 1)
+        rows.append(piece)
+    return rows
 
 
 def kernel_pack(seqs, parts, each, *refs):
@@ -690,9 +696,11 @@
         for i in range(0, fc1_bias.shape[1], 128):
             fc1_bias[layer : layer + 1, i : i + 128] = lines[at : at + 1, :]
             at += 1
-    for i in range(0, table.shape[1], 128):
-        table[:, i : i + 128] = lines[at : at + table.shape[0], :]
-        at += table.shape[0]
+    for i in range(0, table.shape[2], 128):
+        wide = min(128, table.shape[2] - i)
+        for layer in range(2):
+            table[layer, :, i : i + wide] = lines[at : at + HEADS, :wide]
+            at += HEADS
 
 
 def whole_kernel(body, inputs, outputs, scratch=()):
@@ -713,7 +721,7 @@
     held = 2 * (4 * depth + 2 * wide) // parts
     each = held // seqs
     size = -(-each // 16) * 16 + 2 * SMALL_ROWS
-    count = 16 + 2 * (wide // 128) + 2 * HEADS * (smalls[-1].shape[1] // 128)
+    count = 16 + 2 * (wide // 128) + 2 * HEADS * -(-smalls[-1].shape[1] // 128)
     per = -(-count // seqs)
     tail = (seqs * per + SMALL_ROWS, 128)
 
@@ -737,7 +745,8 @@
         [mine],
         [
             ((2, 2, depth), F32), ((2, 2, depth), F32), ((2, rows, 3 * depth), F32),
-            ((2, 2, depth), F32), (smalls[-1].shape, F32), ((2, rows, depth), F32),
+            ((2, 2, depth), F32), ((2, HEADS, smalls[-1].shape[1]), F32),
+            ((2, rows, depth), F32),
             ((2, 2, depth), F32), ((2, rows, wide), F32), ((2, wide), F32),
             ((2, wide // parts, depth), F32),
         ],
@@ -780,8 +789,7 @@
     apart = jnp.pad(apart, [(0, 0)] * 3 + [(0, ASKED - POS), (0, SLOT - POS)])
     masks = jnp.concatenate([apart, apart], -1)
 
-    first_weights, later, masks = lax.optimization_barrier((first_weights, slices[1], masks))
-    weights = [first_weights, whole_weights(place, later, depth, wide)]
+    first_weights, masks = lax.optimization_barrier((first_weights, masks))
 
     field_shape = (height, width, images, depth)
     field = ((WIN, WIN, images, depth), lambda r, c: (r, c, 0, 0))
@@ -880,25 +888,31 @@
         )(*ins)
         return results[:n_out], results[n_out:]
 
-    def run_both(kernel, edge, inputs, halos, outputs, slots, by, limits, held=False):
+    def run_both(kernel, edge, inputs, halos, outputs, slots, by, limits, held=False, beside=None):
         lead = len(halos)
         rim_inputs = [(a, None) for halo in halos for a in halo]
         inputs_a = inputs[:lead] + rim_inputs + inputs[lead:]
         first, rims = run(
             kernel, (edge, True), inputs_a, outputs, slots, limits[0], held=held
         )
+        if beside is not None:
+            rims, beside = lax.optimization_barrier((rims, beside))
+            beside = whole_weights(place, beside, depth, wide)
         rims = send_rims(rims, by)
         second, _ = run(
             kernel, (edge, False), inputs, outputs, slots, limits[1], first, held=held
         )
-        return second, rims
+        return (second, rims) if beside is None else (second, rims, beside)
 
     def total(*shape):
         return (jax.ShapeDtypeStruct(shape, F32), None)
 
-    qkv0, proj0, fc10, fc20 = weights[0]
-    qkv1, proj1, fc11, fc21 = weights[1]
-    (stream1, hidden1, att0, share0, powers0, expanded0, *norms0), halo = run_both(
+    qkv0, proj0, fc10, fc20 = first_weights
+    (
+        (stream1, hidden1, att0, share0, powers0, expanded0, *norms0),
+        halo,
+        (qkv1, proj1, fc11, fc21),
+    ) = run_both(
         kernel_first_layer,
         "first",
         [
@@ -919,6 +933,7 @@
         5,
         -1,
         LIMITS[0],
+        beside=slices[1],
     )
     (att1, share1, powers1), out_halo = run_both(
         kernel_shifted_forward,
@@ -997,20 +1012,18 @@
         8,
         LIMITS[4],
         held=True,
-        group=GROUP,
     )
 
     bias_sums = jnp.stack([bias_sums0, bias_sums1]).reshape(2, ASKED, HEADS, SLOT)
     bias_sums = bias_sums[:, :POS, :, :POS].transpose(0, 2, 1, 3).reshape(2 * HEADS, POS * POS)
     table = jnp.dot(bias_sums, selector, precision=lax.Precision.HIGHEST)
-    table = jnp.pad(table, ((0, 0), (0, -table_size % 128)))
     gains, shifts, d_qkv, d_qv, d_table, d_proj, d_out, d_fc1, d_fc1_bias, d_fc2 = sum_everywhere(
         [g_qkv0, g_proj0, g_fc10, g_fc20, g_qkv1, g_proj1, g_fc11, g_fc21],
         [sums0, sums1, qv_sums0, qv_sums1, fc1_sums0, fc1_sums1, table],
         depth,
         wide,
     )
-    d_table = d_table[:, :table_size].reshape(2, HEADS, table_size).transpose(0, 2, 1)
+    d_table = d_table.transpose(0, 2, 1)
     return (
         mixed.transpose(2, 0, 1, 3), tokens_grad.transpose(2, 0, 1, 3), gains, shifts, d_qkv,
         d_qv, d_table, d_proj, d_out, d_fc1, d_fc1_bias, d_fc2,

time: 252 us -> 251 us (level)
  local copies, waits for them, and re-layouts: 20.1 us -> 17.3 us
    ppermute x14, starting transfers between devices: 23.7 us -> 18.8 us  [shift_by(): lax.ppermute(array, axis, [(i, (i + by) % count) for i in range(count)])]
    ppermute x4, starting transfers between devices: 2 us -> 5.93 us  [shift_both(): return lax.ppermute(array, ('seq', 'wt'), pairs)]
  transfers between devices with their start and end apart: 18 -> 18, of which waited for: 1 -> 1; matrix products, arithmetic and copies ran while one was open for 3% -> 3% of each run, Pallas kernels for 31% -> 24%
where the time goes in v5:
time: 251 us; the launch traced here: 250 us
  Pallas kernels  160 us (64%)
  blocking collectives  40 us (16%)
  starting transfers between devices  24.8 us (10%)
  local copies, waits for them, and re-layouts  17.3 us (7%)
  matrix products  4.2 us (2%)
  other arithmetic  3.09 us (1%)
    pallas_call x9, Pallas kernels, run(): pl.pallas_call(body, grid=(steps,), in_specs=in_specs, out_specs=out_spec...  150 us
    all_to_all x1, blocking collectives, sum_everywhere(): packets = lax.all_to_all(packets, ('seq', 'wt'), 0, 0, tiled=True)  28.9 us
    ppermute x14, starting transfers between devices, shift_by(): lax.ppermute(array, axis, [(i, (i + by) % count) for i in range(count)])  18.8 us
    unnamed x84, local copies, waits for them, and re-layouts  11.5 us
    all_gather x1, blocking collectives, sum_everywhere(): mine = lax.all_gather(mine, 'seq', axis=0)  11.1 us
    pallas_call x3, Pallas kernels, whole_kernel(): pl.pallas_call(body, in_specs=[full] * len(inputs), out_specs=[full] * le...  6.21 us
    ppermute x4, starting transfers between devices, shift_both(): return lax.ppermute(array, ('seq', 'wt'), pairs)  5.93 us
  transfers between devices with their start and end apart: 18, of which 1 were waited for; matrix products, arithmetic and copies ran while one was open for 3% of the time, Pallas kernels for 24%

profile of v5, /device:TPU:0, one launch (start us, length us, event | category | flops | bytes accessed | tf_op | source)
XLA Modules:
  0.0 250.4 jit_solution(15108659716165903952)
XLA Ops:
  0.7 0.8 slice_bitcast_fusion.2
  1.4 0.8 slice_bitcast_fusion
  2.3 0.7 constant_dynamic-update-slice_fusion.14
  3.1 0.8 constant_dynamic-update-slice_fusion.9
  3.9 3.1 %collective-permute-start.2 = (bf16[384,128]{1,0:T(8,128)(2,1)S(1)}, bf16[384,128]{1,0:T(8,128)(2,1)S(1)}, u32[]{:S(2)}, u32[]{:S(2)}) collective-permute-start(bf16[384,128]{1,0:T(8,128)(2,1)S(1)} %get-tuple-element.219.refs_1_), channel_id=1, source_target_pairs={{0,1},{1,2},{2,3},{3,0},{4,5},{5,6},{6,7},{7,4},{8,9},{9,10},{10,1... | collective-permute-start | bytes 294920 | tf_op jit(solution)/shard_map/ppermute | solution.py:506
  7.0 2.6 %collective-permute-start.1 = (bf16[384,128]{1,0:T(8,128)(2,1)S(1)}, bf16[384,128]{1,0:T(8,128)(2,1)S(1)}, u32[]{:S(2)}, u32[]{:S(2)}) collective-permute-start(bf16[384,128]{1,0:T(8,128)(2,1)S(1)} %get-tuple-element.219.refs_1_), channel_id=1, source_target_pairs={{0,2},{1,3},{2,0},{3,1},{4,6},{5,7},{6,4},{7,5},{8,10},{9,11},{10,... | collective-permute-start | bytes 294920 | tf_op jit(solution)/shard_map/ppermute | solution.py:506
  9.6 1.3 collective-permute-start
  10.9 0.7 multiply_bitcast_fusion
  11.6 2.7 %fusion.6 = f32[2,49,4,49]{3,2,0,1:T(4,128)S(1)} fusion(f32[2,4,169,1]{2,1,0,3:T(4,128)S(1)} %reshape.73, s32[49,49]{1,0:T(8,128)} %param.16), kind=kOutput, calls=%fused_computation.9 | convolution fusion | flops 39359592 | bytes 91844 | tf_op jit(solution)/shard_map/dot_general | solution.py:775
  14.5 0.7 squeeze.34.refs_10_
  15.2 0.2 reshape.69
  15.5 0.3 copy.46
  15.8 0.2 ne.15
  15.9 1.3 broadcast_compare_fusion
  17.2 0.5 pad.13
  17.7 1.0 add_convert_fusion.refs_7_.refs_4_
  18.8 0.6 copy-done.28
  19.5 1.8 shard_map.229
  21.3 17.2 %shard_map.230 = (f32[4,4,392,128]{3,2,1,0:T(8,128)}, bf16[28,28,8,128]{3,2,1,0:T(8,128)(2,1)}, bf16[4,4,392,128]{3,2,1,0:T(8,128)(2,1)}, f32[4,4,392,128]{3,2,1...) custom-call(bf16[28,28,8,128]{3,2,1,0:T(8,128)(2,1)} %bitcast.54, ...), custom_call_target="tpu_custom_call" | custom-call | flops 7000000000 | bytes 10000000 | tf_op jit(solution)/shard_map/pallas_call | solution.py:876
  38.5 0.7 collective-permute-start.5
  39.2 0.1 eq.41
  39.3 0.1 squeeze.39.refs_6_.refs_3_
  39.5 0.9 collective-permute-start.4
  40.4 2.3 collective-permute-start.3
  42.7 1.0 collective-permute-start.8
  43.8 2.3 collective-permute-start.6
  46.1 0.1 collective-permute-done.5.refs_4_
  46.2 2.2 collective-permute-start.7
  48.3 21.0 %shard_map.231 = (f32[4,4,392,128]{3,2,1,0:T(8,128)}, bf16[28,28,8,128]{3,2,1,0:T(8,128)(2,1)}, bf16[4,4,392,128]{3,2,1,0:T(8,128)(2,1)}, f32[4,4,392,128]{3,2,1...) custom-call(bf16[28,28,8,128]{3,2,1,0:T(8,128)(2,1)} %bitcast.55, ...), custom_call_target="tpu_custom_call", output_to_operand_aliasing={{0}: (11, {}), {1}: (12, {}), {2}: (13, {}), {3}: (14, {}),... | custom-call | flops 8999999488 | bytes 10000000 | tf_op jit(solution)/shard_map/pallas_call | solution.py:876
  69.4 0.6 copy-done.26
  70.0 0.6 copy-done.27
  70.6 1.8 shard_map.232
  72.5 0.9 copy-done.10
  73.4 1.4 copy-done.19
  74.8 7.0 %shard_map.233 = (bf16[28,28,8,128]{3,2,1,0:T(8,128)(2,1)S(1)}, f32[4,4,392,128]{3,2,1,0:T(8,128)S(1)}, bf16[4,4,8,56,256]{4,3,2,1,0:T(8,128)(2,1)S(1)}, bf16[3,...) custom-call(bf16[28,28,8,128]{3,2,1,0:T(8,128)(2,1)S(1)} %copy-done.19, ...), custom_call_target="tpu_custom_call" | custom-call | flops 7000000000 | bytes 10000000 | tf_op jit(solution)/shard_map/pallas_call | solution.py:876
  81.9 0.9 collective-permute-start.9
  82.9 8.8 %shard_map.234 = (bf16[28,28,8,128]{3,2,1,0:T(8,128)(2,1)S(1)}, f32[4,4,392,128]{3,2,1,0:T(8,128)S(1)}, bf16[4,4,8,56,256]{4,3,2,1,0:T(8,128)(2,1)S(1)}) custom-call(bf16[28,28,8,128]{3,2,1,0:T(8,128)(2,1)S(1)} %copy-done.19, bf16[128,384]{1,0:T(8,128)(2,1)S(1)} %copy-done.10, ...), custom_call_target="tpu_custom_call", output_to_operand_aliasing={{0}: (5, {}), {1}: (6, {}), {2}: (7, {})} | custom-call | flops 8999999488 | bytes 10000000 | tf_op jit(solution)/shard_map/pallas_call | solution.py:876
  91.8 12.4 %shard_map.235 = (bf16[28,28,8,128]{3,2,1,0:T(8,128)(2,1)}, f32[4,4,392,128]{3,2,1,0:T(8,128)S(1)}, bf16[28,28,8,128]{3,2,1,0:T(8,128)(2,1)S(1)}, f32[128,128]{1...) custom-call(bf16[28,28,8,128]{3,2,1,0:T(8,128)(2,1)S(1)} %get-tuple-, ...), custom_call_target="tpu_custom_call" | custom-call | flops 7000000000 | bytes 10000000 | tf_op jit(solution)/shard_map/pallas_call | solution.py:876
  104.2 4.8 %collective-permute-start.14 = (bf16[3,3,8,128]{3,2,1,0:T(8,128)(2,1)S(1)}, bf16[3,3,8,128]{3,2,1,0:T(8,128)(2,1)S(1)}, u32[]{:S(2)}, u32[]{:S(2)}) collective-permute-start(bf16[3,3,8,128]{3,2,1,0:T(8,128)(2,1)S(1)} %get-tuple-element.169), channel_id=1, source_target_pairs={{0,31},{1,28},{2,29},{3,30},{4,3},{5,0},{6,1},{7,2},{8,7},{9,4},{1... | collective-permute-start | bytes 55304 | tf_op jit(solution)/shard_map/ppermute | solution.py:516
  109.0 0.3 collective-permute-start.12
  109.3 2.0 collective-permute-start.13
  111.4 14.7 %shard_map.236 = (bf16[28,28,8,128]{3,2,1,0:T(8,128)(2,1)}, f32[4,4,392,128]{3,2,1,0:T(8,128)S(1)}, bf16[28,28,8,128]{3,2,1,0:T(8,128)(2,1)S(1)}, f32[128,128]{1...) custom-call(bf16[28,28,8,128]{3,2,1,0:T(8,128)(2,1)S(1)} %get-tuple-, ...), custom_call_target="tpu_custom_call", output_to_operand_aliasing={{0}: (10, {}), {1}: (11, {}), {2}: (12, {})} | custom-call | flops 8999999488 | bytes 10000000 | tf_op jit(solution)/shard_map/pallas_call | solution.py:876
  126.1 0.7 copy-done
  126.8 0.7 copy-done.1
  127.5 0.6 copy-done.3
  128.2 0.6 copy-done.4
  128.8 0.6 copy-done.5
  129.4 11.1 %shard_map.237 = (bf16[28,28,8,128]{3,2,1,0:T(8,128)(2,1)S(1)}, f32[128,384]{1,0:T(8,128)S(1)}, f32[2,8,128]{2,1,0:T(8,128)S(1)}, f32[56,256]{1,0:T(8,128)S(1)},...) custom-call(bf16[28,28,8,128]{3,2,1,0:T(8,128)(2,1)S(1)} %copy-done.19,, ...), custom_call_target="tpu_custom_call" | custom-call | flops 7000000000 | bytes 10000000 | tf_op jit(solution)/shard_map/pallas_call | solution.py:876
  140.7 14.0 %shard_map.238 = (bf16[28,28,8,128]{3,2,1,0:T(8,128)(2,1)S(1)}, f32[128,384]{1,0:T(8,128)S(1)}, f32[2,8,128]{2,1,0:T(8,128)S(1)}, f32[56,256]{1,0:T(8,128)S(1)}) custom-call(bf16[28,28,8,128]{3,2,1,0:T(8,128)(2,1)S(1)} %copy-done.19, bf16[28,28,8,128]{3,2,1,0:T(8,128)(2,1)S(1)} %get-tuple-element.164.refs_1_, ...), custom_call_target="tpu_custom_call", output_to_operand_aliasing={{0}: (7, {})} | custom-call | flops 8999999488 | bytes 10000000 | tf_op jit(solution)/shard_map/pallas_call | solution.py:876
  154.7 0.7 copy-done.2
  155.4 0.6 copy-done.6
  156.0 1.1 copy-done.21
  157.1 0.1 stack.10
  157.3 0.5 copy-done.34
  157.8 0.1 copy-done.32
  158.0 43.6 %shard_map.239 = (f32[28,28,8,128]{3,2,1,0:T(8,128)}, f32[128,384]{1,0:T(8,128)}, f32[128,128]{1,0:T(8,128)}, f32[128,512]{1,0:T(8,128)}, f32[128,512]{1,0:T(8,1...) custom-call(bf16[28,28,8,128]{3,2,1,0:T(8,128)(2,1)} %copy-done.21, ...), custom_call_target="tpu_custom_call" | custom-call | flops 16000000000 | bytes 10000000 | tf_op jit(solution)/shard_map/pallas_call | solution.py:876
  201.6 0.9 stack.9
  202.5 0.1 reshape.70
  202.7 1.5 fusion.3.refs_14_
  204.2 2.6 %shard_map.240 = bf16[32,112,128]{2,1,0:T(8,128)(2,1)} custom-call(f32[128,384]{1,0:T(8,128)} %get-tuple-element.190.refs_0_, f32[128,128]{1,0:T(8,128)} %get-tuple-element.191.refs_1_, f32[128,512]{1,0:T(8,128)} %get-tuple-element.192.refs_2_, f32[128,512]{1,0:T(8,128)} %get-tuple-element.193.refs_3_, f32[128,384]{1,0:T(8,128)} %copy-done.2, ...), custom_call_target="tpu_custom_call" | custom-call | tf_op jit(solution)/shard_map/pallas_call | solution.py:708
  206.7 28.9 %all_to_all.5.packet_ref = bf16[32,112,128]{2,1,0:T(8,128)(2,1)} all-to-all(bf16[32,112,128]{2,1,0:T(8,128)(2,1)} %shard_map.240), channel_id=1, replica_groups=mesh['seq'=8,'wt'=4] {'seq','wt'}, dimensions={0} | all-to-all | bytes 1835008 | tf_op jit(solution)/shard_map/all_to_all | solution.py:740
  235.7 1.9 shard_map.241
  237.6 11.1 %all-gather = bf16[896,128]{1,0:T(8,128)(2,1)} all-gather(bf16[112,128]{1,0:T(8,128)(2,1)} %shard_map.241), channel_id=2, replica_groups=mesh['seq'=8,'wt'=4] {'seq'}, dimensions={0}, use_global_device_ids=true | all-gather | bytes 258048 | tf_op jit(solution)/shard_map/all_gather | solution.py:742
  248.7 1.7 shard_map.242
  (97 shorter events, 0.8 us)
Async XLA Ops:
  0.6 14.6 %copy-start.24 = (s32[8,28,28]{2,0,1:T(8,128)S(1)}, s32[8,28,28]{2,0,1:T(8,128)}, u32[]{:S(2)}) copy-start(s32[8,28,28]{2,0,1:T(8,128)} %param.15) | copy-start | bytes 75268
  3.9 11.9 %copy-start.23 = (bf16[384,128]{1,0:T(8,128)(2,1)}, bf16[384,128]{1,0:T(8,128)(2,1)S(1)}, u32[]{:S(2)}) copy-start(bf16[384,128]{1,0:T(8,128)(2,1)S(1)} %get-tuple-element.219.refs_1_) | copy-start | bytes 294916
  3.9 36.5 %copy-start.22 = (bf16[384,128]{1,0:T(8,128)(2,1)}, bf16[384,128]{1,0:T(8,128)(2,1)S(1)}, u32[]{:S(2)}) copy-start(bf16[384,128]{1,0:T(8,128)(2,1)S(1)} %get-tuple-element.138.refs_1_) | copy-start | bytes 294916
  3.9 14.9 %collective-permute-start.2 = (bf16[384,128]{1,0:T(8,128)(2,1)S(1)}, bf16[384,128]{1,0:T(8,128)(2,1)S(1)}, u32[]{:S(2)}, u32[]{:S(2)}) collective-permute-start(bf16[384,128]{1,0:T(8,128)(2,1)S(1)} %get-tuple-element.219.refs_1_), channel_id=1, source_target_pairs={{0,1},{1,2},{2,3},{3,0},{4,5},{5,6},{6,7},{7,4},{8,9},{9,10},{10,1... | collective-permute-start | bytes 294920 | tf_op jit(solution)/shard_map/ppermute | solution.py:506
  7.0 11.8 %collective-permute-start.1 = (bf16[384,128]{1,0:T(8,128)(2,1)S(1)}, bf16[384,128]{1,0:T(8,128)(2,1)S(1)}, u32[]{:S(2)}, u32[]{:S(2)}) collective-permute-start(bf16[384,128]{1,0:T(8,128)(2,1)S(1)} %get-tuple-element.219.refs_1_), channel_id=1, source_target_pairs={{0,2},{1,3},{2,0},{3,1},{4,6},{5,7},{6,4},{7,5},{8,10},{9,11},{10,... | collective-permute-start | bytes 294920 | tf_op jit(solution)/shard_map/ppermute | solution.py:506
  9.6 9.2 %collective-permute-start = (bf16[384,128]{1,0:T(8,128)(2,1)S(1)}, bf16[384,128]{1,0:T(8,128)(2,1)S(1)}, u32[]{:S(2)}, u32[]{:S(2)}) collective-permute-start(bf16[384,128]{1,0:T(8,128)(2,1)S(1)} %get-tuple-element.219.refs_1_), channel_id=1, source_target_pairs={{0,3},{1,0},{2,1},{3,2},{4,7},{5,4},{6,5},{7,6},{8,11},{9,8},{10,9... | collective-permute-start | bytes 294920 | tf_op jit(solution)/shard_map/ppermute | solution.py:506
  18.8 0.7 copy-start.28
  18.8 0.7 copy-start.29
  18.8 0.7 copy-start.30
  21.3 17.9 %copy-start.31 = (s32[49,49]{1,0:T(8,128)S(1)}, s32[49,49]{1,0:T(8,128)}, u32[]{:S(2)}) copy-start(s32[49,49]{1,0:T(8,128)} %param.16) | copy-start | bytes 28816
  38.5 7.7 %collective-permute-start.5 = (bf16[384,128]{1,0:T(8,128)(2,1)S(1)}, bf16[384,128]{1,0:T(8,128)(2,1)S(1)}, u32[]{:S(2)}, u32[]{:S(2)}) collective-permute-start(bf16[384,128]{1,0:T(8,128)(2,1)S(1)} %get-tuple-element.138.refs_1_), channel_id=1, source_target_pairs={{0,1},{1,2},{2,3},{3,0},{4,5},{5,6},{6,7},{7,4},{8,9},{9,10},{10,1... | collective-permute-start | bytes 294920 | tf_op jit(solution)/shard_map/ppermute | solution.py:506
  39.5 29.9 %collective-permute-start.4 = (bf16[384,128]{1,0:T(8,128)(2,1)S(1)}, bf16[384,128]{1,0:T(8,128)(2,1)S(1)}, u32[]{:S(2)}, u32[]{:S(2)}) collective-permute-start(bf16[384,128]{1,0:T(8,128)(2,1)S(1)} %get-tuple-element.138.refs_1_), channel_id=1, source_target_pairs={{0,2},{1,3},{2,0},{3,1},{4,6},{5,7},{6,4},{7,5},{8,10},{9,11},{10,... | collective-permute-start | bytes 294920 | tf_op jit(solution)/shard_map/ppermute | solution.py:506
  40.4 29.0 %collective-permute-start.3 = (bf16[384,128]{1,0:T(8,128)(2,1)S(1)}, bf16[384,128]{1,0:T(8,128)(2,1)S(1)}, u32[]{:S(2)}, u32[]{:S(2)}) collective-permute-start(bf16[384,128]{1,0:T(8,128)(2,1)S(1)} %get-tuple-element.138.refs_1_), channel_id=1, source_target_pairs={{0,3},{1,0},{2,1},{3,2},{4,7},{5,4},{6,5},{7,6},{8,11},{9,8},{10,9... | collective-permute-start | bytes 294920 | tf_op jit(solution)/shard_map/ppermute | solution.py:506
  42.7 29.7 %collective-permute-start.8 = (bf16[3,3,8,128]{3,2,1,0:T(8,128)(2,1)}, bf16[3,3,8,128]{3,2,1,0:T(8,128)(2,1)S(1)}, u32[]{:S(2)}, u32[]{:S(2)}) collective-permute-start(bf16[3,3,8,128]{3,2,1,0:T(8,128)(2,1)} %get-tuple-element.143), channel_id=1, source_target_pairs={{0,31},{1,28},{2,29},{3,30},{4,3},{5,0},{6,1},{7,2},{8,7},{9,4},{1... | collective-permute-start | bytes 55304 | tf_op jit(solution)/shard_map/ppermute | solution.py:516
  43.8 28.7 %collective-permute-start.6 = (bf16[3,28,8,128]{3,2,1,0:T(8,128)(2,1)}, bf16[3,28,8,128]{3,2,1,0:T(8,128)(2,1)S(1)}, u32[]{:S(2)}, u32[]{:S(2)}) collective-permute-start(bf16[3,28,8,128]{3,2,1,0:T(8,128)(2,1)} %get-tuple-element.141), channel_id=1, source_target_pairs={{0,28},{4,0},{8,4},{12,8},{16,12},{20,16},{24,20},{28,24},{1,29},{... | collective-permute-start | bytes 516104 | tf_op jit(solution)/shard_map/ppermute | solution.py:506
  46.2 23.2 %copy-start.25 = (bf16[384,128]{1,0:T(8,128)(2,1)}, bf16[384,128]{1,0:T(8,128)(2,1)S(1)}, u32[]{:S(2)}) copy-start(bf16[384,128]{1,0:T(8,128)(2,1)S(1)} %collective-permute-done.5.refs_4_) | copy-start | bytes 294916
  46.2 26.3 %collective-permute-start.7 = (bf16[28,3,8,128]{3,2,1,0:T(8,128)(2,1)}, bf16[28,3,8,128]{3,2,1,0:T(8,128)(2,1)S(1)}, u32[]{:S(2)}, u32[]{:S(2)}) collective-permute-start(bf16[28,3,8,128]{3,2,1,0:T(8,128)(2,1)} %get-tuple-element.142), channel_id=1, source_target_pairs={{0,3},{1,0},{2,1},{3,2},{4,7},{5,4},{6,5},{7,6},{8,11},{9,8},{10,9... | collective-permute-start | bytes 516104 | tf_op jit(solution)/shard_map/ppermute | solution.py:506
  48.3 24.2 %copy-start.17 = (f32[2,2,128]{2,1,0:T(2,128)S(1)}, f32[2,2,128]{2,1,0:T(2,128)}, u32[]{:S(2)}) copy-start(f32[2,2,128]{2,1,0:T(2,128)} %refs_21_.1) | copy-start | bytes 6148
  69.4 0.6 copy-start.26
  70.0 0.6 copy-start.27
  72.5 0.9 copy-start.10
  73.4 1.4 copy-start.19
  81.8 9.8 %collective-permute-start.11 = (bf16[3,3,8,128]{3,2,1,0:T(8,128)(2,1)S(1)}, bf16[3,3,8,128]{3,2,1,0:T(8,128)(2,1)S(1)}, u32[]{:S(2)}, u32[]{:S(2)}) collective-permute-start(bf16[3,3,8,128]{3,2,1,0:T(8,128)(2,1)S(1)} %get-tuple-element.154), channel_id=1, source_target_pairs={{0,5},{1,6},{2,7},{3,4},{4,9},{5,10},{6,11},{7,8},{8,13},{9,14},{1... | collective-permute-start | bytes 55304 | tf_op jit(solution)/shard_map/ppermute | solution.py:516
  81.9 9.8 %collective-permute-start.9 = (bf16[3,28,8,128]{3,2,1,0:T(8,128)(2,1)S(1)}, bf16[3,28,8,128]{3,2,1,0:T(8,128)(2,1)S(1)}, u32[]{:S(2)}, u32[]{:S(2)}) collective-permute-start(bf16[3,28,8,128]{3,2,1,0:T(8,128)(2,1)S(1)} %get-tuple-element.152), channel_id=1, source_target_pairs={{0,4},{4,8},{8,12},{12,16},{16,20},{20,24},{24,28},{28,0},{1,5},{5... | collective-permute-start | bytes 516104 | tf_op jit(solution)/shard_map/ppermute | solution.py:506
  82.8 8.9 %collective-permute-start.10 = (bf16[28,3,8,128]{3,2,1,0:T(8,128)(2,1)S(1)}, bf16[28,3,8,128]{3,2,1,0:T(8,128)(2,1)S(1)}, u32[]{:S(2)}, u32[]{:S(2)}) collective-permute-start(bf16[28,3,8,128]{3,2,1,0:T(8,128)(2,1)S(1)} %get-tuple-element.153), channel_id=1, source_target_pairs={{0,1},{1,2},{2,3},{3,0},{4,5},{5,6},{6,7},{7,4},{8,9},{9,10},{10,1... | collective-permute-start | bytes 516104 | tf_op jit(solution)/shard_map/ppermute | solution.py:506
  82.8 8.9 %copy-start.7 = (bf16[8,28,28,128]{3,0,2,1:T(8,128)(2,1)S(1)}, bf16[8,28,28,128]{3,0,2,1:T(8,128)(2,1)}, u32[]{:S(2)}) copy-start(bf16[8,28,28,128]{3,0,2,1:T(8,128)(2,1)} %param.27) | copy-start | bytes 4816900
  82.8 8.9 %copy-start.8 = (bf16[128,512]{1,0:T(8,128)(2,1)S(1)}, bf16[128,512]{1,0:T(8,128)(2,1)}, u32[]{:S(2)}) copy-start(bf16[128,512]{1,0:T(8,128)(2,1)} %get-tuple-element.150.refs_7_.refs_4_) | copy-start | bytes 393220
  82.8 8.9 %copy-start.9 = (bf16[512,128]{1,0:T(8,128)(2,1)S(1)}, bf16[512,128]{1,0:T(8,128)(2,1)}, u32[]{:S(2)}) copy-start(bf16[512,128]{1,0:T(8,128)(2,1)} %get-tuple-element.151.refs_8_.refs_5_) | copy-start | bytes 393220
  82.8 8.9 %copy-start.12 = (bf16[128,128]{1,0:T(8,128)(2,1)S(1)}, bf16[128,128]{1,0:T(8,128)(2,1)}, u32[]{:S(2)}) copy-start(bf16[128,128]{1,0:T(8,128)(2,1)} %get-tuple-element.149.refs_6_.refs_3_) | copy-start | bytes 98308
  82.8 8.9 %copy-start.13 = (f32[2,512]{1,0:T(2,128)S(1)}, f32[2,512]{1,0:T(2,128)}, u32[]{:S(2)}) copy-start(f32[2,512]{1,0:T(2,128)} %refs_9_.7) | copy-start | bytes 12292
  82.9 8.9 %copy-start.14 = (f32[2,2,128]{2,1,0:T(2,128)S(1)}, f32[2,2,128]{2,1,0:T(2,128)}, u32[]{:S(2)}) copy-start(f32[2,2,128]{2,1,0:T(2,128)} %refs_8_.5) | copy-start | bytes 6148
  82.9 8.9 %copy-start.15 = (f32[2,2,128]{2,1,0:T(2,128)S(1)}, f32[2,2,128]{2,1,0:T(2,128)}, u32[]{:S(2)}) copy-start(f32[2,2,128]{2,1,0:T(2,128)} %refs_19_.1) | copy-start | bytes 6148
  82.9 8.9 %copy-start.16 = (f32[2,2,128]{2,1,0:T(2,128)S(1)}, f32[2,2,128]{2,1,0:T(2,128)}, u32[]{:S(2)}) copy-start(f32[2,2,128]{2,1,0:T(2,128)} %refs_20_.1) | copy-start | bytes 6148
  82.9 8.9 %copy-start.18 = (f32[4,4,392,128]{3,2,1,0:T(8,128)S(1)}, f32[4,4,392,128]{3,2,1,0:T(8,128)}, u32[]{:S(2)}) copy-start(f32[4,4,392,128]{3,2,1,0:T(8,128)} %get-tuple-element.148.refs_4_.refs_1_) | copy-start | bytes 9633796
  104.2 25.1 %collective-permute-start.14 = (bf16[3,3,8,128]{3,2,1,0:T(8,128)(2,1)S(1)}, bf16[3,3,8,128]{3,2,1,0:T(8,128)(2,1)S(1)}, u32[]{:S(2)}, u32[]{:S(2)}) collective-permute-start(bf16[3,3,8,128]{3,2,1,0:T(8,128)(2,1)S(1)} %get-tuple-element.169), channel_id=1, source_target_pairs={{0,31},{1,28},{2,29},{3,30},{4,3},{5,0},{6,1},{7,2},{8,7},{9,4},{1... | collective-permute-start | bytes 55304 | tf_op jit(solution)/shard_map/ppermute | solution.py:516
  109.0 20.4 %collective-permute-start.12 = (bf16[3,28,8,128]{3,2,1,0:T(8,128)(2,1)S(1)}, bf16[3,28,8,128]{3,2,1,0:T(8,128)(2,1)S(1)}, u32[]{:S(2)}, u32[]{:S(2)}) collective-permute-start(bf16[3,28,8,128]{3,2,1,0:T(8,128)(2,1)S(1)} %get-tuple-element.167), channel_id=1, source_target_pairs={{0,28},{4,0},{8,4},{12,8},{16,12},{20,16},{24,20},{28,24},{1,29},{... | collective-permute-start | bytes 516104 | tf_op jit(solution)/shard_map/ppermute | solution.py:506
  109.3 20.1 %collective-permute-start.13 = (bf16[28,3,8,128]{3,2,1,0:T(8,128)(2,1)S(1)}, bf16[28,3,8,128]{3,2,1,0:T(8,128)(2,1)S(1)}, u32[]{:S(2)}, u32[]{:S(2)}) collective-permute-start(bf16[28,3,8,128]{3,2,1,0:T(8,128)(2,1)S(1)} %get-tuple-element.168), channel_id=1, source_target_pairs={{0,3},{1,0},{2,1},{3,2},{4,7},{5,4},{6,5},{7,6},{8,11},{9,8},{10,9... | collective-permute-start | bytes 516104 | tf_op jit(solution)/shard_map/ppermute | solution.py:506
  111.4 18.0 %copy-start.11 = (bf16[128,384]{1,0:T(8,128)(2,1)S(1)}, bf16[128,384]{1,0:T(8,128)(2,1)}, u32[]{:S(2)}) copy-start(bf16[128,384]{1,0:T(8,128)(2,1)} %get-tuple-element.139.refs_4_.refs_1_.refs_11_.refs_5_) | copy-start | bytes 294916
  126.1 0.7 copy-start
  126.8 0.7 copy-start.1
  127.5 0.6 copy-start.3
  128.2 0.6 copy-start.4
  128.8 0.6 copy-start.5
  129.4 11.1 %copy-start.20 = (f32[4,4,392,128]{3,2,1,0:T(8,128)}, f32[4,4,392,128]{3,2,1,0:T(8,128)S(1)}, u32[]{:S(2)}) copy-start(f32[4,4,392,128]{3,2,1,0:T(8,128)S(1)} %get-tuple-element.178.refs_4_) | copy-start | bytes 9633796
  140.5 16.7 %collective-permute-start.17 = (bf16[3,3,8,128]{3,2,1,0:T(8,128)(2,1)S(1)}, bf16[3,3,8,128]{3,2,1,0:T(8,128)(2,1)S(1)}, u32[]{:S(2)}, u32[]{:S(2)}) collective-permute-start(bf16[3,3,8,128]{3,2,1,0:T(8,128)(2,1)S(1)} %get-tuple-element.177), channel_id=1, source_target_pairs={{0,5},{1,6},{2,7},{3,4},{4,9},{5,10},{6,11},{7,8},{8,13},{9,14},{1... | collective-permute-start | bytes 55304 | tf_op jit(solution)/shard_map/ppermute | solution.py:516
  140.6 16.7 %collective-permute-start.15 = (bf16[3,28,8,128]{3,2,1,0:T(8,128)(2,1)S(1)}, bf16[3,28,8,128]{3,2,1,0:T(8,128)(2,1)S(1)}, u32[]{:S(2)}, u32[]{:S(2)}) collective-permute-start(bf16[3,28,8,128]{3,2,1,0:T(8,128)(2,1)S(1)} %get-tuple-element.175), channel_id=1, source_target_pairs={{0,4},{4,8},{8,12},{12,16},{16,20},{20,24},{24,28},{28,0},{1,5},{5... | collective-permute-start | bytes 516104 | tf_op jit(solution)/shard_map/ppermute | solution.py:506
  140.7 16.6 %collective-permute-start.16 = (bf16[28,3,8,128]{3,2,1,0:T(8,128)(2,1)S(1)}, bf16[28,3,8,128]{3,2,1,0:T(8,128)(2,1)S(1)}, u32[]{:S(2)}, u32[]{:S(2)}) collective-permute-start(bf16[28,3,8,128]{3,2,1,0:T(8,128)(2,1)S(1)} %get-tuple-element.176), channel_id=1, source_target_pairs={{0,1},{1,2},{2,3},{3,0},{4,5},{5,6},{6,7},{7,4},{8,9},{9,10},{10,1... | collective-permute-start | bytes 516104 | tf_op jit(solution)/shard_map/ppermute | solution.py:506
  154.7 0.7 copy-start.2
  155.4 0.6 copy-start.6
  156.0 1.1 copy-start.21
  157.2 0.6 copy-start.34
  157.3 0.7 copy-start.32
  157.3 0.7 copy-start.33

commit v6 on v5

--- a/solution.py
+++ b/solution.py
@@ -22,7 +22,8 @@
 F32 = jnp.float32
 MIB = 1024 * 1024
 VMEM_LIMIT = 56 * MIB
-LIMITS = ((60, 60), (16, 16), (16, 16), (16, 16), 60)
+GROUP = 2
+LIMITS = ((60, 60), (16, 16), (16, 16), (16, 16), 63)
 
 
 def mm(left, right):
@@ -151,6 +152,7 @@
     depth = lanes.shape[1]
     everything = range(images)
     upstream = [window(sc_grad, i, images, ASKED) for i in everything]
+    yield
     centred = [
         mm_nt(
             jnp.concatenate([upstream[i], window(sc_out, i, images, ASKED)], 1).astype(BF),
@@ -158,6 +160,7 @@
         )
         for i in everything
     ]
+    yield
     powers = [powers_ref[0, 0, i].astype(F32) for i in everything]
     score_grads = [powers[i] * centred[i] for i in everything]
     low_grads = [one.astype(BF) for one in score_grads]
@@ -165,7 +168,9 @@
     for i in everything[1:]:
         total = total + low_grads[i].astype(F32)
     bias_acc[...] += total
+    yield
     d_queries = [mm(low_grads[i], head_blocks(window(sc_k, i, images))) for i in everything]
+    yield
     empty = jnp.zeros((ASKED, depth), F32)
     d_both = [
         mm_tn(
@@ -180,6 +185,7 @@
         )
         for i in everything
     ]
+    yield
     for i in everything:
         place = pl.ds(i, SLOT, stride=images)
         sc_dq[pl.ds(i, ASKED, stride=images), :] = d_queries[i] * SCALE
@@ -444,7 +450,7 @@
     gradient = ahead_window(low_ref, low_halo, held, place)
     put_upstream(count, sc_grad, sc_out, gradient, tokens_of(out_ref), share_ref[0, 0])
     grads = (sc_dq, sc_dk, sc_dv)
-    attention_backward(images, (sc_q, sc_k, sc_v), sc_grad, sc_out, powers_ref, grads, bias_acc)
+    yield from attention_backward(images, (sc_q, sc_k, sc_v), sc_grad, sc_out, powers_ref, grads, bias_acc)
     joined = joined_gradients(count, grads, qv_sums)
     g_qkv[...] += mm_tn(hidden, joined)
     block = put_tokens(hidden_grad_out, mm_nt(joined, w_qkv[...]))
@@ -468,6 +474,7 @@
     gradient = grad_ref[0, 0] + norm_backward(upstream, normed, inverse, gains[1, 0:1])
     sums[4] += fold_rows(upstream * normed)
     sums[5] += fold_rows(upstream)
+    yield
     out_low = gradient.astype(BF)
     normed, inverse = get_norm((n_two, r_two))
     inner = (normed * gains[0, 1:2] + shifts[0, 1:2]).astype(BF)
@@ -476,14 +483,17 @@
     expanded_low, inner_grad = feed_forward_backward(
         out_low, inner, activated, slope, w_fc1[...], w_fc2[...]
     )
+    yield
     updated = gradient + norm_backward(inner_grad, normed, inverse, gains[0, 1:2])
     branch_low = updated.astype(BF)
+    yield
     low = mm_nt(branch_low, w_proj[...]).astype(BF).astype(F32)
     attended = att_ref[0, 0]
+    yield
     split_projection(hidden, w_qkv[...], qkv_bias, 0, (sc_q, sc_k, sc_v), count)
     put_upstream(count, sc_grad, sc_out, low, attended.astype(F32), share_ref[0, 0])
     grads = (sc_dq, sc_dk, sc_dv)
-    attention_backward(images, (sc_q, sc_k, sc_v), sc_grad, sc_out, powers_ref, grads, bias_acc)
+    yield from attention_backward(images, (sc_q, sc_k, sc_v), sc_grad, sc_out, powers_ref, grads, bias_acc)
     g_fc2[...] += mm_tn(out_low, activated)
     g_fc1[...] += mm_tn(inner, expanded_low)
     g_proj[...] += mm_tn(attended, branch_low)
@@ -492,8 +502,10 @@
     sums[1] += fold_rows(inner_grad * normed)
     sums[2] += fold_rows(inner_grad)
     sums[3] += fold_rows(branch_low.astype(F32))
+    yield
     joined = joined_gradients(count, grads, qv_sums)
     g_qkv[...] += mm_tn(hidden, joined)
+    yield
     upstream = mm_nt(joined, w_qkv[...])
     term = norm_backward(upstream, normed_one, inverse_one, gains[0, 0:1])
     put_tokens(tokens_grad_out, updated + term)
@@ -861,7 +873,7 @@
                 return ref.at[:, pl.ds(k * size, size)]
 
             each = len(rest) // group
-            for k in range(group):
+            runs = [
                 kernel(
                     images,
                     (row, col * group + k, rows, cols),
@@ -870,6 +882,12 @@
                     *[view(ref, spec, k) for ref, (_, spec) in zip(outs, outputs)],
                     *rest[k * each : (k + 1) * each],
                 )
+                for k in range(group)
+            ]
+            done = object()
+            runs = [one for one in runs if one is not None]
+            while runs:
+                runs = [one for one in runs if next(one, done) is not done]
 
         scratch = [pltpu.VMEM((WIN, WIN, images, depth), BF)] if held else []
         scratch += [pltpu.VMEM((SLOT * images, depth), F32)] * slots
@@ -1012,6 +1030,7 @@
         8,
         LIMITS[4],
         held=True,
+        group=GROUP,
     )
 
     bias_sums = jnp.stack([bias_sums0, bias_sums1]).reshape(2, ASKED, HEADS, SLOT)

time: 251 us -> 248 us (0.988)
  Pallas kernels: 160 us -> 156 us
    pallas_call x9, Pallas kernels: 150 us -> 146 us  [run(): pl.pallas_call(body, grid=(steps,), in_specs=in_specs, out_specs=out_spec...]
    unnamed x84 -> x86, local copies, waits for them, and re-layouts: 11.5 us -> 12 us
where the time goes in v6:
time: 248 us; the launch traced here: 247 us
  Pallas kernels  156 us (63%)
  blocking collectives  39.8 us (16%)
  starting transfers between devices  25 us (10%)
  local copies, waits for them, and re-layouts  17.8 us (7%)
  matrix products  4.2 us (2%)
  other arithmetic  3.09 us (1%)
    pallas_call x9, Pallas kernels, run(): pl.pallas_call(body, grid=(steps,), in_specs=in_specs, out_specs=out_spec...  146 us
    all_to_all x1, blocking collectives, sum_everywhere(): packets = lax.all_to_all(packets, ('seq', 'wt'), 0, 0, tiled=True)  28.7 us
    ppermute x14, starting transfers between devices, shift_by(): lax.ppermute(array, axis, [(i, (i + by) % count) for i in range(count)])  19.1 us
    unnamed x86, local copies, waits for them, and re-layouts  12 us
    all_gather x1, blocking collectives, sum_everywhere(): mine = lax.all_gather(mine, 'seq', axis=0)  11.1 us
    pallas_call x3, Pallas kernels, whole_kernel(): pl.pallas_call(body, in_specs=[full] * len(inputs), out_specs=[full] * le...  6.15 us
    ppermute x4, starting transfers between devices, shift_both(): return lax.ppermute(array, ('seq', 'wt'), pairs)  5.92 us
  transfers between devices with their start and end apart: 18, of which 1 were waited for; matrix products, arithmetic and copies ran while one was open for 3% of the time, Pallas kernels for 24%

profile of v6, /device:TPU:0, one launch (start us, length us, event | category | flops | bytes accessed | tf_op | source)
XLA Modules:
  0.0 247.2 jit_solution(1067050200089428556)
XLA Ops:
  0.7 0.8 slice_bitcast_fusion.2
  1.4 0.8 slice_bitcast_fusion
  2.3 0.7 constant_dynamic-update-slice_fusion.14
  3.1 0.8 constant_dynamic-update-slice_fusion.9
  3.9 3.1 %collective-permute-start.2 = (bf16[384,128]{1,0:T(8,128)(2,1)S(1)}, bf16[384,128]{1,0:T(8,128)(2,1)S(1)}, u32[]{:S(2)}, u32[]{:S(2)}) collective-permute-start(bf16[384,128]{1,0:T(8,128)(2,1)S(1)} %get-tuple-element.219.refs_1_), channel_id=1, source_target_pairs={{0,1},{1,2},{2,3},{3,0},{4,5},{5,6},{6,7},{7,4},{8,9},{9,10},{10,1... | collective-permute-start | bytes 294920 | tf_op jit(solution)/shard_map/ppermute | solution.py:518
  7.0 2.6 %collective-permute-start.1 = (bf16[384,128]{1,0:T(8,128)(2,1)S(1)}, bf16[384,128]{1,0:T(8,128)(2,1)S(1)}, u32[]{:S(2)}, u32[]{:S(2)}) collective-permute-start(bf16[384,128]{1,0:T(8,128)(2,1)S(1)} %get-tuple-element.219.refs_1_), channel_id=1, source_target_pairs={{0,2},{1,3},{2,0},{3,1},{4,6},{5,7},{6,4},{7,5},{8,10},{9,11},{10,... | collective-permute-start | bytes 294920 | tf_op jit(solution)/shard_map/ppermute | solution.py:518
  9.6 1.3 collective-permute-start
  10.9 0.7 multiply_bitcast_fusion
  11.6 2.7 %fusion.6 = f32[2,49,4,49]{3,2,0,1:T(4,128)S(1)} fusion(f32[2,4,169,1]{2,1,0,3:T(4,128)S(1)} %reshape.73, s32[49,49]{1,0:T(8,128)} %param.16), kind=kOutput, calls=%fused_computation.9 | convolution fusion | flops 39359592 | bytes 91844 | tf_op jit(solution)/shard_map/dot_general | solution.py:787
  14.5 0.7 squeeze.34.refs_10_
  15.2 0.2 reshape.69
  15.5 0.3 copy.46
  15.8 0.2 ne.15
  15.9 1.3 broadcast_compare_fusion
  17.2 0.5 pad.13
  17.7 1.0 add_convert_fusion.refs_7_.refs_4_
  18.8 0.6 copy-done.31
  19.5 1.8 shard_map.229
  21.3 17.2 %shard_map.230 = (f32[4,4,392,128]{3,2,1,0:T(8,128)}, bf16[28,28,8,128]{3,2,1,0:T(8,128)(2,1)}, bf16[4,4,392,128]{3,2,1,0:T(8,128)(2,1)}, f32[4,4,392,128]{3,2,1...) custom-call(bf16[28,28,8,128]{3,2,1,0:T(8,128)(2,1)} %bitcast.55, ...), custom_call_target="tpu_custom_call" | custom-call | flops 7000000000 | bytes 10000000 | tf_op jit(solution)/shard_map/pallas_call | solution.py:894
  38.5 0.7 collective-permute-start.5
  39.2 0.1 eq.41
  39.3 0.1 squeeze.39.refs_6_.refs_3_
  39.5 0.9 collective-permute-start.4
  40.4 2.3 collective-permute-start.3
  42.7 1.1 collective-permute-start.8
  43.8 2.3 collective-permute-start.6
  46.1 0.1 collective-permute-done.5.refs_4_
  46.1 2.2 collective-permute-start.7
  48.3 21.0 %shard_map.231 = (f32[4,4,392,128]{3,2,1,0:T(8,128)}, bf16[28,28,8,128]{3,2,1,0:T(8,128)(2,1)}, bf16[4,4,392,128]{3,2,1,0:T(8,128)(2,1)}, f32[4,4,392,128]{3,2,1...) custom-call(bf16[28,28,8,128]{3,2,1,0:T(8,128)(2,1)} %bitcast.56, ...), custom_call_target="tpu_custom_call", output_to_operand_aliasing={{0}: (11, {}), {1}: (12, {}), {2}: (13, {}), {3}: (14, {}),... | custom-call | flops 8999999488 | bytes 10000000 | tf_op jit(solution)/shard_map/pallas_call | solution.py:894
  69.3 0.6 copy-done.29
  70.0 0.6 copy-done.30
  70.6 1.8 shard_map.232
  72.5 0.9 copy-done.15
  73.4 1.4 copy-done.21
  74.8 7.0 %shard_map.233 = (bf16[28,28,8,128]{3,2,1,0:T(8,128)(2,1)S(1)}, f32[4,4,392,128]{3,2,1,0:T(8,128)S(1)}, bf16[4,4,8,56,256]{4,3,2,1,0:T(8,128)(2,1)S(1)}, bf16[3,...) custom-call(bf16[28,28,8,128]{3,2,1,0:T(8,128)(2,1)S(1)} %copy-done.21, ...), custom_call_target="tpu_custom_call" | custom-call | flops 7000000000 | bytes 10000000 | tf_op jit(solution)/shard_map/pallas_call | solution.py:894
  81.9 0.9 collective-permute-start.9
  82.9 8.8 %shard_map.234 = (bf16[28,28,8,128]{3,2,1,0:T(8,128)(2,1)S(1)}, f32[4,4,392,128]{3,2,1,0:T(8,128)S(1)}, bf16[4,4,8,56,256]{4,3,2,1,0:T(8,128)(2,1)S(1)}) custom-call(bf16[28,28,8,128]{3,2,1,0:T(8,128)(2,1)S(1)} %copy-done.22, bf16[128,384]{1,0:T(8,128)(2,1)S(1)} %copy-done.15, ...), custom_call_target="tpu_custom_call", output_to_operand_aliasing={{0}: (5, {}), {1}: (6, {}), {2}: (7, {})} | custom-call | flops 8999999488 | bytes 10000000 | tf_op jit(solution)/shard_map/pallas_call | solution.py:894
  91.8 12.4 %shard_map.235 = (bf16[28,28,8,128]{3,2,1,0:T(8,128)(2,1)}, f32[4,4,392,128]{3,2,1,0:T(8,128)S(1)}, bf16[28,28,8,128]{3,2,1,0:T(8,128)(2,1)S(1)}, f32[128,128]{1...) custom-call(bf16[28,28,8,128]{3,2,1,0:T(8,128)(2,1)S(1)} %get-tuple-, ...), custom_call_target="tpu_custom_call" | custom-call | flops 7000000000 | bytes 10000000 | tf_op jit(solution)/shard_map/pallas_call | solution.py:894
  104.2 4.7 %collective-permute-start.14 = (bf16[3,3,8,128]{3,2,1,0:T(8,128)(2,1)S(1)}, bf16[3,3,8,128]{3,2,1,0:T(8,128)(2,1)S(1)}, u32[]{:S(2)}, u32[]{:S(2)}) collective-permute-start(bf16[3,3,8,128]{3,2,1,0:T(8,128)(2,1)S(1)} %get-tuple-element.169), channel_id=1, source_target_pairs={{0,31},{1,28},{2,29},{3,30},{4,3},{5,0},{6,1},{7,2},{8,7},{9,4},{1... | collective-permute-start | bytes 55304 | tf_op jit(solution)/shard_map/ppermute | solution.py:528
  109.0 0.4 collective-permute-start.12
  109.3 2.0 collective-permute-start.13
  111.3 14.7 %shard_map.236 = (bf16[28,28,8,128]{3,2,1,0:T(8,128)(2,1)}, f32[4,4,392,128]{3,2,1,0:T(8,128)S(1)}, bf16[28,28,8,128]{3,2,1,0:T(8,128)(2,1)S(1)}, f32[128,128]{1...) custom-call(bf16[28,28,8,128]{3,2,1,0:T(8,128)(2,1)S(1)} %get-tuple-, ...), custom_call_target="tpu_custom_call", output_to_operand_aliasing={{0}: (10, {}), {1}: (11, {}), {2}: (12, {})} | custom-call | flops 8999999488 | bytes 10000000 | tf_op jit(solution)/shard_map/pallas_call | solution.py:894
  126.1 1.7 copy-done
  127.8 0.7 copy-done.2
  128.5 0.7 copy-done.3
  129.2 0.6 copy-done.5
  129.9 11.1 %shard_map.237 = (bf16[28,28,8,128]{3,2,1,0:T(8,128)(2,1)S(1)}, f32[128,384]{1,0:T(8,128)S(1)}, f32[2,8,128]{2,1,0:T(8,128)S(1)}, f32[56,256]{1,0:T(8,128)S(1)},...) custom-call(bf16[28,28,8,128]{3,2,1,0:T(8,128)(2,1)S(1)} %copy-done.22,, ...), custom_call_target="tpu_custom_call" | custom-call | flops 7000000000 | bytes 10000000 | tf_op jit(solution)/shard_map/pallas_call | solution.py:894
  141.1 0.3 collective-permute-start.16
  141.4 14.0 %shard_map.238 = (bf16[28,28,8,128]{3,2,1,0:T(8,128)(2,1)S(1)}, f32[128,384]{1,0:T(8,128)S(1)}, f32[2,8,128]{2,1,0:T(8,128)S(1)}, f32[56,256]{1,0:T(8,128)S(1)}) custom-call(bf16[28,28,8,128]{3,2,1,0:T(8,128)(2,1)S(1)} %copy-done.22, bf16[28,28,8,128]{3,2,1,0:T(8,128)(2,1)S(1)} %get-tuple-element.164.refs_1_, ...), custom_call_target="tpu_custom_call", output_to_operand_aliasing={{0}: (7, {})} | custom-call | flops 8999999488 | bytes 10000000 | tf_op jit(solution)/shard_map/pallas_call | solution.py:894
  155.4 1.1 copy-done.1
  156.5 0.7 copy-done.4
  157.2 0.6 copy-done.8
  157.8 0.1 stack.10
  158.0 0.5 copy-done.35
  158.5 0.1 copy-done.23
  158.7 39.9 %shard_map.239 = (f32[28,28,8,128]{3,2,1,0:T(8,128)}, f32[128,384]{1,0:T(8,128)}, f32[128,128]{1,0:T(8,128)}, f32[128,512]{1,0:T(8,128)}, f32[128,512]{1,0:T(8,1...) custom-call(bf16[28,28,8,128]{3,2,1,0:T(8,128)(2,1)} %copy-done.1, ...), custom_call_target="tpu_custom_call" | custom-call | flops 8000000000 | bytes 10000000 | tf_op jit(solution)/shard_map/pallas_call | solution.py:894
  198.6 0.9 stack.9
  199.6 0.1 reshape.70
  199.7 1.5 fusion.3.refs_14_
  201.2 2.5 %shard_map.240 = bf16[32,112,128]{2,1,0:T(8,128)(2,1)} custom-call(f32[128,384]{1,0:T(8,128)} %get-tuple-element.190.refs_0_, f32[128,128]{1,0:T(8,128)} %get-tuple-element.191.refs_1_, f32[128,512]{1,0:T(8,128)} %get-tuple-element.192.refs_2_, f32[128,512]{1,0:T(8,128)} %get-tuple-element.193.refs_3_, f32[128,384]{1,0:T(8,128)} %copy-done.4, ...), custom_call_target="tpu_custom_call" | custom-call | tf_op jit(solution)/shard_map/pallas_call | solution.py:720
  203.8 28.7 %all_to_all.5.packet_ref = bf16[32,112,128]{2,1,0:T(8,128)(2,1)} all-to-all(bf16[32,112,128]{2,1,0:T(8,128)(2,1)} %shard_map.240), channel_id=1, replica_groups=mesh['seq'=8,'wt'=4] {'seq','wt'}, dimensions={0} | all-to-all | bytes 1835008 | tf_op jit(solution)/shard_map/all_to_all | solution.py:752
  232.5 1.9 shard_map.241
  234.4 11.1 %all-gather = bf16[896,128]{1,0:T(8,128)(2,1)} all-gather(bf16[112,128]{1,0:T(8,128)(2,1)} %shard_map.241), channel_id=2, replica_groups=mesh['seq'=8,'wt'=4] {'seq'}, dimensions={0}, use_global_device_ids=true | all-gather | bytes 258048 | tf_op jit(solution)/shard_map/all_gather | solution.py:754
  245.5 1.7 shard_map.242
  (99 shorter events, 0.8 us)
Async XLA Ops:
  0.6 14.6 %copy-start.27 = (s32[8,28,28]{2,0,1:T(8,128)S(1)}, s32[8,28,28]{2,0,1:T(8,128)}, u32[]{:S(2)}) copy-start(s32[8,28,28]{2,0,1:T(8,128)} %param.15) | copy-start | bytes 75268
  3.9 11.9 %copy-start.26 = (bf16[384,128]{1,0:T(8,128)(2,1)}, bf16[384,128]{1,0:T(8,128)(2,1)S(1)}, u32[]{:S(2)}) copy-start(bf16[384,128]{1,0:T(8,128)(2,1)S(1)} %get-tuple-element.219.refs_1_) | copy-start | bytes 294916
  3.9 36.5 %copy-start.25 = (bf16[384,128]{1,0:T(8,128)(2,1)}, bf16[384,128]{1,0:T(8,128)(2,1)S(1)}, u32[]{:S(2)}) copy-start(bf16[384,128]{1,0:T(8,128)(2,1)S(1)} %get-tuple-element.138.refs_1_) | copy-start | bytes 294916
  3.9 14.8 %collective-permute-start.2 = (bf16[384,128]{1,0:T(8,128)(2,1)S(1)}, bf16[384,128]{1,0:T(8,128)(2,1)S(1)}, u32[]{:S(2)}, u32[]{:S(2)}) collective-permute-start(bf16[384,128]{1,0:T(8,128)(2,1)S(1)} %get-tuple-element.219.refs_1_), channel_id=1, source_target_pairs={{0,1},{1,2},{2,3},{3,0},{4,5},{5,6},{6,7},{7,4},{8,9},{9,10},{10,1... | collective-permute-start | bytes 294920 | tf_op jit(solution)/shard_map/ppermute | solution.py:518
  7.0 11.8 %collective-permute-start.1 = (bf16[384,128]{1,0:T(8,128)(2,1)S(1)}, bf16[384,128]{1,0:T(8,128)(2,1)S(1)}, u32[]{:S(2)}, u32[]{:S(2)}) collective-permute-start(bf16[384,128]{1,0:T(8,128)(2,1)S(1)} %get-tuple-element.219.refs_1_), channel_id=1, source_target_pairs={{0,2},{1,3},{2,0},{3,1},{4,6},{5,7},{6,4},{7,5},{8,10},{9,11},{10,... | collective-permute-start | bytes 294920 | tf_op jit(solution)/shard_map/ppermute | solution.py:518
  9.6 9.2 %collective-permute-start = (bf16[384,128]{1,0:T(8,128)(2,1)S(1)}, bf16[384,128]{1,0:T(8,128)(2,1)S(1)}, u32[]{:S(2)}, u32[]{:S(2)}) collective-permute-start(bf16[384,128]{1,0:T(8,128)(2,1)S(1)} %get-tuple-element.219.refs_1_), channel_id=1, source_target_pairs={{0,3},{1,0},{2,1},{3,2},{4,7},{5,4},{6,5},{7,6},{8,11},{9,8},{10,9... | collective-permute-start | bytes 294920 | tf_op jit(solution)/shard_map/ppermute | solution.py:518
  18.8 0.6 copy-start.31
  18.8 0.7 copy-start.32
  18.8 0.7 copy-start.33
  21.3 17.9 %copy-start.34 = (s32[49,49]{1,0:T(8,128)S(1)}, s32[49,49]{1,0:T(8,128)}, u32[]{:S(2)}) copy-start(s32[49,49]{1,0:T(8,128)} %param.16) | copy-start | bytes 28816
  38.5 7.7 %collective-permute-start.5 = (bf16[384,128]{1,0:T(8,128)(2,1)S(1)}, bf16[384,128]{1,0:T(8,128)(2,1)S(1)}, u32[]{:S(2)}, u32[]{:S(2)}) collective-permute-start(bf16[384,128]{1,0:T(8,128)(2,1)S(1)} %get-tuple-element.138.refs_1_), channel_id=1, source_target_pairs={{0,1},{1,2},{2,3},{3,0},{4,5},{5,6},{6,7},{7,4},{8,9},{9,10},{10,1... | collective-permute-start | bytes 294920 | tf_op jit(solution)/shard_map/ppermute | solution.py:518
  39.5 29.9 %collective-permute-start.4 = (bf16[384,128]{1,0:T(8,128)(2,1)S(1)}, bf16[384,128]{1,0:T(8,128)(2,1)S(1)}, u32[]{:S(2)}, u32[]{:S(2)}) collective-permute-start(bf16[384,128]{1,0:T(8,128)(2,1)S(1)} %get-tuple-element.138.refs_1_), channel_id=1, source_target_pairs={{0,2},{1,3},{2,0},{3,1},{4,6},{5,7},{6,4},{7,5},{8,10},{9,11},{10,... | collective-permute-start | bytes 294920 | tf_op jit(solution)/shard_map/ppermute | solution.py:518
  40.4 28.9 %collective-permute-start.3 = (bf16[384,128]{1,0:T(8,128)(2,1)S(1)}, bf16[384,128]{1,0:T(8,128)(2,1)S(1)}, u32[]{:S(2)}, u32[]{:S(2)}) collective-permute-start(bf16[384,128]{1,0:T(8,128)(2,1)S(1)} %get-tuple-element.138.refs_1_), channel_id=1, source_target_pairs={{0,3},{1,0},{2,1},{3,2},{4,7},{5,4},{6,5},{7,6},{8,11},{9,8},{10,9... | collective-permute-start | bytes 294920 | tf_op jit(solution)/shard_map/ppermute | solution.py:518
  42.7 29.7 %collective-permute-start.8 = (bf16[3,3,8,128]{3,2,1,0:T(8,128)(2,1)}, bf16[3,3,8,128]{3,2,1,0:T(8,128)(2,1)S(1)}, u32[]{:S(2)}, u32[]{:S(2)}) collective-permute-start(bf16[3,3,8,128]{3,2,1,0:T(8,128)(2,1)} %get-tuple-element.143), channel_id=1, source_target_pairs={{0,31},{1,28},{2,29},{3,30},{4,3},{5,0},{6,1},{7,2},{8,7},{9,4},{1... | collective-permute-start | bytes 55304 | tf_op jit(solution)/shard_map/ppermute | solution.py:528
  43.8 28.7 %collective-permute-start.6 = (bf16[3,28,8,128]{3,2,1,0:T(8,128)(2,1)}, bf16[3,28,8,128]{3,2,1,0:T(8,128)(2,1)S(1)}, u32[]{:S(2)}, u32[]{:S(2)}) collective-permute-start(bf16[3,28,8,128]{3,2,1,0:T(8,128)(2,1)} %get-tuple-element.141), channel_id=1, source_target_pairs={{0,28},{4,0},{8,4},{12,8},{16,12},{20,16},{24,20},{28,24},{1,29},{... | collective-permute-start | bytes 516104 | tf_op jit(solution)/shard_map/ppermute | solution.py:518
  46.1 23.2 %copy-start.28 = (bf16[384,128]{1,0:T(8,128)(2,1)}, bf16[384,128]{1,0:T(8,128)(2,1)S(1)}, u32[]{:S(2)}) copy-start(bf16[384,128]{1,0:T(8,128)(2,1)S(1)} %collective-permute-done.5.refs_4_) | copy-start | bytes 294916
  46.1 26.3 %collective-permute-start.7 = (bf16[28,3,8,128]{3,2,1,0:T(8,128)(2,1)}, bf16[28,3,8,128]{3,2,1,0:T(8,128)(2,1)S(1)}, u32[]{:S(2)}, u32[]{:S(2)}) collective-permute-start(bf16[28,3,8,128]{3,2,1,0:T(8,128)(2,1)} %get-tuple-element.142), channel_id=1, source_target_pairs={{0,3},{1,0},{2,1},{3,2},{4,7},{5,4},{6,5},{7,6},{8,11},{9,8},{10,9... | collective-permute-start | bytes 516104 | tf_op jit(solution)/shard_map/ppermute | solution.py:518
  48.3 24.1 %copy-start.11 = (f32[2,2,128]{2,1,0:T(2,128)S(1)}, f32[2,2,128]{2,1,0:T(2,128)}, u32[]{:S(2)}) copy-start(f32[2,2,128]{2,1,0:T(2,128)} %refs_21_.1) | copy-start | bytes 6148
  69.3 0.6 copy-start.29
  70.0 0.6 copy-start.30
  72.5 0.9 copy-start.15
  73.4 1.4 copy-start.21
  74.8 8.0 %copy-start.22 = (bf16[28,28,8,128]{3,2,1,0:T(8,128)(2,1)S(1)}, bf16[28,28,8,128]{3,2,1,0:T(8,128)(2,1)}, u32[]{:S(2)}) copy-start(bf16[28,28,8,128]{3,2,1,0:T(8,128)(2,1)} %get-tuple-element.134.refs_0_) | copy-start | bytes 4816900
  81.8 9.8 %collective-permute-start.11 = (bf16[3,3,8,128]{3,2,1,0:T(8,128)(2,1)S(1)}, bf16[3,3,8,128]{3,2,1,0:T(8,128)(2,1)S(1)}, u32[]{:S(2)}, u32[]{:S(2)}) collective-permute-start(bf16[3,3,8,128]{3,2,1,0:T(8,128)(2,1)S(1)} %get-tuple-element.154), channel_id=1, source_target_pairs={{0,5},{1,6},{2,7},{3,4},{4,9},{5,10},{6,11},{7,8},{8,13},{9,14},{1... | collective-permute-start | bytes 55304 | tf_op jit(solution)/shard_map/ppermute | solution.py:528
  81.9 9.8 %collective-permute-start.9 = (bf16[3,28,8,128]{3,2,1,0:T(8,128)(2,1)S(1)}, bf16[3,28,8,128]{3,2,1,0:T(8,128)(2,1)S(1)}, u32[]{:S(2)}, u32[]{:S(2)}) collective-permute-start(bf16[3,28,8,128]{3,2,1,0:T(8,128)(2,1)S(1)} %get-tuple-element.152), channel_id=1, source_target_pairs={{0,4},{4,8},{8,12},{12,16},{16,20},{20,24},{24,28},{28,0},{1,5},{5... | collective-permute-start | bytes 516104 | tf_op jit(solution)/shard_map/ppermute | solution.py:518
  82.8 8.9 %collective-permute-start.10 = (bf16[28,3,8,128]{3,2,1,0:T(8,128)(2,1)S(1)}, bf16[28,3,8,128]{3,2,1,0:T(8,128)(2,1)S(1)}, u32[]{:S(2)}, u32[]{:S(2)}) collective-permute-start(bf16[28,3,8,128]{3,2,1,0:T(8,128)(2,1)S(1)} %get-tuple-element.153), channel_id=1, source_target_pairs={{0,1},{1,2},{2,3},{3,0},{4,5},{5,6},{6,7},{7,4},{8,9},{9,10},{10,1... | collective-permute-start | bytes 516104 | tf_op jit(solution)/shard_map/ppermute | solution.py:518
  82.8 8.9 %copy-start.9 = (f32[2,2,128]{2,1,0:T(2,128)S(1)}, f32[2,2,128]{2,1,0:T(2,128)}, u32[]{:S(2)}) copy-start(f32[2,2,128]{2,1,0:T(2,128)} %refs_19_.1) | copy-start | bytes 6148
  82.8 8.9 %copy-start.10 = (f32[2,2,128]{2,1,0:T(2,128)S(1)}, f32[2,2,128]{2,1,0:T(2,128)}, u32[]{:S(2)}) copy-start(f32[2,2,128]{2,1,0:T(2,128)} %refs_20_.1) | copy-start | bytes 6148
  82.8 8.9 %copy-start.12 = (bf16[8,28,28,128]{3,0,2,1:T(8,128)(2,1)S(1)}, bf16[8,28,28,128]{3,0,2,1:T(8,128)(2,1)}, u32[]{:S(2)}) copy-start(bf16[8,28,28,128]{3,0,2,1:T(8,128)(2,1)} %param.27) | copy-start | bytes 4816900
  82.8 8.9 %copy-start.13 = (bf16[128,512]{1,0:T(8,128)(2,1)S(1)}, bf16[128,512]{1,0:T(8,128)(2,1)}, u32[]{:S(2)}) copy-start(bf16[128,512]{1,0:T(8,128)(2,1)} %get-tuple-element.150.refs_7_.refs_4_) | copy-start | bytes 393220
  82.8 8.9 %copy-start.14 = (bf16[512,128]{1,0:T(8,128)(2,1)S(1)}, bf16[512,128]{1,0:T(8,128)(2,1)}, u32[]{:S(2)}) copy-start(bf16[512,128]{1,0:T(8,128)(2,1)} %get-tuple-element.151.refs_8_.refs_5_) | copy-start | bytes 393220
  82.8 8.9 %copy-start.17 = (bf16[128,128]{1,0:T(8,128)(2,1)S(1)}, bf16[128,128]{1,0:T(8,128)(2,1)}, u32[]{:S(2)}) copy-start(bf16[128,128]{1,0:T(8,128)(2,1)} %get-tuple-element.149.refs_6_.refs_3_) | copy-start | bytes 98308
  82.9 8.9 %copy-start.18 = (f32[2,512]{1,0:T(2,128)S(1)}, f32[2,512]{1,0:T(2,128)}, u32[]{:S(2)}) copy-start(f32[2,512]{1,0:T(2,128)} %refs_9_.7) | copy-start | bytes 12292
  82.9 8.9 %copy-start.19 = (f32[2,2,128]{2,1,0:T(2,128)S(1)}, f32[2,2,128]{2,1,0:T(2,128)}, u32[]{:S(2)}) copy-start(f32[2,2,128]{2,1,0:T(2,128)} %refs_8_.5) | copy-start | bytes 6148
  82.9 8.9 %copy-start.20 = (f32[4,4,392,128]{3,2,1,0:T(8,128)S(1)}, f32[4,4,392,128]{3,2,1,0:T(8,128)}, u32[]{:S(2)}) copy-start(f32[4,4,392,128]{3,2,1,0:T(8,128)} %get-tuple-element.148.refs_4_.refs_1_) | copy-start | bytes 9633796
  104.2 25.6 %collective-permute-start.14 = (bf16[3,3,8,128]{3,2,1,0:T(8,128)(2,1)S(1)}, bf16[3,3,8,128]{3,2,1,0:T(8,128)(2,1)S(1)}, u32[]{:S(2)}, u32[]{:S(2)}) collective-permute-start(bf16[3,3,8,128]{3,2,1,0:T(8,128)(2,1)S(1)} %get-tuple-element.169), channel_id=1, source_target_pairs={{0,31},{1,28},{2,29},{3,30},{4,3},{5,0},{6,1},{7,2},{8,7},{9,4},{1... | collective-permute-start | bytes 55304 | tf_op jit(solution)/shard_map/ppermute | solution.py:528
  109.0 20.9 %collective-permute-start.12 = (bf16[3,28,8,128]{3,2,1,0:T(8,128)(2,1)S(1)}, bf16[3,28,8,128]{3,2,1,0:T(8,128)(2,1)S(1)}, u32[]{:S(2)}, u32[]{:S(2)}) collective-permute-start(bf16[3,28,8,128]{3,2,1,0:T(8,128)(2,1)S(1)} %get-tuple-element.167), channel_id=1, source_target_pairs={{0,28},{4,0},{8,4},{12,8},{16,12},{20,16},{24,20},{28,24},{1,29},{... | collective-permute-start | bytes 516104 | tf_op jit(solution)/shard_map/ppermute | solution.py:518
  109.3 20.5 %collective-permute-start.13 = (bf16[28,3,8,128]{3,2,1,0:T(8,128)(2,1)S(1)}, bf16[28,3,8,128]{3,2,1,0:T(8,128)(2,1)S(1)}, u32[]{:S(2)}, u32[]{:S(2)}) collective-permute-start(bf16[28,3,8,128]{3,2,1,0:T(8,128)(2,1)S(1)} %get-tuple-element.168), channel_id=1, source_target_pairs={{0,3},{1,0},{2,1},{3,2},{4,7},{5,4},{6,5},{7,6},{8,11},{9,8},{10,9... | collective-permute-start | bytes 516104 | tf_op jit(solution)/shard_map/ppermute | solution.py:518
  111.3 18.5 %copy-start.16 = (bf16[128,384]{1,0:T(8,128)(2,1)S(1)}, bf16[128,384]{1,0:T(8,128)(2,1)}, u32[]{:S(2)}) copy-start(bf16[128,384]{1,0:T(8,128)(2,1)} %get-tuple-element.139.refs_4_.refs_1_.refs_11_.refs_5_) | copy-start | bytes 294916
  126.1 1.7 copy-start
  127.8 0.7 copy-start.2
  128.5 0.7 copy-start.3
  129.2 0.6 copy-start.5
  129.8 11.1 %copy-start.6 = (f32[4,8,128]{2,1,0:T(8,128)}, f32[4,8,128]{2,1,0:T(8,128)S(1)}, u32[]{:S(2)}) copy-start(f32[4,8,128]{2,1,0:T(8,128)S(1)} %get-tuple-element.199.refs_9_) | copy-start | bytes 49156
  129.8 11.1 %copy-start.7 = (f32[8,512]{1,0:T(8,128)}, f32[8,512]{1,0:T(8,128)S(1)}, u32[]{:S(2)}) copy-start(f32[8,512]{1,0:T(8,128)S(1)} %get-tuple-element.203.refs_13_) | copy-start | bytes 49156
  141.0 16.9 %collective-permute-start.17 = (bf16[3,3,8,128]{3,2,1,0:T(8,128)(2,1)S(1)}, bf16[3,3,8,128]{3,2,1,0:T(8,128)(2,1)S(1)}, u32[]{:S(2)}, u32[]{:S(2)}) collective-permute-start(bf16[3,3,8,128]{3,2,1,0:T(8,128)(2,1)S(1)} %get-tuple-element.177), channel_id=1, source_target_pairs={{0,5},{1,6},{2,7},{3,4},{4,9},{5,10},{6,11},{7,8},{8,13},{9,14},{1... | collective-permute-start | bytes 55304 | tf_op jit(solution)/shard_map/ppermute | solution.py:528
  141.1 16.9 %collective-permute-start.15 = (bf16[3,28,8,128]{3,2,1,0:T(8,128)(2,1)S(1)}, bf16[3,28,8,128]{3,2,1,0:T(8,128)(2,1)S(1)}, u32[]{:S(2)}, u32[]{:S(2)}) collective-permute-start(bf16[3,28,8,128]{3,2,1,0:T(8,128)(2,1)S(1)} %get-tuple-element.175), channel_id=1, source_target_pairs={{0,4},{4,8},{8,12},{12,16},{16,20},{20,24},{24,28},{28,0},{1,5},{5... | collective-permute-start | bytes 516104 | tf_op jit(solution)/shard_map/ppermute | solution.py:518
  141.1 16.8 %collective-permute-start.16 = (bf16[28,3,8,128]{3,2,1,0:T(8,128)(2,1)S(1)}, bf16[28,3,8,128]{3,2,1,0:T(8,128)(2,1)S(1)}, u32[]{:S(2)}, u32[]{:S(2)}) collective-permute-start(bf16[28,3,8,128]{3,2,1,0:T(8,128)(2,1)S(1)} %get-tuple-element.176), channel_id=1, source_target_pairs={{0,1},{1,2},{2,3},{3,0},{4,5},{5,6},{6,7},{7,4},{8,9},{9,10},{10,1... | collective-permute-start | bytes 516104 | tf_op jit(solution)/shard_map/ppermute | solution.py:518
  155.4 1.2 copy-start.1
  156.5 0.7 copy-start.4
  157.2 0.6 copy-start.8
  157.9 0.6 copy-start.35
  157.9 0.7 copy-start.23
  158.0 0.7 copy-start.24
